TPU v7x, 256 devices: a whole 4x4x8 slice. The times are simulated.
256 devices in a mesh: lat: 16 (over y, x_lo, core), lon: 16 (over z, x_hi).
Axes of the slice: x: 4 (x_hi: 2, x_lo: 2; x = x_hi * 2 + x_lo), y: 4, z: 8, core: 2. Of those that a mesh axis runs over, the one named last changes fastest.
Arguments:
- fields: bfloat16 [256, 128, 2048], P(None, 'lat', 'lon'), may hold values from -6 to 6
- grad_out: bfloat16 [256, 128, 2048], P(None, 'lat', 'lon'), may hold values from -6 to 6
- weight: bfloat16 [9, 256, 256], replicated, may hold values from -0.375 to 0.375
- basis_table: bfloat16 [9, 128, 7, 33], replicated, may hold values from -0.75 to 0.75
- lon_reach: int32 [128], replicated, may hold values from 1 to 16, as said below
Outputs:
- field_grad: bfloat16 [256, 128, 2048], P(None, 'lat', 'lon')
- weight_grad: float32 [9, 256, 256], replicated
Inputs may be any that keep to these rules, and one draw needn't show every extreme that they name: lon_reach equals 16 on the rows nearest the poles, equals 1 on the rows farthest from both ends, and is larger near the poles than near the middle.
All inputs are finite; a program needn't handle non-finite values.
Results may differ from a plain program's by a relative error of at most 0.0049.
Values may be sent and summed in bfloat16 or wider, within the bound.
No kernel may reach another device: no remote copies, remote signals or barrier semaphores. Data moves between devices by JAX's collectives and lax.ppermute only.
A program may use at most 192 MiB of HBM per device.

v0:
```python
import jax
import jax.numpy as jnp
from jax import lax
from jax.sharding import PartitionSpec as P


def extended(cells, sides, width, closed):
    for axis, dim in sides:
        count = lax.axis_size(axis)
        ends = count if closed else count - 1
        head = lax.slice_in_dim(cells, 0, width, axis=dim)
        tail = lax.slice_in_dim(cells, cells.shape[dim] - width, cells.shape[dim], axis=dim)
        cells = jnp.concatenate(
            [
                lax.ppermute(tail, axis, [(i, (i + 1) % count) for i in range(ends)]),
                cells,
                lax.ppermute(head, axis, [((i + 1) % count, i) for i in range(ends)]),
            ],
            axis=dim,
        )
    return cells


def masked_basis(basis_table, lon_reach):
    tap_count = basis_table.shape[3]
    col_half = (tap_count - 1) // 2
    offset = jnp.abs(lax.iota(jnp.int32, tap_count) - col_half)
    keeping = offset[None, :] <= lon_reach[:, None]
    return jnp.where(keeping[None, :, None, :], basis_table, jnp.zeros_like(basis_table))


def banded_rows(rows_basis, width, adjoint):
    tap_count = rows_basis.shape[3]
    span_cols = width + tap_count - 1
    col_index = lax.iota(jnp.int32, span_cols)[:, None, None]
    out_index = lax.iota(jnp.int32, width)[None, :, None]
    tap_index = lax.iota(jnp.int32, tap_count)[None, None, :]
    if adjoint:
        matches = out_index - col_index + tap_count - 1 == tap_index
    else:
        matches = col_index - out_index == tap_index
    selector = matches.astype(jnp.bfloat16)
    banded = jnp.einsum("kast,clt->kascl", rows_basis, selector, preferred_element_type=jnp.float32)
    return banded.astype(jnp.bfloat16)


def local(fields, grad_out, weight, basis_table, lon_reach):
    channels, lat_dev, lon_dev = fields.shape
    basis_count, nlat_all, row_span, tap_count = basis_table.shape
    row_half = (row_span - 1) // 2
    col_half = (tap_count - 1) // 2
    first_row = lax.axis_index("lat") * lat_dev
    masked = masked_basis(basis_table, lon_reach)
    own_rows = lax.dynamic_slice_in_dim(masked, first_row, lat_dev, 1)
    basis_pad = jnp.pad(masked, ((0, 0), (row_half, row_half), (0, 0), (0, 0)))
    near_rows = lax.dynamic_slice_in_dim(basis_pad, first_row, lat_dev + 2 * row_half, 1)
    back_rows = jnp.stack(
        [
            near_rows[
                :, 2 * row_half - shift_row : 2 * row_half - shift_row + lat_dev, shift_row, :
            ]
            for shift_row in range(row_span)
        ],
        axis=2,
    )
    ext_fields = extended(fields, (("lat", 1),), row_half, False)
    ext_fields = extended(ext_fields, (("lon", 2),), col_half, True)
    mixed = jnp.einsum(
        "kcd,dal->kcal", weight, grad_out, preferred_element_type=jnp.float32
    ).astype(jnp.bfloat16)
    ext_mixed = extended(mixed, (("lat", 2),), row_half, False)
    ext_mixed = extended(ext_mixed, (("lon", 3),), col_half, True)
    forward_band = banded_rows(own_rows, lon_dev, False)
    windows = jnp.stack(
        [ext_fields[:, shift_row : shift_row + lat_dev, :] for shift_row in range(row_span)], axis=2
    )
    response = jnp.einsum(
        "casw,kaswl->kcal", windows, forward_band, preferred_element_type=jnp.float32
    ).astype(jnp.bfloat16)
    local_grad = jnp.einsum("kcal,dal->kcd", response, grad_out, preferred_element_type=jnp.float32)
    summed = lax.psum(local_grad, ("lat", "lon"))
    weight_grad = summed / nlat_all
    adjoint_band = banded_rows(back_rows, lon_dev, True)
    z_window = jnp.stack(
        [
            ext_mixed[:, :, 2 * row_half - shift_row : 2 * row_half - shift_row + lat_dev, :]
            for shift_row in range(row_span)
        ],
        axis=3,
    )
    field_grad = jnp.einsum(
        "kcasw,kaswp->cap", z_window, adjoint_band, preferred_element_type=jnp.float32
    ).astype(jnp.bfloat16)
    return (field_grad, weight_grad)


def solution(mesh):
    in_specs = (P(None, "lat", "lon"), P(None, "lat", "lon"), P(), P(), P())
    out_specs = (P(None, "lat", "lon"), P())
    return jax.shard_map(local, mesh=mesh, in_specs=in_specs, out_specs=out_specs, check_vma=False)
```

profile of v0, /device:TPU:1, one launch (start us, length us, event | category | flops | bytes accessed | tf_op | source)
XLA Modules:
  0.0 442.9 jit_solution(473551989835045361)
XLA Ops:
  7.2 0.0 copy-start
  7.2 0.0 all-reduce.3.cloned.1.call-start
  7.2 1.4 copy.21
  8.6 0.0 copy-done
  8.6 1.4 convolution_convert_fusion.2
  10.1 0.0 copy-start.2
  10.1 2.2 copy-done.2
  12.3 2.2 fusion.62
  14.5 4.5 %collective-permute-start = (bf16[9,256,3,128]{1,3,2,0:T(8,128)(2,1)}, bf16[9,256,3,128]{1,3,2,0:T(8,128)(2,1)}, u32[]{:S(2)}, u32[]{:S(2)}) collective-permute-start(bf16[9,256,3,128]{1,3,2,0:T(8,128)(2,1)} %get-tuple-element.10), channel_id=1, source_target_pairs={{0,16},{16,32},{32,48},{48,64},{64,80},{80,96},{96,112},{112,128},... | collective-permute-start | bytes 5308424 | tf_op jit(solution)/shard_map/ppermute | solution.py:15
  19.0 3.1 collective-permute-start.1
  22.2 0.0 copy-done.7
  22.2 0.3 copy.24
  22.5 0.0 copy-start.3
  22.5 0.9 fusion.63
  23.4 2.4 collective-permute-start.4
  25.8 1.9 collective-permute-start.5
  27.8 0.0 copy-done.6
  27.8 2.2 copy.19
  30.0 0.0 copy-done.11
  30.0 0.1 broadcast_compare_fusion
  30.1 1.7 broadcast_select_fusion
  31.9 9.9 %convolution_convert_fusion = bf16[9,8,7,160,128]{4,1,3,2,0:T(8,128)(2,1)} fusion(s32[160,128]{1,0:T(8,128)S(1)} %iota_subtract_fusion, bf16[9,128,7,33]{3,1,2,0:T(8,128)(2,1)S(1)} %broadcast_select_fusion, s32[]{:T(128)S(6)} %select_n.12), kind=kOutput, calls=%fused_computation.5 | convolution fusion | flops 692244480 | bytes 20854788 | tf_op jit(solution)/shard_map/kast,clt->kascl/dot_general | solution.py:43
  42.0 1.2 fusion.19
  43.2 0.0 collective-permute-done.4
  43.2 20.4 %collective-permute-done.5 = bf16[256,3,128]{0,2,1:T(8,128)(2,1)S(1)} collective-permute-done((bf16[256,3,128]{0,2,1:T(8,128)(2,1)}, bf16[256,3,128]{0,2,1:T(8,128)(2,1)S(1)}, u32[]{:S(2)}, u32[]{:S(2)}) %collective-permute-start.5) | collective-permute-done | bytes 196640 | tf_op jit(solution)/shard_map/ppermute | solution.py:17
  63.6 0.0 copy-done.3
  63.6 2.8 collective-permute-start.6
  66.4 5.6 %collective-permute-start.7 = (bf16[256,14,16]{0,2,1:T(8,128)(2,1)S(1)}, bf16[256,14,16]{0,2,1:T(8,128)(2,1)}, u32[]{:S(2)}, u32[]{:S(2)}) collective-permute-start(bf16[256,14,16]{0,2,1:T(8,128)(2,1)S(1)} %get-tuple-element.13), channel_id=1, source_target_pairs={{1,0},{2,1},{3,2},{4,3},{5,4},{6,5},{7,6},{8,7},{9,8},{10,9},{11,1... | collective-permute-start | bytes 344072 | tf_op jit(solution)/shard_map/ppermute | solution.py:17
  72.0 0.0 copy-start.9
  72.0 1.8 collective-permute-done.6
  73.9 0.0 copy-done.5
  73.9 0.0 copy-done.9
  73.9 0.0 collective-permute-done.7
  73.9 1.3 pad_maximum_fusion.1
  75.2 0.0 copy-start.8
  75.2 0.9 fusion.54
  76.1 0.9 fusion.53
  77.0 0.9 fusion.52
  77.9 0.9 fusion.51
  78.9 0.9 fusion.50
  79.8 0.9 fusion.49
  80.7 0.9 fusion.48
  81.6 17.3 %fusion.20 = f32[9,256,256]{2,1,0:T(8,128)} fusion(bf16[9,8,7,160,128]{4,1,3,2,0:T(8,128)(2,1)} %convolution_convert_fusion, bf16[256,8,7,160]{0,3,2,1:T(8,128)(2,1)} %fusion.48, bf16[256,8,128]{2,1,0:T(8,128)(2,1)S(1)} %copy-done.8), kind=kOutput, calls=%fused_computation.33 | convolution fusion | flops 6495141888 | bytes 28114944 | tf_op jit(solution)/shard_map/kcal,dal->kcd/dot_general | solution.py:80
  98.9 0.0 all-reduce.3.cloned.1.call-update
  99.0 0.0 collective-permute-done
  99.0 0.0 collective-permute-done.1
  99.0 3.3 pad_maximum_fusion.4
  102.3 0.2 collective-permute-start.2
  102.5 5.2 %collective-permute-start.3 = (bf16[9,256,14,16]{1,3,2,0:T(8,128)(2,1)}, bf16[9,256,14,16]{1,3,2,0:T(8,128)(2,1)S(1)}, u32[]{:S(2)}, u32[]{:S(2)}) collective-permute-start(bf16[9,256,14,16]{1,3,2,0:T(8,128)(2,1)} %get-tuple-element.9), channel_id=1, source_target_pairs={{1,0},{2,1},{3,2},{4,3},{5,4},{6,5},{7,6},{8,7},{9,8},{10,9},{11,1... | collective-permute-start | bytes 3096584 | tf_op jit(solution)/shard_map/ppermute | solution.py:17
  107.7 10.4 %convolution_convert_fusion.1 = bf16[9,8,7,160,128]{4,1,3,2,0:T(8,128)(2,1)} fusion(pred[160,128,33,1,1]{1,0,2,4,3:T(32,128)(4,1)S(1)} %copy-done.4, bf16[9,8,7,33]{3,1,2,0:T(8,128)(2,1)S(1)} %copy-done.10), kind=kOutput, calls=%fused_computation.6 | convolution fusion | flops 691568640 | bytes 21352944 | tf_op jit(solution)/shard_map/kast,clt->kascl/dot_general | solution.py:43
  118.1 262.5 %all-reduce.3.cloned.1.call-done = f32[9,256,256]{2,1,0:T(8,128)} async-done(((f32[9,256,256]{2,1,0:T(8,128)}), f32[9,256,256]{2,1,0:T(8,128)}) %all-reduce.3.cloned.1.call-update) | async-done | bytes 2359312 | tf_op jit(solution)/shard_map/psum | solution.py:81
  380.6 3.3 broadcast_multiply_fusion
  383.8 0.0 collective-permute-done.2
  383.8 0.0 collective-permute-done.3
  383.8 8.7 %pad_maximum_fusion = bf16[9,256,14,160]{1,3,2,0:T(8,128)(2,1)S(1)} fusion(bf16[9,256,14,16]{1,3,2,0:T(8,128)(2,1)S(1)} %collective-permute-done.3, bf16[9,256,3,128]{1,3,2,0:T(8,128)(2,1)} %collective-permute-done.1, bf16[9,256,8,128]{1,3,2,0:T(8,128)(2,1)} %copy-done.2, bf16[9,256,3,128]{1,3,2,0:T(8,128)(2,1)} %collective-permute-done, ...), kind=kLoop, calls=%fused_computation.7 | loop fusion | flops 51609600 | bytes 20643840 | tf_op jit(solution)/shard_map/concatenate | solution.py:13
  392.5 2.9 fusion.11
  395.5 2.9 fusion.10
  398.4 2.9 fusion.9
  401.2 3.0 fusion.8
  404.2 2.9 fusion.7
  407.1 2.9 fusion.6
  410.0 2.8 fusion.5
  412.8 22.1 %fusion.42 = bf16[256,8,128]{0,2,1:T(8,128)(2,1)S(1)} fusion(bf16[9,256,8,7,160]{1,4,2,0,3:T(8,128)(2,1)} %fusion.5, bf16[9,8,7,160,128]{4,1,3,2,0:T(8,128)(2,1)} %convolution_convert_fusion.1), kind=kOutput, calls=%fused_computation.37 | convolution fusion | flops 5285085184 | bytes 62455808 | tf_op jit(solution)/shard_map/kcasw,kaswp->cap/dot_general | solution.py:91
  435.0 1.1 copy.36
  (22 shorter events, 0.3 us)
Async XLA Ops:
  7.2 1.5 copy-start
  7.2 373.4 %all-reduce.3.cloned.1.call-start = ((), (), s32[]{:S(2)}) async-start(), calls=%async_computation | async-start | bytes 4718592 | tf_op jit(solution)/shard_map/psum | solution.py:81
  10.1 2.2 copy-start.2
  12.3 9.9 %copy-start.7 = (bf16[256,8,128]{2,1,0:T(8,128)(2,1)S(1)}, bf16[256,8,128]{2,1,0:T(8,128)(2,1)}, u32[]{:S(2)}) copy-start(bf16[256,8,128]{2,1,0:T(8,128)(2,1)} %param.5) | copy-start | bytes 1572868
  12.3 15.5 %copy-start.6 = (bf16[9,128,7,33]{1,2,3,0:T(8,128)(2,1)S(1)}, bf16[9,128,7,33]{1,2,3,0:T(8,128)(2,1)}, u32[]{:S(2)}) copy-start(bf16[9,128,7,33]{1,2,3,0:T(8,128)(2,1)} %param.8) | copy-start | bytes 1596676
  12.3 17.7 %copy-start.11 = (s32[128]{0:T(128)S(1)}, s32[128]{0:T(128)}, u32[]{:S(2)}) copy-start(s32[128]{0:T(128)} %param.9) | copy-start | bytes 1540
  14.5 84.5 %collective-permute-start = (bf16[9,256,3,128]{1,3,2,0:T(8,128)(2,1)}, bf16[9,256,3,128]{1,3,2,0:T(8,128)(2,1)}, u32[]{:S(2)}, u32[]{:S(2)}) collective-permute-start(bf16[9,256,3,128]{1,3,2,0:T(8,128)(2,1)} %get-tuple-element.10), channel_id=1, source_target_pairs={{0,16},{16,32},{32,48},{48,64},{64,80},{80,96},{96,112},{112,128},... | collective-permute-start | bytes 5308424 | tf_op jit(solution)/shard_map/ppermute | solution.py:15
  19.0 80.0 %collective-permute-start.1 = (bf16[9,256,3,128]{1,3,2,0:T(8,128)(2,1)}, bf16[9,256,3,128]{1,3,2,0:T(8,128)(2,1)}, u32[]{:S(2)}, u32[]{:S(2)}) collective-permute-start(bf16[9,256,3,128]{1,3,2,0:T(8,128)(2,1)} %get-tuple-element.11), channel_id=1, source_target_pairs={{16,0},{32,16},{48,32},{64,48},{80,64},{96,80},{112,96},{128,112},... | collective-permute-start | bytes 5308424 | tf_op jit(solution)/shard_map/ppermute | solution.py:17
  22.5 41.1 %copy-start.3 = (bf16[256,8,128]{0,2,1:T(8,128)(2,1)}, bf16[256,8,128]{0,2,1:T(8,128)(2,1)S(1)}, u32[]{:S(2)}) copy-start(bf16[256,8,128]{0,2,1:T(8,128)(2,1)S(1)} %copy.24) | copy-start | bytes 1572868
  23.4 19.8 %collective-permute-start.4 = (bf16[256,3,128]{0,2,1:T(8,128)(2,1)}, bf16[256,3,128]{0,2,1:T(8,128)(2,1)S(1)}, u32[]{:S(2)}, u32[]{:S(2)}) collective-permute-start(bf16[256,3,128]{0,2,1:T(8,128)(2,1)} %get-tuple-element.14), channel_id=1, source_target_pairs={{0,16},{16,32},{32,48},{48,64},{64,80},{80,96},{96,112},{112,128},... | collective-permute-start | bytes 589832 | tf_op jit(solution)/shard_map/ppermute | solution.py:15
  25.8 37.7 %collective-permute-start.5 = (bf16[256,3,128]{0,2,1:T(8,128)(2,1)}, bf16[256,3,128]{0,2,1:T(8,128)(2,1)S(1)}, u32[]{:S(2)}, u32[]{:S(2)}) collective-permute-start(bf16[256,3,128]{0,2,1:T(8,128)(2,1)} %get-tuple-element.15), channel_id=1, source_target_pairs={{16,0},{32,16},{48,32},{64,48},{80,64},{96,80},{112,96},{128,112},... | collective-permute-start | bytes 589832 | tf_op jit(solution)/shard_map/ppermute | solution.py:17
  63.6 10.3 %copy-start.5 = (bf16[256,3,128]{0,2,1:T(8,128)(2,1)}, bf16[256,3,128]{0,2,1:T(8,128)(2,1)S(1)}, u32[]{:S(2)}) copy-start(bf16[256,3,128]{0,2,1:T(8,128)(2,1)S(1)} %collective-permute-done.5) | copy-start | bytes 589828
  63.6 10.3 %collective-permute-start.6 = (bf16[256,14,16]{0,2,1:T(8,128)(2,1)S(1)}, bf16[256,14,16]{0,2,1:T(8,128)(2,1)S(1)}, u32[]{:S(2)}, u32[]{:S(2)}) collective-permute-start(bf16[256,14,16]{0,2,1:T(8,128)(2,1)S(1)} %get-tuple-element.12), channel_id=1, source_target_pairs={{0,1},{1,2},{2,3},{3,4},{4,5},{5,6},{6,7},{7,8},{8,9},{9,10},{10,1... | collective-permute-start | bytes 344072 | tf_op jit(solution)/shard_map/ppermute | solution.py:15
  66.4 7.5 %collective-permute-start.7 = (bf16[256,14,16]{0,2,1:T(8,128)(2,1)S(1)}, bf16[256,14,16]{0,2,1:T(8,128)(2,1)}, u32[]{:S(2)}, u32[]{:S(2)}) collective-permute-start(bf16[256,14,16]{0,2,1:T(8,128)(2,1)S(1)} %get-tuple-element.13), channel_id=1, source_target_pairs={{1,0},{2,1},{3,2},{4,3},{5,4},{6,5},{7,6},{8,7},{9,8},{10,9},{11,1... | collective-permute-start | bytes 344072 | tf_op jit(solution)/shard_map/ppermute | solution.py:17
  72.0 1.8 copy-start.9
  75.2 6.4 %copy-start.8 = (bf16[256,8,128]{2,1,0:T(8,128)(2,1)S(1)}, bf16[256,8,128]{2,1,0:T(8,128)(2,1)}, u32[]{:S(2)}) copy-start(bf16[256,8,128]{2,1,0:T(8,128)(2,1)} %param.6) | copy-start | bytes 1572868
  99.0 8.8 %copy-start.4 = (pred[160,128,33,1,1]{1,0,2,4,3:T(32,128)(4,1)S(1)}, pred[160,128,33,1,1]{1,0,2,4,3:T(32,128)(4,1)}, u32[]{:S(2)}) copy-start(pred[160,128,33,1,1]{1,0,2,4,3:T(32,128)(4,1)} %fusion.19) | copy-start | bytes 2027524
  99.0 8.8 %copy-start.10 = (bf16[9,8,7,33]{3,1,2,0:T(8,128)(2,1)S(1)}, bf16[9,8,7,33]{3,1,2,0:T(8,128)(2,1)}, u32[]{:S(2)}) copy-start(bf16[9,8,7,33]{3,1,2,0:T(8,128)(2,1)} %copy-done.9) | copy-start | bytes 99796
  102.3 281.5 %collective-permute-start.2 = (bf16[9,256,14,16]{1,3,2,0:T(8,128)(2,1)}, bf16[9,256,14,16]{1,3,2,0:T(8,128)(2,1)S(1)}, u32[]{:S(2)}, u32[]{:S(2)}) collective-permute-start(bf16[9,256,14,16]{1,3,2,0:T(8,128)(2,1)} %get-tuple-element.8), channel_id=1, source_target_pairs={{0,1},{1,2},{2,3},{3,4},{4,5},{5,6},{6,7},{7,8},{8,9},{9,10},{10,1... | collective-permute-start | bytes 3096584 | tf_op jit(solution)/shard_map/ppermute | solution.py:15
  102.5 281.3 %collective-permute-start.3 = (bf16[9,256,14,16]{1,3,2,0:T(8,128)(2,1)}, bf16[9,256,14,16]{1,3,2,0:T(8,128)(2,1)S(1)}, u32[]{:S(2)}, u32[]{:S(2)}) collective-permute-start(bf16[9,256,14,16]{1,3,2,0:T(8,128)(2,1)} %get-tuple-element.9), channel_id=1, source_target_pairs={{1,0},{2,1},{3,2},{4,3},{5,4},{6,5},{7,6},{8,7},{9,8},{10,9},{11,1... | collective-permute-start | bytes 3096584 | tf_op jit(solution)/shard_map/ppermute | solution.py:17
  412.8 23.2 %copy-start.1 = (bf16[9,256,256]{2,1,0:T(8,128)(2,1)S(1)}, bf16[9,256,256]{2,1,0:T(8,128)(2,1)}, u32[]{:S(2)}) copy-start(bf16[9,256,256]{2,1,0:T(8,128)(2,1)} %param.7) | copy-start | bytes 3538948
Sparse Core Ops, SparseCore 0:
  99.1 281.4 all-reduce.2
where the time goes:
time: 444 us; the launch traced here: 443 us
  waiting for transfers between devices  285 us (64%)
  matrix products  61.2 us (14%)
  local copies, waits for them, and re-layouts  37.3 us (8%)
  starting transfers between devices  25.8 us (6%)
  other arithmetic  19.6 us (4%)
  between operations  14.3 us (3%)
    psum x1, waiting for transfers between devices, local(): summed = lax.psum(local_grad, ('lat', 'lon'))  262 us
    unnamed x46, local copies, waits for them, and re-layouts  30.4 us
    dot_general x1, matrix products, local(): jnp.einsum('kcasw,kaswp->cap', z_window, adjoint_band, preferred_element_...  22.1 us
    ppermute x4, waiting for transfers between devices, extended(): lax.ppermute(head, axis, [((i + 1) % count, i) for i in range(ends)])  20.4 us
    dot_general x2, matrix products, banded_rows(): jnp.einsum('kast,clt->kascl', rows_basis, selector, preferred_element_typ...  20.3 us
    dot_general x1, matrix products, local(): jnp.einsum('kcal,dal->kcd', response, grad_out, preferred_element_type=jn...  17.3 us
    ppermute x4, starting transfers between devices, extended(): lax.ppermute(head, axis, [((i + 1) % count, i) for i in range(ends)])  15.8 us
    ppermute x4, starting transfers between devices, extended(): lax.ppermute(tail, axis, [(i, (i + 1) % count) for i in range(ends)])  9.99 us
  transfers between devices with their start and end apart: 9, of which 3 were waited for; matrix products, arithmetic and copies ran while one was open for 13% of the time, Pallas kernels for 0%

commit v1 on v0

v1 whole, which is shorter than its diff:
```python
import jax
import jax.numpy as jnp
from jax import lax
from jax.experimental import pallas as pl
from jax.experimental.pallas import tpu as pltpu
from jax.sharding import Mesh, PartitionSpec as P

LAT = ("y", "x_lo", "core")
LON = ("z", "x_hi")
PLANE = ("y", "x_hi", "x_lo")
BLOCK = 32
bf16, f32 = jnp.bfloat16, jnp.float32


def shift(x, axes, step, closed):
    count = 1
    for axis in axes:
        count *= lax.axis_size(axis)
    pairs = [(i, (i + step) % count) for i in range(count) if closed or 0 <= i + step < count]
    return lax.ppermute(x, axes, pairs)


def tap_rows(basis_table, lon_reach, first_row, lat_dev):
    basis_count, nlat_all, row_span, tap_count = basis_table.shape
    half = row_span // 2
    near = lat_dev + 2 * half
    start = jnp.clip(first_row - half, 0, nlat_all - near)
    table = lax.dynamic_slice_in_dim(basis_table, start, near, 1)
    reach = lax.dynamic_slice_in_dim(lon_reach, start, near, 0)
    offset = jnp.abs(lax.iota(jnp.int32, tap_count) - tap_count // 2)
    table = jnp.where((offset[None, :] <= reach[:, None])[None, :, None, :], table, jnp.zeros_like(table))
    table = jnp.pad(table, ((0, 0), (half, half), (0, 0), (0, 0)))
    table = lax.dynamic_slice_in_dim(table, first_row - start, near, 1)
    table = jnp.flip(table, 3)
    rows = jnp.stack(
        [table[:, s : s + lat_dev, row_span - 1 - s, :] for s in range(row_span)], axis=2
    )
    rows = jnp.pad(rows, ((0, 0), (0, 0), (0, 1), (0, 2 * BLOCK - tap_count)))
    rows = jnp.transpose(rows, (1, 0, 2, 3)).astype(f32)
    return rows.reshape(lat_dev, basis_count, (row_span + 1) * BLOCK * 2 // 128, 128)


def spread_kernel(core_ref, main, up, down, left, right, taps, f_ref, q_ref, keep, send, ext, band):
    lat_dev, lon_dev, channels = main.shape
    half = up.shape[0]
    basis_count, groups = taps.shape[1], taps.shape[2]
    side = left.shape[1]
    row_span = 2 * half + 1
    ext[:half, side : side + lon_dev, :] = up[...]
    ext[half : half + lat_dev, side : side + lon_dev, :] = main[...]
    ext[half + lat_dev :, side : side + lon_dev, :] = down[...]
    ext[:, :side, :] = left[...]
    ext[:, side + lon_dev :, :] = right[...]

    def row(i, carry):
        for k in range(basis_count):
            for p in range(groups):
                line = jnp.broadcast_to(taps[i, k, p : p + 1, :], (BLOCK, 128))
                line = pltpu.roll(line, 0, 1, stride=1, stride_axis=0)
                band[k * BLOCK : (k + 1) * BLOCK, p * 128 : (p + 1) * 128] = line.astype(bf16)
        for j in range(lon_dev // BLOCK):
            parts = [ext[i + s, j * BLOCK : (j + 2) * BLOCK, :] for s in range(row_span)]
            window = jnp.concatenate(parts + [jnp.zeros_like(parts[0])], axis=0)
            out = jnp.dot(band[...], window, preferred_element_type=f32).astype(bf16)
            for k in range(basis_count):
                at = pl.ds(pl.multiple_of(i * lon_dev + j * BLOCK, BLOCK), BLOCK)
                q_ref[k, at, :] = out[k * BLOCK : (k + 1) * BLOCK, :]
        return carry

    lax.fori_loop(0, lat_dev, row, 0)
    first = core_ref[0] == 0

    def grad(k, carry):
        out = jnp.dot(f_ref[...], q_ref[k], preferred_element_type=f32)
        low, high = out[:, : channels // 2], out[:, channels // 2 :]
        keep[k] = jnp.where(first, low, high)
        send[k] = jnp.where(first, high, low)
        return carry

    lax.fori_loop(0, basis_count, grad, 0)


def spread(core, main, up, down, left, right, taps, cells):
    lat_dev, lon_dev, channels = main.shape
    basis_count = taps.shape[1]
    near, wide = lat_dev + 2 * up.shape[0], lon_dev + 2 * left.shape[1]
    vmem = pl.BlockSpec(memory_space=pltpu.VMEM)
    half = jax.ShapeDtypeStruct((basis_count, channels, channels // 2), f32)
    return pl.pallas_call(
        spread_kernel,
        out_shape=(jax.ShapeDtypeStruct((basis_count, lat_dev * lon_dev, channels), bf16), half, half),
        in_specs=[pl.BlockSpec(memory_space=pltpu.SMEM)] + [vmem] * 7,
        out_specs=(vmem, vmem, vmem),
        scratch_shapes=[
            pltpu.VMEM((near, wide, channels), bf16),
            pltpu.VMEM((basis_count * BLOCK, taps.shape[2] * 128), bf16),
        ],
        compiler_params=pltpu.CompilerParams(vmem_limit_bytes=40 * 1024 * 1024),
        cost_estimate=pl.CostEstimate(flops=4 * 10**9, bytes_accessed=10**7, transcendentals=0),
    )(core, main, up, down, left, right, taps, cells)


def mix_kernel(w_ref, q_ref, out_ref):
    basis_count, cells, channels = q_ref.shape

    def part(j, carry):
        at = pl.ds(pl.multiple_of(j * 256, 256), 256)
        total = jnp.zeros((channels, 256), f32)
        for k in range(basis_count):
            total += lax.dot_general(
                w_ref[k], q_ref[k, at, :], (((1,), (1,)), ((), ())), preferred_element_type=f32
            )
        out_ref[:, at] = total.astype(bf16)
        return carry

    lax.fori_loop(0, cells // 256, part, 0)


def mix(weight, q):
    basis_count, cells, channels = q.shape
    vmem = pl.BlockSpec(memory_space=pltpu.VMEM)
    return pl.pallas_call(
        mix_kernel,
        out_shape=jax.ShapeDtypeStruct((channels, cells), bf16),
        in_specs=[vmem, vmem],
        out_specs=vmem,
        compiler_params=pltpu.CompilerParams(vmem_limit_bytes=30 * 1024 * 1024),
        cost_estimate=pl.CostEstimate(flops=12 * 10**8, bytes_accessed=7 * 10**6, transcendentals=0),
    )(weight, q)


def all_to_all(x, axes):
    return lax.all_to_all(x, axes, 0, 0, tiled=True)


def to_all(x, count):
    return jnp.broadcast_to(x[None], (count,) + x.shape)


def reduce_all(keep, send, core, scale):
    swap = [(0, 1), (1, 0)]
    basis_count, channels, half = keep.shape
    plane = 1
    for axis in PLANE:
        plane *= lax.axis_size(axis)
    depth = lax.axis_size("z")
    own = keep + lax.ppermute(send, "core", swap)
    own = own.reshape(plane, -1, half).astype(bf16)
    own = jnp.sum(all_to_all(own, PLANE).astype(f32), axis=0).astype(bf16)
    own = jnp.sum(all_to_all(to_all(own, depth), ("z",)).astype(f32), axis=0)
    own = (own * scale).astype(bf16)
    own = all_to_all(to_all(own, plane), PLANE).reshape(basis_count, channels, half)
    other = lax.ppermute(own, "core", swap)
    low, high = jnp.where(core == 0, own, other), jnp.where(core == 0, other, own)
    return jnp.concatenate([low, high], axis=2).astype(f32)


def local(fields, grad_out, weight, basis_table, lon_reach):
    channels, lat_dev, lon_dev = fields.shape
    nlat_all = basis_table.shape[1]
    half, side = basis_table.shape[2] // 2, basis_table.shape[3] // 2
    core = lax.axis_index("core")
    taps = tap_rows(basis_table, lon_reach, lax.axis_index(LAT) * lat_dev, lat_dev)
    main = jnp.transpose(grad_out, (1, 2, 0))
    up = shift(main[lat_dev - half :], LAT, 1, False)
    down = shift(main[:half], LAT, -1, False)
    tall = lambda at: jnp.concatenate([up[:, at], main[:, at], down[:, at]], axis=0)
    left = shift(tall(slice(lon_dev - side, lon_dev)), LON, 1, True)
    right = shift(tall(slice(0, side)), LON, -1, True)
    cells = fields.reshape(channels, lat_dev * lon_dev)
    q, keep, send = spread(core[None].astype(jnp.int32), main, up, down, left, right, taps, cells)
    field_grad = mix(weight, q).reshape(channels, lat_dev, lon_dev)
    weight_grad = reduce_all(keep, send, core, 1.0 / nlat_all)
    return field_grad, weight_grad


def solution(mesh):
    fine = Mesh(mesh.devices.reshape(4, 2, 2, 8, 2), ("y", "x_lo", "core", "z", "x_hi"))
    split = P(None, LAT, LON)
    return jax.shard_map(
        local,
        mesh=fine,
        in_specs=(split, split, P(), P(), P()),
        out_specs=(split, P()),
        check_vma=False,
    )
```

time: 444 us -> 96.6 us (0.22)
  waiting for transfers between devices: 285 us -> 12.8 us
  matrix products: 61.2 us -> 0 us
  blocking collectives: 0 us -> 43.3 us
  local copies, waits for them, and re-layouts: 37.3 us -> 8.96 us
  other arithmetic: 19.6 us -> 2.07 us
  between operations: 14.3 us -> 0.94 us
  Pallas kernels: 0 us -> 9.2 us
  starting transfers between devices: 25.8 us -> 19 us
    psum x1 -> x0, waiting for transfers between devices: 262 us -> none  [local(): summed = lax.psum(local_grad, ('lat', 'lon'))]
    dot_general x5 -> x0, matrix products: 61.2 us -> none  [the longest x1 22.1 us: local(): jnp.einsum('kcasw,kaswp->cap', z_window, adjoint_band, preferred_element_...]
    all_to_all x0 -> x3, blocking collectives: none -> 43.3 us  [all_to_all(): return lax.all_to_all(x, axes, 0, 0, tiled=True)]
    unnamed x46 -> x22, local copies, waits for them, and re-layouts: 30.4 us -> 7.47 us
    concatenate x2, other arithmetic: 9.98 us -> 0.03 us  [local(): jnp.concatenate([up[:, at], main[:, at], down[:, at]], axis=0)]
    ppermute x8 -> x6, waiting for transfers between devices: 22.2 us -> 12.8 us  [the longest x4 9.92 us: shift(): return lax.ppermute(x, axes, pairs)]
    pallas_call x0 -> x2, Pallas kernels: none -> 9.2 us  [the longest x1 7.18 us: spread(): pl.pallas_call(spread_kernel, out_shape=(jax.ShapeDtypeStruct((basis_coun...]
    ppermute x8 -> x6, starting transfers between devices: 25.8 us -> 19 us  [the longest x4 14.4 us: shift(): return lax.ppermute(x, axes, pairs)]
  transfers between devices with their start and end apart: 9 -> 6, of which waited for: 3 -> 4; matrix products, arithmetic and copies ran while one was open for 13% -> 3% of each run, Pallas kernels for 0% -> 2%
where the time goes in v1:
time: 96.6 us; the launch traced here: 96.3 us
  blocking collectives  43.3 us (45%)
  starting transfers between devices  19 us (20%)
  waiting for transfers between devices  12.8 us (13%)
  Pallas kernels  9.2 us (10%)
  local copies, waits for them, and re-layouts  8.96 us (9%)
  other arithmetic  2.07 us (2%)
    all_to_all x3, blocking collectives, all_to_all(): return lax.all_to_all(x, axes, 0, 0, tiled=True)  43.3 us
    ppermute x4, starting transfers between devices, shift(): return lax.ppermute(x, axes, pairs)  14.4 us
    ppermute x4, waiting for transfers between devices, shift(): return lax.ppermute(x, axes, pairs)  9.92 us
    unnamed x22, local copies, waits for them, and re-layouts  7.47 us
    pallas_call x1, Pallas kernels, spread(): pl.pallas_call(spread_kernel, out_shape=(jax.ShapeDtypeStruct((basis_coun...  7.18 us
    ppermute x1, starting transfers between devices, reduce_all(): other = lax.ppermute(own, 'core', swap)  4.68 us
    ppermute x1, waiting for transfers between devices, reduce_all(): own = keep + lax.ppermute(send, 'core', swap)  2.84 us
    pallas_call x1, Pallas kernels, mix(): pl.pallas_call(mix_kernel, out_shape=jax.ShapeDtypeStruct((channels, cell...  2.02 us
  transfers between devices with their start and end apart: 6, of which 4 were waited for; matrix products, arithmetic and copies ran while one was open for 3% of the time, Pallas kernels for 2%

profile of v1, /device:TPU:1, one launch (start us, length us, event | category | flops | bytes accessed | tf_op | source)
XLA Modules:
  0.0 96.3 jit_solution(1645682613668442964)
XLA Ops:
  0.6 0.0 copy-start
  0.6 1.4 %copy.12 = bf16[256,8,128]{0,2,1:T(8,128)(2,1)S(1)} copy(bf16[256,8,128]{2,1,0:T(8,128)(2,1)} %param.6) | data formatting | bytes 1048576 | tf_op args[1]
  2.1 0.0 copy-start.5
  2.1 4.5 %collective-permute-start = (bf16[3,128,256]{2,1,0:T(8,128)(2,1)S(1)}, bf16[3,128,256]{2,1,0:T(8,128)(2,1)S(1)}, u32[]{:S(2)}, u32[]{:S(2)}) collective-permute-start(bf16[3,128,256]{2,1,0:T(8,128)(2,1)S(1)} %get-tuple-element.13), channel_id=1, source_target_pairs={{0,16},{16,32},{32,48},{48,64},{64,80},{80,96},{96,112},{112,128},... | collective-permute-start | bytes 589832 | tf_op jit(solution)/shard_map/ppermute | solution.py:20
  6.6 1.9 %collective-permute-start.1 = (bf16[3,128,256]{2,1,0:T(8,128)(2,1)S(1)}, bf16[3,128,256]{2,1,0:T(8,128)(2,1)S(1)}, u32[]{:S(2)}, u32[]{:S(2)}) collective-permute-start(bf16[3,128,256]{2,1,0:T(8,128)(2,1)S(1)} %get-tuple-element.12), channel_id=1, source_target_pairs={{16,0},{32,16},{48,32},{64,48},{80,64},{96,80},{112,96},{128,112},... | collective-permute-start | bytes 589832 | tf_op jit(solution)/shard_map/ppermute | solution.py:20
  8.6 0.0 copy-done
  8.6 0.2 constant_dynamic-slice_fusion
  8.8 0.6 copy.15
  9.4 0.0 copy-done.5
  9.4 0.1 dynamic_slice.9
  9.5 0.1 broadcast_compare_fusion
  9.6 0.2 pad_dynamic-slice_fusion.6
  9.8 0.1 slice.75
  9.9 0.1 slice.77
  9.9 0.1 slice.79
  10.0 0.1 slice.81
  10.1 0.1 slice.83
  10.2 0.1 slice.85
  10.3 0.1 slice.87
  10.5 0.0 copy-start.4
  10.6 0.0 collective-permute-done.up
  10.6 3.0 %collective-permute-done.1.down = bf16[3,128,256]{2,1,0:T(8,128)(2,1)S(1)} collective-permute-done((bf16[3,128,256]{2,1,0:T(8,128)(2,1)S(1)}, bf16[3,128,256]{2,1,0:T(8,128)(2,1)S(1)}, u32[]{:S(2)}, u32[]{:S(2)}) %collective-permute-start.1) | collective-permute-done | bytes 196640 | tf_op jit(solution)/shard_map/ppermute | solution.py:20
  13.6 7.8 %collective-permute-start.3 = (bf16[14,16,256]{2,1,0:T(8,128)(2,1)S(1)}, bf16[14,16,256]{2,1,0:T(8,128)(2,1)S(1)}, u32[]{:S(2)}, u32[]{:S(2)}) collective-permute-start(bf16[14,16,256]{2,1,0:T(8,128)(2,1)S(1)} %pad_maximum_fusion.1), channel_id=1, source_target_pairs={{0,15},{1,0},{2,1},{3,2},{4,3},{5,4},{6,5},{7,6},{8,7},{9,8},{10,9... | collective-permute-start | bytes 344072 | tf_op jit(solution)/shard_map/ppermute | solution.py:20
  21.4 0.1 collective-permute-start.2
  21.6 0.1 copy.14
  21.6 0.1 reshape.62.taps
  21.8 0.0 copy-done.4
  21.8 0.1 copy.19
  21.9 1.3 %collective-permute-done.3.right = bf16[14,16,256]{2,1,0:T(8,128)(2,1)S(1)} collective-permute-done((bf16[14,16,256]{2,1,0:T(8,128)(2,1)S(1)}, bf16[14,16,256]{2,1,0:T(8,128)(2,1)S(1)}, u32[]{:S(2)}, u32[]{:S(2)}) %collective-permute-start.3) | collective-permute-done | bytes 114720 | tf_op jit(solution)/shard_map/ppermute | solution.py:20
  23.2 5.6 %collective-permute-done.2.left = bf16[14,16,256]{2,1,0:T(8,128)(2,1)S(1)} collective-permute-done((bf16[14,16,256]{2,1,0:T(8,128)(2,1)S(1)}, bf16[14,16,256]{2,1,0:T(8,128)(2,1)S(1)}, u32[]{:S(2)}, u32[]{:S(2)}) %collective-permute-start.2) | collective-permute-done | bytes 114720 | tf_op jit(solution)/shard_map/ppermute | solution.py:20
  28.8 7.2 %shard_map.68 = (bf16[9,1024,256]{2,1,0:T(8,128)(2,1)S(1)}, f32[9,256,128]{2,1,0:T(8,128)S(1)}, f32[9,256,128]{2,1,0:T(8,128)S(1)}) custom-call(s32[1]{0:T(128)} %bitcast.core_ref, bf16[8,128,256]{2,1,0:T(8,128)(2,1)S(1)} %bitcast.17, bf16[3,128,256]{2,1,0:T(8,128)(2,1)S(1)} %collective-permute-done.up, ...), custom_call_target="tpu_custom_call" | custom-call | flops 4000000000 | bytes 10000000 | tf_op jit(solution)/shard_map/pallas_call | solution.py:89
  36.0 0.0 copy-start.1
  36.0 2.1 %copy-done.1 = bf16[9,1024,256]{2,1,0:T(8,128)(2,1)} copy-done((bf16[9,1024,256]{2,1,0:T(8,128)(2,1)}, bf16[9,1024,256]{2,1,0:T(8,128)(2,1)S(1)}, u32[]{:S(2)}) %copy-start.1) | copy-done | bytes 4718616
  38.1 0.0 collective-permute-start.4
  38.1 2.8 %collective-permute-done.4 = f32[9,256,128]{2,1,0:T(8,128)S(1)} collective-permute-done((f32[9,256,128]{2,1,0:T(8,128)S(1)}, f32[9,256,128]{2,1,0:T(8,128)S(1)}, u32[]{:S(2)}, u32[]{:S(2)}) %collective-permute-start.4) | collective-permute-done | bytes 1179680 | tf_op jit(solution)/shard_map/ppermute | solution.py:147
  41.0 0.1 add_convert_fusion
  41.1 17.5 %all_to_all.15 = bf16[16,144,128]{2,1,0:T(8,128)(2,1)S(1)} all-to-all(bf16[16,144,128]{2,1,0:T(8,128)(2,1)S(1)} %bitcast.21), channel_id=1, replica_groups=mesh['y'=4,'x_lo'=2,'core'=2,'z'=8,'x_hi'=2] {'y','x_hi','x_lo'}, dimensions={0} | all-to-all | bytes 1179648 | tf_op jit(solution)/shard_map/all_to_all | solution.py:133
  58.6 0.1 reduce_sum.21
  58.7 12.1 %all_to_all.16 = bf16[8,144,128]{2,1,0:T(8,128)(2,1)S(1)} all-to-all(bf16[8,144,128]{2,1,0:T(8,128)(2,1)S(1)} %broadcast_in_dim.32), channel_id=1, replica_groups=mesh['y'=4,'x_lo'=2,'core'=2,'z'=8,'x_hi'=2] {'z'}, dimensions={0} | all-to-all | bytes 589824 | tf_op jit(solution)/shard_map/all_to_all | solution.py:133
  70.9 0.0 copy-start.3
  70.9 0.1 broadcast_in_dim.33
  71.0 13.7 %all_to_all.17 = bf16[16,144,128]{2,1,0:T(8,128)(2,1)S(1)} all-to-all(bf16[16,144,128]{2,1,0:T(8,128)(2,1)S(1)} %broadcast_in_dim.33), channel_id=1, replica_groups=mesh['y'=4,'x_lo'=2,'core'=2,'z'=8,'x_hi'=2] {'y','x_hi','x_lo'}, dimensions={0} | all-to-all | bytes 1179648 | tf_op jit(solution)/shard_map/all_to_all | solution.py:133
  84.7 4.7 %collective-permute-start.5 = (bf16[9,256,128]{2,1,0:T(8,128)(2,1)S(1)}, bf16[9,256,128]{2,1,0:T(8,128)(2,1)S(1)}, u32[]{:S(2)}, u32[]{:S(2)}) collective-permute-start(bf16[9,256,128]{2,1,0:T(8,128)(2,1)S(1)} %bitcast.19), channel_id=1, source_target_pairs={{0,16},{16,0},{1,17},{17,1},{2,18},{18,2},{3,19},{19,3},{4,20},{20... | collective-permute-start | bytes 1769480 | tf_op jit(solution)/shard_map/ppermute | solution.py:153
  89.4 0.0 copy-done.3
  89.4 0.0 copy-start.2
  89.4 2.3 %copy-done.2 = bf16[9,1024,256]{2,1,0:T(8,128)(2,1)S(1)} copy-done((bf16[9,1024,256]{2,1,0:T(8,128)(2,1)S(1)}, bf16[9,1024,256]{2,1,0:T(8,128)(2,1)}, u32[]{:S(2)}) %copy-start.2) | copy-done | bytes 4718616
  91.7 2.0 %shard_map.69 = bf16[256,1024]{1,0:T(8,128)(2,1)S(1)} custom-call(bf16[9,256,256]{2,1,0:T(8,128)(2,1)S(1)} %copy-done.3, bf16[9,1024,256]{2,1,0:T(8,128)(2,1)S(1)} %copy-done.2), custom_call_target="tpu_custom_call" | custom-call | flops 1200000000 | bytes 7000000 | tf_op jit(solution)/shard_map/pallas_call | solution.py:122
  93.8 0.9 copy.17
  94.6 0.0 collective-permute-done.5
  94.6 0.1 broadcast_select_fusion.1
  94.7 1.6 %maximum_convert_fusion = f32[9,256,256]{2,1,0:T(8,128)} fusion(bf16[9,256,128]{2,1,0:T(8,128)(2,1)S(1)} %get-tuple-element.9, bf16[9,256,128]{2,1,0:T(8,128)(2,1)S(1)} %get-tuple-element.8), kind=kLoop, calls=%fused_computation | loop fusion | flops 2359296 | bytes 3538944 | tf_op jit(solution)/shard_map/convert_element_type | solution.py:155
  (20 shorter events, 0.3 us)
Async XLA Ops:
  0.6 8.0 %copy-start = (bf16[9,128,7,33]{1,2,3,0:T(8,128)(2,1)S(1)}, bf16[9,128,7,33]{1,2,3,0:T(8,128)(2,1)}, u32[]{:S(2)}) copy-start(bf16[9,128,7,33]{1,2,3,0:T(8,128)(2,1)} %param.8) | copy-start | bytes 1596676
  2.1 7.3 %copy-start.5 = (s32[128]{0:T(128)S(1)}, s32[128]{0:T(128)}, u32[]{:S(2)}) copy-start(s32[128]{0:T(128)} %param.9) | copy-start | bytes 1540
  2.1 8.5 %collective-permute-start = (bf16[3,128,256]{2,1,0:T(8,128)(2,1)S(1)}, bf16[3,128,256]{2,1,0:T(8,128)(2,1)S(1)}, u32[]{:S(2)}, u32[]{:S(2)}) collective-permute-start(bf16[3,128,256]{2,1,0:T(8,128)(2,1)S(1)} %get-tuple-element.13), channel_id=1, source_target_pairs={{0,16},{16,32},{32,48},{48,64},{64,80},{80,96},{96,112},{112,128},... | collective-permute-start | bytes 589832 | tf_op jit(solution)/shard_map/ppermute | solution.py:20
  6.6 7.0 %collective-permute-start.1 = (bf16[3,128,256]{2,1,0:T(8,128)(2,1)S(1)}, bf16[3,128,256]{2,1,0:T(8,128)(2,1)S(1)}, u32[]{:S(2)}, u32[]{:S(2)}) collective-permute-start(bf16[3,128,256]{2,1,0:T(8,128)(2,1)S(1)} %get-tuple-element.12), channel_id=1, source_target_pairs={{16,0},{32,16},{48,32},{64,48},{80,64},{96,80},{112,96},{128,112},... | collective-permute-start | bytes 589832 | tf_op jit(solution)/shard_map/ppermute | solution.py:20
  10.5 11.3 %copy-start.4 = (bf16[256,8,128]{2,1,0:T(8,128)(2,1)S(1)}, bf16[256,8,128]{2,1,0:T(8,128)(2,1)}, u32[]{:S(2)}) copy-start(bf16[256,8,128]{2,1,0:T(8,128)(2,1)} %param.5) | copy-start | bytes 1572868
  13.6 9.6 %collective-permute-start.3 = (bf16[14,16,256]{2,1,0:T(8,128)(2,1)S(1)}, bf16[14,16,256]{2,1,0:T(8,128)(2,1)S(1)}, u32[]{:S(2)}, u32[]{:S(2)}) collective-permute-start(bf16[14,16,256]{2,1,0:T(8,128)(2,1)S(1)} %pad_maximum_fusion.1), channel_id=1, source_target_pairs={{0,15},{1,0},{2,1},{3,2},{4,3},{5,4},{6,5},{7,6},{8,7},{9,8},{10,9... | collective-permute-start | bytes 344072 | tf_op jit(solution)/shard_map/ppermute | solution.py:20
  21.4 7.3 %collective-permute-start.2 = (bf16[14,16,256]{2,1,0:T(8,128)(2,1)S(1)}, bf16[14,16,256]{2,1,0:T(8,128)(2,1)S(1)}, u32[]{:S(2)}, u32[]{:S(2)}) collective-permute-start(bf16[14,16,256]{2,1,0:T(8,128)(2,1)S(1)} %pad_maximum_fusion), channel_id=1, source_target_pairs={{0,1},{1,2},{2,3},{3,4},{4,5},{5,6},{6,7},{7,8},{8,9},{9,10},{10,1... | collective-permute-start | bytes 344072 | tf_op jit(solution)/shard_map/ppermute | solution.py:20
  36.0 2.1 %copy-start.1 = (bf16[9,1024,256]{2,1,0:T(8,128)(2,1)}, bf16[9,1024,256]{2,1,0:T(8,128)(2,1)S(1)}, u32[]{:S(2)}) copy-start(bf16[9,1024,256]{2,1,0:T(8,128)(2,1)S(1)} %get-tuple-element.5.q_ref) | copy-start | bytes 14155780
  38.1 2.8 %collective-permute-start.4 = (f32[9,256,128]{2,1,0:T(8,128)S(1)}, f32[9,256,128]{2,1,0:T(8,128)S(1)}, u32[]{:S(2)}, u32[]{:S(2)}) collective-permute-start(f32[9,256,128]{2,1,0:T(8,128)S(1)} %get-tuple-element.7), channel_id=1, source_target_pairs={{0,16},{16,0},{1,17},{17,1},{2,18},{18,2},{3,19},{19,3},{4,20},{20... | collective-permute-start | bytes 3538952 | tf_op jit(solution)/shard_map/ppermute | solution.py:147
  70.9 18.5 %copy-start.3 = (bf16[9,256,256]{2,1,0:T(8,128)(2,1)S(1)}, bf16[9,256,256]{2,1,0:T(8,128)(2,1)}, u32[]{:S(2)}) copy-start(bf16[9,256,256]{2,1,0:T(8,128)(2,1)} %w_ref.1) | copy-start | bytes 3538948
  84.7 9.9 %collective-permute-start.5 = (bf16[9,256,128]{2,1,0:T(8,128)(2,1)S(1)}, bf16[9,256,128]{2,1,0:T(8,128)(2,1)S(1)}, u32[]{:S(2)}, u32[]{:S(2)}) collective-permute-start(bf16[9,256,128]{2,1,0:T(8,128)(2,1)S(1)} %bitcast.19), channel_id=1, source_target_pairs={{0,16},{16,0},{1,17},{17,1},{2,18},{18,2},{3,19},{19,3},{4,20},{20... | collective-permute-start | bytes 1769480 | tf_op jit(solution)/shard_map/ppermute | solution.py:153
  89.4 2.3 %copy-start.2 = (bf16[9,1024,256]{2,1,0:T(8,128)(2,1)S(1)}, bf16[9,1024,256]{2,1,0:T(8,128)(2,1)}, u32[]{:S(2)}) copy-start(bf16[9,1024,256]{2,1,0:T(8,128)(2,1)} %copy-done.1) | copy-start | bytes 14155780

commit v2 on v1

v2 whole, which is shorter than its diff:
```python
import jax
import jax.numpy as jnp
from jax import lax
from jax.experimental import pallas as pl
from jax.experimental.pallas import tpu as pltpu
from jax.sharding import Mesh, PartitionSpec as P

LAT = ("y", "x_lo", "core")
LON = ("z", "x_hi")
PLANE = ("y", "x_hi", "x_lo")
BLOCK = 32
bf16, f32 = jnp.bfloat16, jnp.float32


def shift(x, axes, step, closed):
    count = 1
    for axis in axes:
        count *= lax.axis_size(axis)
    pairs = [(i, (i + step) % count) for i in range(count) if closed or 0 <= i + step < count]
    return lax.ppermute(x, axes, pairs)


def tap_rows(basis_table, lon_reach, first_row, lat_dev):
    basis_count, nlat_all, row_span, tap_count = basis_table.shape
    half = row_span // 2
    near = lat_dev + 2 * half
    start = jnp.clip(first_row - half, 0, nlat_all - near)
    table = lax.dynamic_slice_in_dim(basis_table, start, near, 1)
    reach = lax.dynamic_slice_in_dim(lon_reach, start, near, 0)
    offset = jnp.abs(lax.iota(jnp.int32, tap_count) - tap_count // 2)
    table = jnp.where((offset[None, :] <= reach[:, None])[None, :, None, :], table, jnp.zeros_like(table))
    table = jnp.pad(table, ((0, 0), (half, half), (0, 0), (0, 0)))
    table = lax.dynamic_slice_in_dim(table, first_row - start, near, 1)
    table = jnp.flip(table, 3)
    rows = jnp.stack(
        [table[:, s : s + lat_dev, row_span - 1 - s, :] for s in range(row_span)], axis=2
    )
    rows = jnp.pad(rows, ((0, 0), (0, 0), (0, 1), (0, 2 * BLOCK - tap_count)))
    rows = jnp.transpose(rows, (1, 0, 2, 3)).astype(f32)
    return rows.reshape(lat_dev, basis_count, (row_span + 1) * BLOCK * 2 // 128, 128)


def band_kernel(taps, band):
    lat_dev, basis_count, groups, _ = taps.shape
    for i in range(lat_dev):
        for k in range(basis_count):
            for p in range(groups):
                line = jnp.broadcast_to(taps[i, k, p : p + 1, :], (BLOCK, 128))
                line = pltpu.roll(line, 0, 1, stride=1, stride_axis=0)
                band[i, k * BLOCK : (k + 1) * BLOCK, p * 128 : (p + 1) * 128] = line.astype(bf16)


def convolve(band, ext, place, q_ref):
    basis_count, lat_dev, columns, _ = q_ref.shape
    row_span = ext.shape[0] - lat_dev + 1
    for i in range(lat_dev):
        for j in range(columns // BLOCK):
            parts = [ext[(i + s,) + place(j)] for s in range(row_span)]
            window = jnp.concatenate(parts + [jnp.zeros_like(parts[0])], axis=0)
            out = jnp.dot(band[i], window, preferred_element_type=f32).astype(bf16)
            for k in range(basis_count):
                q_ref[k, i, j * BLOCK : (j + 1) * BLOCK, :] = out[k * BLOCK : (k + 1) * BLOCK, :]


def middle_kernel(band, main, up, down, f_ref, q_ref, total, ext):
    lat_dev, half = main.shape[0], up.shape[0]
    ext[:half] = up[...]
    ext[half : half + lat_dev] = main[...]
    ext[half + lat_dev :] = down[...]
    side = BLOCK // 2
    convolve(band, ext, lambda j: (slice(side + j * BLOCK, side + (j + 2) * BLOCK),), q_ref)
    for k in range(q_ref.shape[0]):
        cells = q_ref[k].reshape(f_ref.shape[1], q_ref.shape[3])
        total[k] = jnp.dot(f_ref[...], cells, preferred_element_type=f32)


def edge_kernel(core_ref, band, main, up, down, left, right, f_ref, total, q_ref, keep, send, ext):
    lat_dev, lon_dev, channels = main.shape
    half, side = up.shape[0], left.shape[1]
    inner = 2 * BLOCK - side
    for first, last, source in ((0, half, up), (half, half + lat_dev, main), (half + lat_dev, 2 * half + lat_dev, down)):
        ext[first:last, 0, side:, :] = source[:, :inner, :]
        ext[first:last, 1, :inner, :] = source[:, lon_dev - inner :, :]
    ext[:, 0, :side, :] = left[...]
    ext[:, 1, inner:, :] = right[...]
    convolve(band, ext, lambda j: (j,), q_ref)
    low_core = core_ref[0] == 0
    for k in range(q_ref.shape[0]):
        cells = q_ref[k].reshape(f_ref.shape[1], channels)
        out = total[k] + jnp.dot(f_ref[...], cells, preferred_element_type=f32)
        low, high = out[:, : channels // 2], out[:, channels // 2 :]
        keep[k] = jnp.where(low_core, low, high)
        send[k] = jnp.where(low_core, high, low)


def call(kernel, out_shape, operands, scratch=(), scalars=0, flops=10**9):
    vmem = pl.BlockSpec(memory_space=pltpu.VMEM)
    smem = pl.BlockSpec(memory_space=pltpu.SMEM)
    return pl.pallas_call(
        kernel,
        out_shape=out_shape,
        in_specs=[smem] * scalars + [vmem] * (len(operands) - scalars),
        out_specs=jax.tree.map(lambda _: vmem, out_shape),
        scratch_shapes=list(scratch),
        compiler_params=pltpu.CompilerParams(vmem_limit_bytes=40 * 1024 * 1024),
        cost_estimate=pl.CostEstimate(flops=flops, bytes_accessed=10**6, transcendentals=0),
    )(*operands)


def mix_kernel(w_ref, mid_ref, edge_ref, out_ref):
    basis_count, lat_dev, columns, channels = mid_ref.shape
    for i in range(0, lat_dev, 2):
        total = jnp.zeros((channels, 4 * columns), f32)
        for k in range(basis_count):
            parts = []
            for row in (i, i + 1):
                parts += [edge_ref[k, row, :BLOCK], mid_ref[k, row], edge_ref[k, row, BLOCK:]]
            total += lax.dot_general(
                w_ref[k], jnp.concatenate(parts, axis=0), (((1,), (1,)), ((), ())), preferred_element_type=f32
            )
        out_ref[:, i * 2 * columns : (i + 2) * 2 * columns] = total.astype(bf16)


def all_to_all(x, axes):
    return lax.all_to_all(x, axes, 0, 0, tiled=True)


def to_all(x, count):
    return jnp.broadcast_to(x[None], (count,) + x.shape)


def reduce_all(keep, send, core, scale, beside):
    swap = [(0, 1), (1, 0)]
    basis_count, channels, half = keep.shape
    plane = 1
    for axis in PLANE:
        plane *= lax.axis_size(axis)
    depth = lax.axis_size("z")
    came, beside = lax.optimization_barrier((lax.ppermute(send, "core", swap), beside))
    own = keep + came
    own = own.reshape(plane, -1, half).astype(bf16)
    own = jnp.sum(all_to_all(own, PLANE).astype(f32), axis=0).astype(bf16)
    own = jnp.sum(all_to_all(to_all(own, depth), ("z",)).astype(f32), axis=0)
    own = (own * scale).astype(bf16)
    own = all_to_all(to_all(own, plane), PLANE).reshape(basis_count, channels, half)
    other = lax.ppermute(own, "core", swap)
    low, high = jnp.where(core == 0, own, other), jnp.where(core == 0, other, own)
    return jnp.concatenate([low, high], axis=2).astype(f32), beside


def local(fields, grad_out, weight, basis_table, lon_reach):
    channels, lat_dev, lon_dev = fields.shape
    nlat_all = basis_table.shape[1]
    half, side = basis_table.shape[2] // 2, basis_table.shape[3] // 2
    core = lax.axis_index("core")
    taps = tap_rows(basis_table, lon_reach, lax.axis_index(LAT) * lat_dev, lat_dev)
    main = jnp.transpose(grad_out, (1, 2, 0))
    up = shift(main[lat_dev - half :], LAT, 1, False)
    down = shift(main[:half], LAT, -1, False)
    tall = lambda at: jnp.concatenate([up[:, at], main[:, at], down[:, at]], axis=0)
    left = shift(tall(slice(lon_dev - side, lon_dev)), LON, 1, True)
    right = shift(tall(slice(0, side)), LON, -1, True)
    basis_count = basis_table.shape[0]
    near = lat_dev + 2 * half
    wide = 2 * BLOCK
    f_mid = fields[:, :, BLOCK : lon_dev - BLOCK].reshape(channels, lat_dev * wide)
    f_edge = jnp.concatenate([fields[:, :, :BLOCK], fields[:, :, lon_dev - BLOCK :]], axis=2)
    f_edge = f_edge.reshape(channels, lat_dev * wide)
    shape = jax.ShapeDtypeStruct
    q_shape = shape((basis_count, lat_dev, wide, channels), bf16)
    part = shape((basis_count, channels, channels // 2), f32)
    band_shape = shape((lat_dev, basis_count * BLOCK, taps.shape[2] * 128), bf16)
    band = call(band_kernel, band_shape, (taps,))
    q_mid, total = call(
        middle_kernel,
        (q_shape, shape((basis_count, channels, channels), f32)),
        (band, main, up, down, f_mid),
        [pltpu.VMEM((near, lon_dev, channels), bf16)],
    )
    q_edge, keep, send = call(
        edge_kernel,
        (q_shape, part, part),
        (core[None].astype(jnp.int32), band, main, up, down, left, right, f_edge, total),
        [pltpu.VMEM((near, 2, wide, channels), bf16)],
        scalars=1,
    )
    mixed = call(mix_kernel, shape((channels, lat_dev * lon_dev), bf16), (weight, q_mid, q_edge))
    field_grad = mixed.reshape(channels, lat_dev, lon_dev)
    weight_grad, field_grad = reduce_all(keep, send, core, 1.0 / nlat_all, field_grad)
    return field_grad, weight_grad


def solution(mesh):
    fine = Mesh(mesh.devices.reshape(4, 2, 2, 8, 2), ("y", "x_lo", "core", "z", "x_hi"))
    split = P(None, LAT, LON)
    return jax.shard_map(
        local,
        mesh=fine,
        in_specs=(split, split, P(), P(), P()),
        out_specs=(split, P()),
        check_vma=False,
    )
```

time: 96.6 us -> 96.2 us (level)
  waiting for transfers between devices: 12.8 us -> 2.7 us
  local copies, waits for them, and re-layouts: 8.96 us -> 16.3 us
  other arithmetic: 2.07 us -> 4.12 us
  blocking collectives: 43.3 us -> 45.3 us
  Pallas kernels: 9.2 us -> 7.39 us
    ppermute x4, waiting for transfers between devices: 9.92 us -> 0.56 us  [shift(): return lax.ppermute(x, axes, pairs)]
    reshape x0 -> x2, local copies, waits for them, and re-layouts: none -> 3.59 us  [the longest x1 1.79 us: local(): fields[:, :, BLOCK:lon_dev - BLOCK].reshape(channels, lat_dev * wide)]
    ppermute x1, waiting for transfers between devices: 2.84 us -> 0.51 us  [reduce_all(): lax.ppermute(send, 'core', swap)]
    all_to_all x3, blocking collectives: 43.3 us -> 45.3 us  [all_to_all(): return lax.all_to_all(x, axes, 0, 0, tiled=True)]
    unnamed x22 -> x36, local copies, waits for them, and re-layouts: 7.47 us -> 9.3 us
    pallas_call x2 -> x4, Pallas kernels: 9.2 us -> 7.39 us  [call(): pl.pallas_call(kernel, out_shape=out_shape, in_specs=[smem] * scalars + [...]
    ppermute x1, waiting for transfers between devices: 0.01 us -> 1.63 us  [reduce_all(): other = lax.ppermute(own, 'core', swap)]
    concatenate x2, other arithmetic: 0.03 us -> 1.36 us  [local(): jnp.concatenate([up[:, at], main[:, at], down[:, at]], axis=0)]
  transfers between devices with their start and end apart: 6 -> 6, of which waited for: 4 -> 3; matrix products, arithmetic and copies ran while one was open for 3% -> 13% of each run, Pallas kernels for 2% -> 4%
where the time goes in v2:
time: 96.2 us; the launch traced here: 95.7 us
  blocking collectives  45.3 us (47%)
  starting transfers between devices  19 us (20%)
  local copies, waits for them, and re-layouts  16.3 us (17%)
  Pallas kernels  7.39 us (8%)
  other arithmetic  4.12 us (4%)
  waiting for transfers between devices  2.7 us (3%)
  between operations  0.97 us (1%)
    all_to_all x3, blocking collectives, all_to_all(): return lax.all_to_all(x, axes, 0, 0, tiled=True)  45.3 us
    ppermute x4, starting transfers between devices, shift(): return lax.ppermute(x, axes, pairs)  14.2 us
    unnamed x36, local copies, waits for them, and re-layouts  9.3 us
    pallas_call x4, Pallas kernels, call(): pl.pallas_call(kernel, out_shape=out_shape, in_specs=[smem] * scalars + [...  7.39 us
    ppermute x1, starting transfers between devices, reduce_all(): other = lax.ppermute(own, 'core', swap)  4.69 us
  transfers between devices with their start and end apart: 6, of which 3 were waited for; matrix products, arithmetic and copies ran while one was open for 13% of the time, Pallas kernels for 4%

profile of v2, /device:TPU:1, one launch (start us, length us, event | category | flops | bytes accessed | tf_op | source)
XLA Modules:
  0.0 95.7 jit_solution(2641591303881327382)
XLA Ops:
  0.6 0.0 copy-start
  0.6 0.0 copy-start.11
  0.7 1.4 %copy.26 = bf16[256,8,128]{0,2,1:T(8,128)(2,1)S(1)} copy(bf16[256,8,128]{2,1,0:T(8,128)(2,1)} %param.6) | data formatting | bytes 1048576 | tf_op args[1]
  2.1 4.5 %collective-permute-start = (bf16[3,128,256]{2,1,0:T(8,128)(2,1)S(1)}, bf16[3,128,256]{2,1,0:T(8,128)(2,1)S(1)}, u32[]{:S(2)}, u32[]{:S(2)}) collective-permute-start(bf16[3,128,256]{2,1,0:T(8,128)(2,1)S(1)} %get-tuple-element.23), channel_id=1, source_target_pairs={{0,16},{16,32},{32,48},{48,64},{64,80},{80,96},{96,112},{112,128},... | collective-permute-start | bytes 589832 | tf_op jit(solution)/shard_map/ppermute | solution.py:20
  6.6 1.9 %collective-permute-start.1 = (bf16[3,128,256]{2,1,0:T(8,128)(2,1)S(1)}, bf16[3,128,256]{2,1,0:T(8,128)(2,1)S(1)}, u32[]{:S(2)}, u32[]{:S(2)}) collective-permute-start(bf16[3,128,256]{2,1,0:T(8,128)(2,1)S(1)} %get-tuple-element.22), channel_id=1, source_target_pairs={{16,0},{32,16},{48,32},{64,48},{80,64},{96,80},{112,96},{128,112},... | collective-permute-start | bytes 589832 | tf_op jit(solution)/shard_map/ppermute | solution.py:20
  8.6 0.0 copy-done
  8.6 0.0 copy-start.9
  8.6 0.2 constant_dynamic-slice_fusion
  8.8 0.6 copy.32
  9.4 0.0 copy-done.11
  9.4 0.1 dynamic_slice.9
  9.5 0.1 broadcast_compare_fusion
  9.6 0.2 pad_dynamic-slice_fusion.6
  9.8 0.1 slice.76
  9.9 0.1 slice.78
  9.9 0.1 slice.80
  10.0 0.1 slice.82
  10.1 0.1 slice.84
  10.3 0.1 slice.86
  10.3 0.1 slice.88
  10.6 0.1 copy.25
  10.6 0.8 reshape.66.taps
  11.4 0.0 copy-done.9
  11.4 0.2 fusion
  11.6 0.3 copy.33
  11.9 0.3 copy.34
  12.3 0.7 pad_maximum_fusion
  13.0 0.0 collective-permute-done.up
  13.0 0.0 copy-start.3
  13.0 0.6 collective-permute-done.1.down
  13.6 0.7 pad_maximum_fusion.1
  14.3 2.5 %collective-permute-start.2 = (bf16[14,16,256]{2,1,0:T(8,128)(2,1)}, bf16[14,16,256]{2,1,0:T(8,128)(2,1)}, u32[]{:S(2)}, u32[]{:S(2)}) collective-permute-start(bf16[14,16,256]{2,1,0:T(8,128)(2,1)} %pad_maximum_fusion.1), channel_id=1, source_target_pairs={{0,1},{1,2},{2,3},{3,4},{4,5},{5,6},{6,7},{7,8},{8,9},{9,10},{10,1... | collective-permute-start | bytes 344072 | tf_op jit(solution)/shard_map/ppermute | solution.py:20
  16.7 0.7 pad_maximum_fusion.2
  17.4 5.3 %collective-permute-start.3 = (bf16[14,16,256]{2,1,0:T(8,128)(2,1)}, bf16[14,16,256]{2,1,0:T(8,128)(2,1)}, u32[]{:S(2)}, u32[]{:S(2)}) collective-permute-start(bf16[14,16,256]{2,1,0:T(8,128)(2,1)} %pad_maximum_fusion.2), channel_id=1, source_target_pairs={{0,15},{1,0},{2,1},{3,2},{4,3},{5,4},{6,5},{7,6},{8,7},{9,8},{10,9... | collective-permute-start | bytes 344072 | tf_op jit(solution)/shard_map/ppermute | solution.py:20
  22.7 0.9 copy-done.8
  23.6 0.7 shard_map.68.band
  24.3 0.0 copy-done.10
  24.3 1.0 %slice.99 = bf16[256,8,64]{2,1,0:T(8,128)(2,1)} slice(bf16[256,8,128]{2,1,0:T(8,128)(2,1)S(1)} %copy-done.10), slice={[0:256], [0:8], [32:96]} | slice | bytes 524288 | tf_op jit(solution)/shard_map/slice | solution.py:166
  25.3 2.0 %copy.35 = bf16[256,8,64]{0,2,1:T(8,128)(2,1)} copy(bf16[256,8,64]{2,1,0:T(8,128)(2,1)} %slice.99) | data formatting | bytes 524288
  27.3 1.8 %copy.30.f_ref = bf16[256,512]{1,0:T(8,128)(2,1)} copy(bf16[256,512]{0,1:T(8,128)(2,1)} %bitcast.20) | data formatting | bytes 524288 | tf_op jit(solution)/shard_map/reshape | solution.py:166
  29.1 1.8 %copy.31.f_ref = bf16[256,512]{1,0:T(8,128)(2,1)} copy(bf16[256,512]{0,1:T(8,128)(2,1)} %bitcast.21) | data formatting | bytes 524288 | tf_op jit(solution)/shard_map/reshape | solution.py:168
  30.9 0.9 copy-done.4
  31.9 0.9 copy-done.6
  32.8 0.9 copy-done.7
  33.7 2.1 %shard_map.69 = (bf16[9,8,64,256]{3,2,1,0:T(8,128)(2,1)S(1)}, f32[9,256,256]{2,1,0:T(8,128)S(1)}) custom-call(bf16[8,288,512]{2,1,0:T(8,128)(2,1)S(1)} %shard_map.68.band, bf16[8,128,256]{2,1,0:T(8,128)(2,1)S(1)} %bitcast.14, bf16[3,128,256]{2,1,0:T(8,128)(2,1)S(1)} %copy-done.4, bf16[3,128,256]{2,1,0:T(8,128)(2,1)S(1)} %copy-done.6, ...), custom_call_target="tpu_custom_call" | custom-call | flops 1000000000 | bytes 1000000 | tf_op jit(solution)/shard_map/pallas_call | solution.py:99
  35.9 0.0 collective-permute-done.2.left
  35.9 0.0 collective-permute-done.3.right
  35.9 0.0 copy-done.2
  35.9 0.0 copy-start.1
  35.9 3.2 %shard_map.70 = (bf16[9,8,64,256]{3,2,1,0:T(8,128)(2,1)S(1)}, f32[9,256,128]{2,1,0:T(8,128)S(1)}, f32[9,256,128]{2,1,0:T(8,128)S(1)}) custom-call(s32[1]{0:T(128)} %bitcast.core_ref, bf16[8,288,512]{2,1,0:T(8,128)(2,1)S(1)} %shard_map.68.band, bf16[8,128,256]{2,1,0:T(8,128)(2,1)S(1)} %bitcast.15, bf16[3,128,256]{2,1,0:T(8,128)(2,1)S(1)} %copy-done.4, ...), custom_call_target="tpu_custom_call" | custom-call | flops 1000000000 | bytes 1000000 | tf_op jit(solution)/shard_map/pallas_call | solution.py:99
  39.1 0.1 collective-permute-start.4
  39.2 1.4 %shard_map.71 = bf16[256,1024]{1,0:T(8,128)(2,1)S(1)} custom-call(bf16[9,256,256]{2,1,0:T(8,128)(2,1)S(1)} %copy-done.1, bf16[9,8,64,256]{3,2,1,0:T(8,128)(2,1)S(1)} %get-tuple-element.11.mid_ref, bf16[9,8,64,256]{3,2,1,0:T(8,128)(2,1)S(1)} %get-tuple-element.12.edge_ref), custom_call_target="tpu_custom_call" | custom-call | flops 1000000000 | bytes 1000000 | tf_op jit(solution)/shard_map/pallas_call | solution.py:99
  40.6 0.9 copy.36
  41.5 0.5 collective-permute-done.4
  42.0 0.1 add_convert_fusion
  42.1 16.9 %all_to_all.15 = bf16[16,144,128]{2,1,0:T(8,128)(2,1)S(1)} all-to-all(bf16[16,144,128]{2,1,0:T(8,128)(2,1)S(1)} %bitcast.19), channel_id=1, replica_groups=mesh['y'=4,'x_lo'=2,'core'=2,'z'=8,'x_hi'=2] {'y','x_hi','x_lo'}, dimensions={0} | all-to-all | bytes 1179648 | tf_op jit(solution)/shard_map/all_to_all | solution.py:125
  59.1 0.1 reduce_sum.21
  59.2 15.4 %all_to_all.16 = bf16[8,144,128]{2,1,0:T(8,128)(2,1)S(1)} all-to-all(bf16[8,144,128]{2,1,0:T(8,128)(2,1)S(1)} %broadcast_in_dim.32), channel_id=1, replica_groups=mesh['y'=4,'x_lo'=2,'core'=2,'z'=8,'x_hi'=2] {'z'}, dimensions={0} | all-to-all | bytes 589824 | tf_op jit(solution)/shard_map/all_to_all | solution.py:125
  74.6 0.1 broadcast_in_dim.33
  74.7 13.0 %all_to_all.17 = bf16[16,144,128]{2,1,0:T(8,128)(2,1)S(1)} all-to-all(bf16[16,144,128]{2,1,0:T(8,128)(2,1)S(1)} %broadcast_in_dim.33), channel_id=1, replica_groups=mesh['y'=4,'x_lo'=2,'core'=2,'z'=8,'x_hi'=2] {'y','x_hi','x_lo'}, dimensions={0} | all-to-all | bytes 1179648 | tf_op jit(solution)/shard_map/all_to_all | solution.py:125
  87.7 4.7 %collective-permute-start.5 = (bf16[9,256,128]{2,1,0:T(8,128)(2,1)S(1)}, bf16[9,256,128]{2,1,0:T(8,128)(2,1)S(1)}, u32[]{:S(2)}, u32[]{:S(2)}) collective-permute-start(bf16[9,256,128]{2,1,0:T(8,128)(2,1)S(1)} %bitcast.17), channel_id=1, source_target_pairs={{0,16},{16,0},{1,17},{17,1},{2,18},{18,2},{3,19},{19,3},{4,20},{20... | collective-permute-start | bytes 1769480 | tf_op jit(solution)/shard_map/ppermute | solution.py:146
  92.4 1.6 %collective-permute-done.5 = bf16[9,256,128]{2,1,0:T(8,128)(2,1)S(1)} collective-permute-done((bf16[9,256,128]{2,1,0:T(8,128)(2,1)S(1)}, bf16[9,256,128]{2,1,0:T(8,128)(2,1)S(1)}, u32[]{:S(2)}, u32[]{:S(2)}) %collective-permute-start.5) | collective-permute-done | bytes 589856 | tf_op jit(solution)/shard_map/ppermute | solution.py:146
  94.0 0.1 broadcast_select_fusion.1
  94.1 1.6 %maximum_convert_fusion = f32[9,256,256]{2,1,0:T(8,128)} fusion(bf16[9,256,128]{2,1,0:T(8,128)(2,1)S(1)} %get-tuple-element.17, bf16[9,256,128]{2,1,0:T(8,128)(2,1)S(1)} %get-tuple-element.16), kind=kLoop, calls=%fused_computation | loop fusion | flops 2359296 | bytes 3538944 | tf_op jit(solution)/shard_map/convert_element_type | solution.py:148
  (28 shorter events, 0.3 us)
Async XLA Ops:
  0.6 8.0 %copy-start = (bf16[9,128,7,33]{1,2,3,0:T(8,128)(2,1)S(1)}, bf16[9,128,7,33]{1,2,3,0:T(8,128)(2,1)}, u32[]{:S(2)}) copy-start(bf16[9,128,7,33]{1,2,3,0:T(8,128)(2,1)} %param.8) | copy-start | bytes 1596676
  0.6 8.7 %copy-start.11 = (s32[128]{0:T(128)S(1)}, s32[128]{0:T(128)}, u32[]{:S(2)}) copy-start(s32[128]{0:T(128)} %param.9) | copy-start | bytes 1540
  2.1 10.9 %collective-permute-start = (bf16[3,128,256]{2,1,0:T(8,128)(2,1)S(1)}, bf16[3,128,256]{2,1,0:T(8,128)(2,1)S(1)}, u32[]{:S(2)}, u32[]{:S(2)}) collective-permute-start(bf16[3,128,256]{2,1,0:T(8,128)(2,1)S(1)} %get-tuple-element.23), channel_id=1, source_target_pairs={{0,16},{16,32},{32,48},{48,64},{64,80},{80,96},{96,112},{112,128},... | collective-permute-start | bytes 589832 | tf_op jit(solution)/shard_map/ppermute | solution.py:20
  6.6 7.0 %collective-permute-start.1 = (bf16[3,128,256]{2,1,0:T(8,128)(2,1)S(1)}, bf16[3,128,256]{2,1,0:T(8,128)(2,1)S(1)}, u32[]{:S(2)}, u32[]{:S(2)}) collective-permute-start(bf16[3,128,256]{2,1,0:T(8,128)(2,1)S(1)} %get-tuple-element.22), channel_id=1, source_target_pairs={{16,0},{32,16},{48,32},{64,48},{80,64},{96,80},{112,96},{128,112},... | collective-permute-start | bytes 589832 | tf_op jit(solution)/shard_map/ppermute | solution.py:20
  8.6 2.8 %copy-start.9 = (bf16[256,8,128]{2,1,0:T(8,128)(2,1)S(1)}, bf16[256,8,128]{2,1,0:T(8,128)(2,1)}, u32[]{:S(2)}) copy-start(bf16[256,8,128]{2,1,0:T(8,128)(2,1)} %param.5) | copy-start | bytes 1572868
  13.0 11.3 %copy-start.10 = (bf16[256,8,128]{2,1,0:T(8,128)(2,1)S(1)}, bf16[256,8,128]{2,1,0:T(8,128)(2,1)}, u32[]{:S(2)}) copy-start(bf16[256,8,128]{2,1,0:T(8,128)(2,1)} %param.5) | copy-start | bytes 1572868
  13.0 4.4 %copy-start.3 = (bf16[3,128,256]{2,1,0:T(8,128)(2,1)}, bf16[3,128,256]{2,1,0:T(8,128)(2,1)S(1)}, u32[]{:S(2)}) copy-start(bf16[3,128,256]{2,1,0:T(8,128)(2,1)S(1)} %collective-permute-done.up) | copy-start | bytes 589828
  13.6 3.8 %copy-start.5 = (bf16[3,128,256]{2,1,0:T(8,128)(2,1)}, bf16[3,128,256]{2,1,0:T(8,128)(2,1)S(1)}, u32[]{:S(2)}) copy-start(bf16[3,128,256]{2,1,0:T(8,128)(2,1)S(1)} %collective-permute-done.1.down) | copy-start | bytes 589828
  14.3 21.6 %collective-permute-start.2 = (bf16[14,16,256]{2,1,0:T(8,128)(2,1)}, bf16[14,16,256]{2,1,0:T(8,128)(2,1)}, u32[]{:S(2)}, u32[]{:S(2)}) collective-permute-start(bf16[14,16,256]{2,1,0:T(8,128)(2,1)} %pad_maximum_fusion.1), channel_id=1, source_target_pairs={{0,1},{1,2},{2,3},{3,4},{4,5},{5,6},{6,7},{7,8},{8,9},{9,10},{10,1... | collective-permute-start | bytes 344072 | tf_op jit(solution)/shard_map/ppermute | solution.py:20
  17.4 18.5 %collective-permute-start.3 = (bf16[14,16,256]{2,1,0:T(8,128)(2,1)}, bf16[14,16,256]{2,1,0:T(8,128)(2,1)}, u32[]{:S(2)}, u32[]{:S(2)}) collective-permute-start(bf16[14,16,256]{2,1,0:T(8,128)(2,1)} %pad_maximum_fusion.2), channel_id=1, source_target_pairs={{0,15},{1,0},{2,1},{3,2},{4,3},{5,4},{6,5},{7,6},{8,7},{9,8},{10,9... | collective-permute-start | bytes 344072 | tf_op jit(solution)/shard_map/ppermute | solution.py:20
  22.7 0.9 copy-start.8
  30.9 0.9 copy-start.4
  31.8 0.9 copy-start.6
  32.8 0.9 copy-start.7
  33.7 2.2 %copy-start.2 = (bf16[256,512]{1,0:T(8,128)(2,1)S(1)}, bf16[256,512]{1,0:T(8,128)(2,1)}, u32[]{:S(2)}) copy-start(bf16[256,512]{1,0:T(8,128)(2,1)} %copy.31.f_ref) | copy-start | bytes 786436
  35.9 3.3 %copy-start.1 = (bf16[9,256,256]{2,1,0:T(8,128)(2,1)S(1)}, bf16[9,256,256]{2,1,0:T(8,128)(2,1)}, u32[]{:S(2)}) copy-start(bf16[9,256,256]{2,1,0:T(8,128)(2,1)} %w_ref.1) | copy-start | bytes 3538948
  39.1 2.9 %collective-permute-start.4 = (f32[9,256,128]{2,1,0:T(8,128)S(1)}, f32[9,256,128]{2,1,0:T(8,128)S(1)}, u32[]{:S(2)}, u32[]{:S(2)}) collective-permute-start(f32[9,256,128]{2,1,0:T(8,128)S(1)} %get-tuple-element.10), channel_id=1, source_target_pairs={{0,16},{16,0},{1,17},{17,1},{2,18},{18,2},{3,19},{19,3},{4,20},{20... | collective-permute-start | bytes 3538952 | tf_op jit(solution)/shard_map/ppermute | solution.py:139
  87.7 6.3 %collective-permute-start.5 = (bf16[9,256,128]{2,1,0:T(8,128)(2,1)S(1)}, bf16[9,256,128]{2,1,0:T(8,128)(2,1)S(1)}, u32[]{:S(2)}, u32[]{:S(2)}) collective-permute-start(bf16[9,256,128]{2,1,0:T(8,128)(2,1)S(1)} %bitcast.17), channel_id=1, source_target_pairs={{0,16},{16,0},{1,17},{17,1},{2,18},{18,2},{3,19},{19,3},{4,20},{20... | collective-permute-start | bytes 1769480 | tf_op jit(solution)/shard_map/ppermute | solution.py:146

commit v3 on v2

--- a/solution.py
+++ b/solution.py
@@ -20,34 +20,50 @@
     return lax.ppermute(x, axes, pairs)
 
 
-def tap_rows(basis_table, lon_reach, first_row, lat_dev):
-    basis_count, nlat_all, row_span, tap_count = basis_table.shape
-    half = row_span // 2
-    near = lat_dev + 2 * half
-    start = jnp.clip(first_row - half, 0, nlat_all - near)
+def tap_rows(basis_table, lon_reach, start, near):
+    basis_count, _, row_span, tap_count = basis_table.shape
     table = lax.dynamic_slice_in_dim(basis_table, start, near, 1)
     reach = lax.dynamic_slice_in_dim(lon_reach, start, near, 0)
     offset = jnp.abs(lax.iota(jnp.int32, tap_count) - tap_count // 2)
     table = jnp.where((offset[None, :] <= reach[:, None])[None, :, None, :], table, jnp.zeros_like(table))
-    table = jnp.pad(table, ((0, 0), (half, half), (0, 0), (0, 0)))
-    table = lax.dynamic_slice_in_dim(table, first_row - start, near, 1)
-    table = jnp.flip(table, 3)
-    rows = jnp.stack(
-        [table[:, s : s + lat_dev, row_span - 1 - s, :] for s in range(row_span)], axis=2
-    )
-    rows = jnp.pad(rows, ((0, 0), (0, 0), (0, 1), (0, 2 * BLOCK - tap_count)))
-    rows = jnp.transpose(rows, (1, 0, 2, 3)).astype(f32)
-    return rows.reshape(lat_dev, basis_count, (row_span + 1) * BLOCK * 2 // 128, 128)
-
-
-def band_kernel(taps, band):
-    lat_dev, basis_count, groups, _ = taps.shape
+    table = jnp.flip(table, (2, 3)).astype(f32)
+    table = jnp.pad(table, ((0, 0), (0, 0), (0, 1), (0, 2 * BLOCK - tap_count)))
+    table = jnp.transpose(table, (1, 0, 2, 3))
+    return table.reshape(near, basis_count, (row_span + 1) * BLOCK * 2 // 128, 128)
+
+
+def prepare_kernel(off_ref, taps, f_ref, band, f_mid, f_edge):
+    near, basis_count, groups, _ = taps.shape
+    lat_dev = band.shape[0]
+    lane = lax.broadcasted_iota(jnp.int32, (1, 128), 1)
+    rows = [jnp.clip(off_ref[0] + r, 0, near - 1) for r in range(near + 1)]
     for i in range(lat_dev):
         for k in range(basis_count):
             for p in range(groups):
-                line = jnp.broadcast_to(taps[i, k, p : p + 1, :], (BLOCK, 128))
+                first = taps[rows[i + 2 * p], k, p : p + 1, :]
+                second = taps[rows[i + 2 * p + 1], k, p : p + 1, :]
+                line = jnp.broadcast_to(jnp.where(lane < 2 * BLOCK, first, second), (BLOCK, 128))
                 line = pltpu.roll(line, 0, 1, stride=1, stride_axis=0)
                 band[i, k * BLOCK : (k + 1) * BLOCK, p * 128 : (p + 1) * 128] = line.astype(bf16)
+    for i in range(0, lat_dev, 2):
+        even = f_ref[:, i * 128 : (i + 1) * 128].astype(f32)
+        odd = f_ref[:, (i + 1) * 128 : (i + 2) * 128].astype(f32)
+        back = lambda x: pltpu.roll(x, 128 - BLOCK, 1)
+        ahead = lambda x: pltpu.roll(x, BLOCK, 1)
+        at = slice(i * 64, (i + 2) * 64)
+        f_mid[:, at] = jnp.where(lane < 64, back(even), ahead(odd)).astype(bf16)
+        f_edge[:, at] = jnp.where(lane < 64, ahead(even), back(odd)).astype(bf16)
+
+
+def rim_kernel(main, up, down, tail, head):
+    half, lat_dev, side = up.shape[0], main.shape[0], tail.shape[1]
+    last = main.shape[1] - side
+    tail[:half] = up[:, last:, :]
+    tail[half : half + lat_dev] = main[:, last:, :]
+    tail[half + lat_dev :] = down[:, last:, :]
+    head[:half] = up[:, :side, :]
+    head[half : half + lat_dev] = main[:, :side, :]
+    head[half + lat_dev :] = down[:, :side, :]
 
 
 def convolve(band, ext, place, q_ref):
@@ -74,23 +90,21 @@
         total[k] = jnp.dot(f_ref[...], cells, preferred_element_type=f32)
 
 
-def edge_kernel(core_ref, band, main, up, down, left, right, f_ref, total, q_ref, keep, send, ext):
+def edge_kernel(band, main, up, down, left, right, f_ref, total, q_ref, low, high, ext):
     lat_dev, lon_dev, channels = main.shape
     half, side = up.shape[0], left.shape[1]
     inner = 2 * BLOCK - side
     for first, last, source in ((0, half, up), (half, half + lat_dev, main), (half + lat_dev, 2 * half + lat_dev, down)):
-        ext[first:last, 0, side:, :] = source[:, :inner, :]
-        ext[first:last, 1, :inner, :] = source[:, lon_dev - inner :, :]
-    ext[:, 0, :side, :] = left[...]
-    ext[:, 1, inner:, :] = right[...]
+        ext[first:last, 0, :inner, :] = source[:, lon_dev - inner :, :]
+        ext[first:last, 1, side:, :] = source[:, :inner, :]
+    ext[:, 0, inner:, :] = right[...]
+    ext[:, 1, :side, :] = left[...]
     convolve(band, ext, lambda j: (j,), q_ref)
-    low_core = core_ref[0] == 0
     for k in range(q_ref.shape[0]):
         cells = q_ref[k].reshape(f_ref.shape[1], channels)
         out = total[k] + jnp.dot(f_ref[...], cells, preferred_element_type=f32)
-        low, high = out[:, : channels // 2], out[:, channels // 2 :]
-        keep[k] = jnp.where(low_core, low, high)
-        send[k] = jnp.where(low_core, high, low)
+        low[k] = out[:, : channels // 2]
+        high[k] = out[:, channels // 2 :]
 
 
 def call(kernel, out_shape, operands, scratch=(), scalars=0, flops=10**9):
@@ -114,7 +128,7 @@
         for k in range(basis_count):
             parts = []
             for row in (i, i + 1):
-                parts += [edge_ref[k, row, :BLOCK], mid_ref[k, row], edge_ref[k, row, BLOCK:]]
+                parts += [edge_ref[k, row, BLOCK:], mid_ref[k, row], edge_ref[k, row, :BLOCK]]
             total += lax.dot_general(
                 w_ref[k], jnp.concatenate(parts, axis=0), (((1,), (1,)), ((), ())), preferred_element_type=f32
             )
@@ -129,13 +143,14 @@
     return jnp.broadcast_to(x[None], (count,) + x.shape)
 
 
-def reduce_all(keep, send, core, scale, beside):
+def reduce_all(low, high, core, scale, beside):
     swap = [(0, 1), (1, 0)]
-    basis_count, channels, half = keep.shape
+    basis_count, channels, half = low.shape
     plane = 1
     for axis in PLANE:
         plane *= lax.axis_size(axis)
     depth = lax.axis_size("z")
+    keep, send = jnp.where(core == 0, low, high), jnp.where(core == 0, high, low)
     came, beside = lax.optimization_barrier((lax.ppermute(send, "core", swap), beside))
     own = keep + came
     own = own.reshape(plane, -1, half).astype(bf16)
@@ -150,43 +165,48 @@
 
 def local(fields, grad_out, weight, basis_table, lon_reach):
     channels, lat_dev, lon_dev = fields.shape
-    nlat_all = basis_table.shape[1]
-    half, side = basis_table.shape[2] // 2, basis_table.shape[3] // 2
+    basis_count, nlat_all, row_span, tap_count = basis_table.shape
+    half, side = row_span // 2, tap_count // 2
+    near, wide = lat_dev + 2 * half, 2 * BLOCK
+    shape = jax.ShapeDtypeStruct
     core = lax.axis_index("core")
-    taps = tap_rows(basis_table, lon_reach, lax.axis_index(LAT) * lat_dev, lat_dev)
     main = jnp.transpose(grad_out, (1, 2, 0))
     up = shift(main[lat_dev - half :], LAT, 1, False)
     down = shift(main[:half], LAT, -1, False)
-    tall = lambda at: jnp.concatenate([up[:, at], main[:, at], down[:, at]], axis=0)
-    left = shift(tall(slice(lon_dev - side, lon_dev)), LON, 1, True)
-    right = shift(tall(slice(0, side)), LON, -1, True)
-    basis_count = basis_table.shape[0]
-    near = lat_dev + 2 * half
-    wide = 2 * BLOCK
-    f_mid = fields[:, :, BLOCK : lon_dev - BLOCK].reshape(channels, lat_dev * wide)
-    f_edge = jnp.concatenate([fields[:, :, :BLOCK], fields[:, :, lon_dev - BLOCK :]], axis=2)
-    f_edge = f_edge.reshape(channels, lat_dev * wide)
-    shape = jax.ShapeDtypeStruct
+    rim = shape((near, side, channels), bf16)
+    tail, head = call(rim_kernel, (rim, rim), (main, up, down), flops=10**6)
+    left = shift(tail, LON, 1, True)
+    right = shift(head, LON, -1, True)
+    above = lax.axis_index(LAT) * lat_dev - half
+    start = jnp.clip(above, 0, nlat_all - near)
+    taps = tap_rows(basis_table, lon_reach, start, near)
+    band, f_mid, f_edge = call(
+        prepare_kernel,
+        (
+            shape((lat_dev, basis_count * BLOCK, taps.shape[2] * 128), bf16),
+            shape((channels, lat_dev * wide), bf16),
+            shape((channels, lat_dev * wide), bf16),
+        ),
+        ((above - start)[None], taps, fields.reshape(channels, lat_dev * lon_dev)),
+        scalars=1,
+    )
     q_shape = shape((basis_count, lat_dev, wide, channels), bf16)
     part = shape((basis_count, channels, channels // 2), f32)
-    band_shape = shape((lat_dev, basis_count * BLOCK, taps.shape[2] * 128), bf16)
-    band = call(band_kernel, band_shape, (taps,))
     q_mid, total = call(
         middle_kernel,
         (q_shape, shape((basis_count, channels, channels), f32)),
         (band, main, up, down, f_mid),
         [pltpu.VMEM((near, lon_dev, channels), bf16)],
     )
-    q_edge, keep, send = call(
+    q_edge, low, high = call(
         edge_kernel,
         (q_shape, part, part),
-        (core[None].astype(jnp.int32), band, main, up, down, left, right, f_edge, total),
+        (band, main, up, down, left, right, f_edge, total),
         [pltpu.VMEM((near, 2, wide, channels), bf16)],
-        scalars=1,
     )
     mixed = call(mix_kernel, shape((channels, lat_dev * lon_dev), bf16), (weight, q_mid, q_edge))
     field_grad = mixed.reshape(channels, lat_dev, lon_dev)
-    weight_grad, field_grad = reduce_all(keep, send, core, 1.0 / nlat_all, field_grad)
+    weight_grad, field_grad = reduce_all(low, high, core, 1.0 / nlat_all, field_grad)
     return field_grad, weight_grad
 
 

time: 96.2 us -> 94.2 us (0.979)
  local copies, waits for them, and re-layouts: 16.3 us -> 14.2 us
  blocking collectives: 45.3 us -> 46.4 us
  waiting for transfers between devices: 2.7 us -> 1.64 us
    concatenate x3 -> x0, other arithmetic: 2.08 us -> none  [the longest x2 1.36 us: local(): jnp.concatenate([up[:, at], main[:, at], down[:, at]], axis=0)]
    slice x14 -> x0, local copies, waits for them, and re-layouts: 2.04 us -> none  [the longest x1 1 us: local(): fields[:, :, BLOCK:lon_dev - BLOCK].reshape(channels, lat_dev * wide)]
    rev x0 -> x1, local copies, waits for them, and re-layouts: none -> 1.92 us  [tap_rows(): table = jnp.flip(table, (2, 3)).astype(f32)]
    unnamed x36 -> x19, local copies, waits for them, and re-layouts: 9.3 us -> 7.85 us
    reshape x1, other arithmetic: 0.02 us -> 1.29 us  [tap_rows(): table.reshape(near, basis_count, (row_span + 1) * BLOCK * 2 // 128, 128)]
    all_to_all x3, blocking collectives: 45.3 us -> 46.4 us  [all_to_all(): return lax.all_to_all(x, axes, 0, 0, tiled=True)]
    reshape x4 -> x2, local copies, waits for them, and re-layouts: 4.44 us -> 3.52 us  [tap_rows(): table.reshape(near, basis_count, (row_span + 1) * BLOCK * 2 // 128, 128)]
    pallas_call x4 -> x5, Pallas kernels: 7.39 us -> 8.28 us  [call(): pl.pallas_call(kernel, out_shape=out_shape, in_specs=[smem] * scalars + [...]
  transfers between devices with their start and end apart: 6 -> 6, of which waited for: 3 -> 1; matrix products, arithmetic and copies ran while one was open for 13% -> 10% of each run, Pallas kernels for 4% -> 5%
where the time goes in v3:
time: 94.2 us; the launch traced here: 93.7 us
  blocking collectives  46.4 us (49%)
  starting transfers between devices  18.6 us (20%)
  local copies, waits for them, and re-layouts  14.2 us (15%)
  Pallas kernels  8.28 us (9%)
  other arithmetic  3.71 us (4%)
  waiting for transfers between devices  1.64 us (2%)
    all_to_all x3, blocking collectives, all_to_all(): return lax.all_to_all(x, axes, 0, 0, tiled=True)  46.4 us
    ppermute x4, starting transfers between devices, shift(): return lax.ppermute(x, axes, pairs)  14.4 us
    pallas_call x5, Pallas kernels, call(): pl.pallas_call(kernel, out_shape=out_shape, in_specs=[smem] * scalars + [...  8.28 us
    unnamed x19, local copies, waits for them, and re-layouts  7.85 us
    ppermute x1, starting transfers between devices, reduce_all(): other = lax.ppermute(own, 'core', swap)  4.14 us
    reshape x2, local copies, waits for them, and re-layouts, tap_rows(): table.reshape(near, basis_count, (row_span + 1) * BLOCK * 2 // 128, 128)  3.52 us
    rev x1, local copies, waits for them, and re-layouts, tap_rows(): table = jnp.flip(table, (2, 3)).astype(f32)  1.92 us
  transfers between devices with their start and end apart: 6, of which 1 were waited for; matrix products, arithmetic and copies ran while one was open for 10% of the time, Pallas kernels for 5%

profile of v3, /device:TPU:1, one launch (start us, length us, event | category | flops | bytes accessed | tf_op | source)
XLA Modules:
  0.0 93.7 jit_solution(13068570166183294233)
XLA Ops:
  0.6 0.0 copy-start.7
  0.6 0.0 copy-start.5
  0.7 1.4 %copy.10 = bf16[256,8,128]{0,2,1:T(8,128)(2,1)S(1)} copy(bf16[256,8,128]{2,1,0:T(8,128)(2,1)} %param.6) | data formatting | bytes 1048576 | tf_op args[1]
  2.0 0.0 copy-start.6
  2.0 0.7 fusion
  2.8 5.1 %collective-permute-start.1 = (bf16[3,128,256]{2,1,0:T(8,128)(2,1)}, bf16[3,128,256]{2,1,0:T(8,128)(2,1)S(1)}, u32[]{:S(2)}, u32[]{:S(2)}) collective-permute-start(bf16[3,128,256]{2,1,0:T(8,128)(2,1)} %get-tuple-element.28), channel_id=1, source_target_pairs={{16,0},{32,16},{48,32},{64,48},{80,64},{96,80},{112,96},{128,112},... | collective-permute-start | bytes 589832 | tf_op jit(solution)/shard_map/ppermute | solution.py:20
  7.9 1.9 %collective-permute-start = (bf16[3,128,256]{2,1,0:T(8,128)(2,1)S(1)}, bf16[3,128,256]{2,1,0:T(8,128)(2,1)S(1)}, u32[]{:S(2)}, u32[]{:S(2)}) collective-permute-start(bf16[3,128,256]{2,1,0:T(8,128)(2,1)S(1)} %get-tuple-element.29), channel_id=1, source_target_pairs={{0,16},{16,32},{32,48},{48,64},{64,80},{80,96},{96,112},{112,128},... | collective-permute-start | bytes 589832 | tf_op jit(solution)/shard_map/ppermute | solution.py:20
  9.9 0.0 copy-done.7
  9.9 0.1 dynamic_slice.6
  10.0 0.1 broadcast_compare_fusion
  10.0 0.0 copy-done.5
  10.0 0.3 dynamic-slice_select_fusion
  10.3 0.0 copy-done.6
  10.3 0.9 copy.14
  11.2 1.9 %rev.4 = bf16[9,14,7,33]{1,2,3,0:T(8,128)(2,1)} reverse(bf16[9,14,7,33]{1,2,3,0:T(8,128)(2,1)S(1)} %dynamic-slice_select_fusion), dimensions={2,3} | reverse | bytes 116424 | tf_op jit(solution)/shard_map/jit(_flip)/rev | solution.py:29
  13.1 1.3 %convert_bitcast_fusion = f32[14,9,8,64]{0,2,3,1:T(8,128)S(1)} fusion(bf16[9,14,7,33]{1,2,3,0:T(8,128)(2,1)} %rev.4), kind=kLoop, calls=%fused_computation | loop fusion | flops 64512 | bytes 316260 | tf_op jit(solution)/shard_map/reshape | solution.py:32
  14.4 1.6 %copy.9 = f32[14,9,8,64]{3,2,1,0:T(8,128)} copy(f32[14,9,8,64]{0,2,3,1:T(8,128)S(1)} %convert_bitcast_fusion) | data formatting | bytes 516096 | tf_op jit(solution)/shard_map/reshape | solution.py:32
  16.0 1.9 %reshape.62.taps = f32[14,9,4,128]{3,2,1,0:T(4,128)} reshape(f32[14,9,8,64]{3,2,1,0:T(8,128)} %copy.9) | data formatting | bytes 516096 | tf_op jit(solution)/shard_map/reshape | solution.py:32
  17.9 0.0 collective-permute-done.1.down
  17.9 0.0 collective-permute-done.up
  17.9 0.7 shard_map.69
  18.6 2.1 %collective-permute-start.2 = (bf16[14,16,256]{2,1,0:T(8,128)(2,1)}, bf16[14,16,256]{2,1,0:T(8,128)(2,1)}, u32[]{:S(2)}, u32[]{:S(2)}) collective-permute-start(bf16[14,16,256]{2,1,0:T(8,128)(2,1)} %get-tuple-element.15), channel_id=1, source_target_pairs={{0,1},{1,2},{2,3},{3,4},{4,5},{5,6},{6,7},{7,8},{8,9},{9,10},{10,1... | collective-permute-start | bytes 344072 | tf_op jit(solution)/shard_map/ppermute | solution.py:20
  20.7 5.3 %collective-permute-start.3 = (bf16[14,16,256]{2,1,0:T(8,128)(2,1)}, bf16[14,16,256]{2,1,0:T(8,128)(2,1)}, u32[]{:S(2)}, u32[]{:S(2)}) collective-permute-start(bf16[14,16,256]{2,1,0:T(8,128)(2,1)} %get-tuple-element.16), channel_id=1, source_target_pairs={{0,15},{1,0},{2,1},{3,2},{4,3},{5,4},{6,5},{7,6},{8,7},{9,8},{10,9... | collective-permute-start | bytes 344072 | tf_op jit(solution)/shard_map/ppermute | solution.py:20
  26.0 0.0 copy-start.1
  26.0 1.0 %copy-done.1 = bf16[32,8,8,128]{3,1,2,0:T(8,128)(2,1)S(1)} copy-done((bf16[32,8,8,128]{3,1,2,0:T(8,128)(2,1)S(1)}, bf16[32,8,8,128]{3,1,2,0:T(8,128)(2,1)}, u32[]{:S(2)}) %copy-start.1) | copy-done | bytes 524312
  27.1 0.0 copy-start.2
  27.1 0.9 %copy-done.2 = f32[14,9,4,128]{3,2,1,0:T(4,128)S(1)} copy-done((f32[14,9,4,128]{3,2,1,0:T(4,128)S(1)}, f32[14,9,4,128]{3,2,1,0:T(4,128)}, u32[]{:S(2)}) %copy-start.2) | copy-done | bytes 258072
  28.0 1.0 %shard_map.68 = (bf16[8,288,512]{2,1,0:T(8,128)(2,1)S(1)}, bf16[256,512]{1,0:T(8,128)(2,1)S(1)}, bf16[256,512]{1,0:T(8,128)(2,1)S(1)}) custom-call(s32[1]{0:T(128)} %bitcast.off_ref, f32[14,9,4,128]{3,2,1,0:T(4,128)S(1)} %copy-done.2, bf16[256,1024]{1,0:T(8,128)(2,1)S(1)} %bitcast.19), custom_call_target="tpu_custom_call" | custom-call | flops 1000000000 | bytes 1000000 | tf_op jit(solution)/shard_map/pallas_call | solution.py:113
  29.0 0.0 copy-start.3
  29.0 0.7 copy-done.3
  29.7 0.0 copy-start.4
  29.7 0.9 %copy-done.4 = bf16[256,512]{1,0:T(8,128)(2,1)S(1)} copy-done((bf16[256,512]{1,0:T(8,128)(2,1)S(1)}, bf16[256,512]{1,0:T(8,128)(2,1)}, u32[]{:S(2)}) %copy-start.4) | copy-done | bytes 262168
  30.6 2.1 %shard_map.70 = (bf16[9,8,64,256]{3,2,1,0:T(8,128)(2,1)S(1)}, f32[9,256,256]{2,1,0:T(8,128)S(1)}) custom-call(bf16[8,288,512]{2,1,0:T(8,128)(2,1)S(1)} %get-tuple-element.14.band, bf16[8,128,256]{2,1,0:T(8,128)(2,1)S(1)} %bitcast.16, bf16[3,128,256]{2,1,0:T(8,128)(2,1)S(1)} %collective-permute-done.up, bf16[3,128,256]{2,1,0:T(8,128)(2,1)S(1)} %collective-permute-done.1.down, ...), custom_call_target="tpu_custom_call" | custom-call | flops 1000000000 | bytes 1000000 | tf_op jit(solution)/shard_map/pallas_call | solution.py:113
  32.7 0.0 collective-permute-done.2.left
  32.8 0.0 collective-permute-done.3.right
  32.8 3.1 %shard_map.71 = (bf16[9,8,64,256]{3,2,1,0:T(8,128)(2,1)S(1)}, f32[9,256,128]{2,1,0:T(8,128)S(1)}, f32[9,256,128]{2,1,0:T(8,128)S(1)}) custom-call(bf16[8,288,512]{2,1,0:T(8,128)(2,1)S(1)} %get-tuple-element.14.band, bf16[8,128,256]{2,1,0:T(8,128)(2,1)S(1)} %bitcast.17, bf16[3,128,256]{2,1,0:T(8,128)(2,1)S(1)} %collective-permute-done.up, ...), custom_call_target="tpu_custom_call" | custom-call | flops 1000000000 | bytes 1000000 | tf_op jit(solution)/shard_map/pallas_call | solution.py:113
  35.9 0.0 copy-start
  35.9 0.1 broadcast_select_fusion.2
  36.0 0.1 collective-permute-start.4
  36.1 1.0 %copy-done = bf16[9,256,256]{2,1,0:T(8,128)(2,1)S(1)} copy-done((bf16[9,256,256]{2,1,0:T(8,128)(2,1)S(1)}, bf16[9,256,256]{2,1,0:T(8,128)(2,1)}, u32[]{:S(2)}) %copy-start) | copy-done | bytes 1179672
  37.1 1.4 %shard_map.72 = bf16[256,1024]{1,0:T(8,128)(2,1)S(1)} custom-call(bf16[9,256,256]{2,1,0:T(8,128)(2,1)S(1)} %copy-done, bf16[9,8,64,256]{3,2,1,0:T(8,128)(2,1)S(1)} %get-tuple-element.22.mid_ref, bf16[9,8,64,256]{3,2,1,0:T(8,128)(2,1)S(1)} %get-tuple-element.23.edge_ref), custom_call_target="tpu_custom_call" | custom-call | flops 1000000000 | bytes 1000000 | tf_op jit(solution)/shard_map/pallas_call | solution.py:113
  38.6 0.9 copy.12
  39.5 0.0 collective-permute-done.4
  39.5 0.2 add_convert_fusion
  39.6 17.6 %all_to_all.15 = bf16[16,144,128]{2,1,0:T(8,128)(2,1)S(1)} all-to-all(bf16[16,144,128]{2,1,0:T(8,128)(2,1)S(1)} %bitcast.20), channel_id=1, replica_groups=mesh['y'=4,'x_lo'=2,'core'=2,'z'=8,'x_hi'=2] {'y','x_hi','x_lo'}, dimensions={0} | all-to-all | bytes 1179648 | tf_op jit(solution)/shard_map/all_to_all | solution.py:139
  57.2 0.1 reduce_sum.21
  57.3 16.8 %all_to_all.16 = bf16[8,144,128]{2,1,0:T(8,128)(2,1)S(1)} all-to-all(bf16[8,144,128]{2,1,0:T(8,128)(2,1)S(1)} %broadcast_in_dim.32), channel_id=1, replica_groups=mesh['y'=4,'x_lo'=2,'core'=2,'z'=8,'x_hi'=2] {'z'}, dimensions={0} | all-to-all | bytes 589824 | tf_op jit(solution)/shard_map/all_to_all | solution.py:139
  74.2 0.1 broadcast_in_dim.33
  74.3 12.0 %all_to_all.17 = bf16[16,144,128]{2,1,0:T(8,128)(2,1)S(1)} all-to-all(bf16[16,144,128]{2,1,0:T(8,128)(2,1)S(1)} %broadcast_in_dim.33), channel_id=1, replica_groups=mesh['y'=4,'x_lo'=2,'core'=2,'z'=8,'x_hi'=2] {'y','x_hi','x_lo'}, dimensions={0} | all-to-all | bytes 1179648 | tf_op jit(solution)/shard_map/all_to_all | solution.py:139
  86.3 4.1 %collective-permute-start.5 = (bf16[9,256,128]{2,1,0:T(8,128)(2,1)S(1)}, bf16[9,256,128]{2,1,0:T(8,128)(2,1)S(1)}, u32[]{:S(2)}, u32[]{:S(2)}) collective-permute-start(bf16[9,256,128]{2,1,0:T(8,128)(2,1)S(1)} %bitcast.21), channel_id=1, source_target_pairs={{0,16},{16,0},{1,17},{17,1},{2,18},{18,2},{3,19},{19,3},{4,20},{20... | collective-permute-start | bytes 1769480 | tf_op jit(solution)/shard_map/ppermute | solution.py:161
  90.4 1.6 %collective-permute-done.5 = bf16[9,256,128]{2,1,0:T(8,128)(2,1)S(1)} collective-permute-done((bf16[9,256,128]{2,1,0:T(8,128)(2,1)S(1)}, bf16[9,256,128]{2,1,0:T(8,128)(2,1)S(1)}, u32[]{:S(2)}, u32[]{:S(2)}) %collective-permute-start.5) | collective-permute-done | bytes 589856 | tf_op jit(solution)/shard_map/ppermute | solution.py:161
  92.0 0.1 broadcast_select_fusion.1
  92.1 1.6 %maximum_convert_fusion = f32[9,256,256]{2,1,0:T(8,128)} fusion(bf16[9,256,128]{2,1,0:T(8,128)(2,1)S(1)} %get-tuple-element.27, bf16[9,256,128]{2,1,0:T(8,128)(2,1)S(1)} %get-tuple-element.26), kind=kLoop, calls=%fused_computation.1 | loop fusion | flops 2359296 | bytes 3538944 | tf_op jit(solution)/shard_map/convert_element_type | solution.py:163
  (4 shorter events, 0.1 us)
Async XLA Ops:
  0.6 9.2 %copy-start.7 = (s32[128]{0:T(128)S(1)}, s32[128]{0:T(128)}, u32[]{:S(2)}) copy-start(s32[128]{0:T(128)} %param.9) | copy-start | bytes 1540
  0.6 9.4 %copy-start.5 = (bf16[9,128,7,33]{1,2,3,0:T(8,128)(2,1)S(1)}, bf16[9,128,7,33]{1,2,3,0:T(8,128)(2,1)}, u32[]{:S(2)}) copy-start(bf16[9,128,7,33]{1,2,3,0:T(8,128)(2,1)} %param.8) | copy-start | bytes 1596676
  2.0 8.3 %copy-start.6 = (bf16[256,8,128]{2,1,0:T(8,128)(2,1)S(1)}, bf16[256,8,128]{2,1,0:T(8,128)(2,1)}, u32[]{:S(2)}) copy-start(bf16[256,8,128]{2,1,0:T(8,128)(2,1)} %param.5) | copy-start | bytes 1572868
  2.8 15.2 %collective-permute-start.1 = (bf16[3,128,256]{2,1,0:T(8,128)(2,1)}, bf16[3,128,256]{2,1,0:T(8,128)(2,1)S(1)}, u32[]{:S(2)}, u32[]{:S(2)}) collective-permute-start(bf16[3,128,256]{2,1,0:T(8,128)(2,1)} %get-tuple-element.28), channel_id=1, source_target_pairs={{16,0},{32,16},{48,32},{64,48},{80,64},{96,80},{112,96},{128,112},... | collective-permute-start | bytes 589832 | tf_op jit(solution)/shard_map/ppermute | solution.py:20
  7.9 10.0 %collective-permute-start = (bf16[3,128,256]{2,1,0:T(8,128)(2,1)S(1)}, bf16[3,128,256]{2,1,0:T(8,128)(2,1)S(1)}, u32[]{:S(2)}, u32[]{:S(2)}) collective-permute-start(bf16[3,128,256]{2,1,0:T(8,128)(2,1)S(1)} %get-tuple-element.29), channel_id=1, source_target_pairs={{0,16},{16,32},{32,48},{48,64},{64,80},{80,96},{96,112},{112,128},... | collective-permute-start | bytes 589832 | tf_op jit(solution)/shard_map/ppermute | solution.py:20
  18.6 14.1 %collective-permute-start.2 = (bf16[14,16,256]{2,1,0:T(8,128)(2,1)}, bf16[14,16,256]{2,1,0:T(8,128)(2,1)}, u32[]{:S(2)}, u32[]{:S(2)}) collective-permute-start(bf16[14,16,256]{2,1,0:T(8,128)(2,1)} %get-tuple-element.15), channel_id=1, source_target_pairs={{0,1},{1,2},{2,3},{3,4},{4,5},{5,6},{6,7},{7,8},{8,9},{9,10},{10,1... | collective-permute-start | bytes 344072 | tf_op jit(solution)/shard_map/ppermute | solution.py:20
  20.7 12.0 %collective-permute-start.3 = (bf16[14,16,256]{2,1,0:T(8,128)(2,1)}, bf16[14,16,256]{2,1,0:T(8,128)(2,1)}, u32[]{:S(2)}, u32[]{:S(2)}) collective-permute-start(bf16[14,16,256]{2,1,0:T(8,128)(2,1)} %get-tuple-element.16), channel_id=1, source_target_pairs={{0,15},{1,0},{2,1},{3,2},{4,3},{5,4},{6,5},{7,6},{8,7},{9,8},{10,9... | collective-permute-start | bytes 344072 | tf_op jit(solution)/shard_map/ppermute | solution.py:20
  26.0 1.0 %copy-start.1 = (bf16[32,8,8,128]{3,1,2,0:T(8,128)(2,1)S(1)}, bf16[32,8,8,128]{3,1,2,0:T(8,128)(2,1)}, u32[]{:S(2)}) copy-start(bf16[32,8,8,128]{3,1,2,0:T(8,128)(2,1)} %copy.14) | copy-start | bytes 1572868
  27.1 0.9 %copy-start.2 = (f32[14,9,4,128]{3,2,1,0:T(4,128)S(1)}, f32[14,9,4,128]{3,2,1,0:T(4,128)}, u32[]{:S(2)}) copy-start(f32[14,9,4,128]{3,2,1,0:T(4,128)} %reshape.62.taps) | copy-start | bytes 774148
  29.0 0.7 copy-start.3
  29.7 0.9 %copy-start.4 = (bf16[256,512]{1,0:T(8,128)(2,1)S(1)}, bf16[256,512]{1,0:T(8,128)(2,1)}, u32[]{:S(2)}) copy-start(bf16[256,512]{1,0:T(8,128)(2,1)} %copy-done.3) | copy-start | bytes 786436
  35.9 1.3 %copy-start = (bf16[9,256,256]{2,1,0:T(8,128)(2,1)S(1)}, bf16[9,256,256]{2,1,0:T(8,128)(2,1)}, u32[]{:S(2)}) copy-start(bf16[9,256,256]{2,1,0:T(8,128)(2,1)} %w_ref.1) | copy-start | bytes 3538948
  36.0 3.4 %collective-permute-start.4 = (f32[9,256,128]{2,1,0:T(8,128)S(1)}, f32[9,256,128]{2,1,0:T(8,128)S(1)}, u32[]{:S(2)}, u32[]{:S(2)}) collective-permute-start(f32[9,256,128]{2,1,0:T(8,128)S(1)} %broadcast_select_fusion.2), channel_id=1, source_target_pairs={{0,16},{16,0},{1,17},{17,1},{2,18},{18,2},{3,19},{19,3},{4,20},{20... | collective-permute-start | bytes 3538952 | tf_op jit(solution)/shard_map/ppermute | solution.py:154
  86.3 5.8 %collective-permute-start.5 = (bf16[9,256,128]{2,1,0:T(8,128)(2,1)S(1)}, bf16[9,256,128]{2,1,0:T(8,128)(2,1)S(1)}, u32[]{:S(2)}, u32[]{:S(2)}) collective-permute-start(bf16[9,256,128]{2,1,0:T(8,128)(2,1)S(1)} %bitcast.21), channel_id=1, source_target_pairs={{0,16},{16,0},{1,17},{17,1},{2,18},{18,2},{3,19},{19,3},{4,20},{20... | collective-permute-start | bytes 1769480 | tf_op jit(solution)/shard_map/ppermute | solution.py:161

commit v4 on v3

--- a/solution.py
+++ b/solution.py
@@ -21,38 +21,45 @@
 
 
 def tap_rows(basis_table, lon_reach, start, near):
-    basis_count, _, row_span, tap_count = basis_table.shape
+    tap_count = basis_table.shape[3]
     table = lax.dynamic_slice_in_dim(basis_table, start, near, 1)
     reach = lax.dynamic_slice_in_dim(lon_reach, start, near, 0)
     offset = jnp.abs(lax.iota(jnp.int32, tap_count) - tap_count // 2)
     table = jnp.where((offset[None, :] <= reach[:, None])[None, :, None, :], table, jnp.zeros_like(table))
-    table = jnp.flip(table, (2, 3)).astype(f32)
-    table = jnp.pad(table, ((0, 0), (0, 0), (0, 1), (0, 2 * BLOCK - tap_count)))
-    table = jnp.transpose(table, (1, 0, 2, 3))
-    return table.reshape(near, basis_count, (row_span + 1) * BLOCK * 2 // 128, 128)
-
-
-def prepare_kernel(off_ref, taps, f_ref, band, f_mid, f_edge):
-    near, basis_count, groups, _ = taps.shape
+    return jnp.transpose(table, (0, 2, 1, 3))
+
+
+def prepare_kernel(off_ref, taps, f_ref, band, f_mid, f_edge, lines):
+    basis_count, row_span, near, tap_count = taps.shape
     lat_dev = band.shape[0]
-    lane = lax.broadcasted_iota(jnp.int32, (1, 128), 1)
-    rows = [jnp.clip(off_ref[0] + r, 0, near - 1) for r in range(near + 1)]
-    for i in range(lat_dev):
+    half = row_span // 2
+    wide = 2 * BLOCK
+    tap = lax.broadcasted_iota(jnp.int32, (tap_count, 128), 0)
+    lane = lax.broadcasted_iota(jnp.int32, (tap_count, 128), 1)
+    lines[...] = jnp.zeros_like(lines)
+    for s in range(row_span):
+        turn = (lane == s % 2 * wide + tap_count - 1 - tap).astype(bf16)
         for k in range(basis_count):
-            for p in range(groups):
-                first = taps[rows[i + 2 * p], k, p : p + 1, :]
-                second = taps[rows[i + 2 * p + 1], k, p : p + 1, :]
-                line = jnp.broadcast_to(jnp.where(lane < 2 * BLOCK, first, second), (BLOCK, 128))
+            lines[k, s, 8 : 8 + near, :] = jnp.dot(taps[k, s], turn, preferred_element_type=f32)
+    off = off_ref[0] + 8 + 2 * half
+    for k in range(basis_count):
+        for p in range((row_span + 1) // 2):
+            pair = lines[k, 2 * p, pl.ds(off - 2 * p, lat_dev), :]
+            if 2 * p + 1 < row_span:
+                pair = pair + lines[k, 2 * p + 1, pl.ds(off - 2 * p - 1, lat_dev), :]
+            for i in range(lat_dev):
+                line = jnp.broadcast_to(pair[i : i + 1, :], (BLOCK, 128))
                 line = pltpu.roll(line, 0, 1, stride=1, stride_axis=0)
                 band[i, k * BLOCK : (k + 1) * BLOCK, p * 128 : (p + 1) * 128] = line.astype(bf16)
+    lane = lax.broadcasted_iota(jnp.int32, (1, 128), 1)
     for i in range(0, lat_dev, 2):
         even = f_ref[:, i * 128 : (i + 1) * 128].astype(f32)
         odd = f_ref[:, (i + 1) * 128 : (i + 2) * 128].astype(f32)
         back = lambda x: pltpu.roll(x, 128 - BLOCK, 1)
         ahead = lambda x: pltpu.roll(x, BLOCK, 1)
-        at = slice(i * 64, (i + 2) * 64)
-        f_mid[:, at] = jnp.where(lane < 64, back(even), ahead(odd)).astype(bf16)
-        f_edge[:, at] = jnp.where(lane < 64, ahead(even), back(odd)).astype(bf16)
+        at = slice(i * wide, (i + 2) * wide)
+        f_mid[:, at] = jnp.where(lane < wide, back(even), ahead(odd)).astype(bf16)
+        f_edge[:, at] = jnp.where(lane < wide, ahead(even), back(odd)).astype(bf16)
 
 
 def rim_kernel(main, up, down, tail, head):
@@ -71,7 +78,7 @@
     row_span = ext.shape[0] - lat_dev + 1
     for i in range(lat_dev):
         for j in range(columns // BLOCK):
-            parts = [ext[(i + s,) + place(j)] for s in range(row_span)]
+            parts = [ext[(i + row_span - 1 - s,) + place(j)] for s in range(row_span)]
             window = jnp.concatenate(parts + [jnp.zeros_like(parts[0])], axis=0)
             out = jnp.dot(band[i], window, preferred_element_type=f32).astype(bf16)
             for k in range(basis_count):
@@ -107,7 +114,7 @@
         high[k] = out[:, channels // 2 :]
 
 
-def call(kernel, out_shape, operands, scratch=(), scalars=0, flops=10**9):
+def call(kernel, out_shape, operands, scratch=(), scalars=0, flops=10**9, mib=16):
     vmem = pl.BlockSpec(memory_space=pltpu.VMEM)
     smem = pl.BlockSpec(memory_space=pltpu.SMEM)
     return pl.pallas_call(
@@ -116,7 +123,7 @@
         in_specs=[smem] * scalars + [vmem] * (len(operands) - scalars),
         out_specs=jax.tree.map(lambda _: vmem, out_shape),
         scratch_shapes=list(scratch),
-        compiler_params=pltpu.CompilerParams(vmem_limit_bytes=40 * 1024 * 1024),
+        compiler_params=pltpu.CompilerParams(vmem_limit_bytes=mib * 1024 * 1024),
         cost_estimate=pl.CostEstimate(flops=flops, bytes_accessed=10**6, transcendentals=0),
     )(*operands)
 
@@ -174,21 +181,24 @@
     up = shift(main[lat_dev - half :], LAT, 1, False)
     down = shift(main[:half], LAT, -1, False)
     rim = shape((near, side, channels), bf16)
-    tail, head = call(rim_kernel, (rim, rim), (main, up, down), flops=10**6)
+    tail, head = call(rim_kernel, (rim, rim), (main, up, down), flops=10**6, mib=4)
     left = shift(tail, LON, 1, True)
     right = shift(head, LON, -1, True)
     above = lax.axis_index(LAT) * lat_dev - half
-    start = jnp.clip(above, 0, nlat_all - near)
-    taps = tap_rows(basis_table, lon_reach, start, near)
+    held = min(16, nlat_all)
+    start = jnp.clip(above, 0, nlat_all - held)
+    taps = tap_rows(basis_table, lon_reach, start, held)
     band, f_mid, f_edge = call(
         prepare_kernel,
         (
-            shape((lat_dev, basis_count * BLOCK, taps.shape[2] * 128), bf16),
+            shape((lat_dev, basis_count * BLOCK, (row_span + 1) * wide), bf16),
             shape((channels, lat_dev * wide), bf16),
             shape((channels, lat_dev * wide), bf16),
         ),
         ((above - start)[None], taps, fields.reshape(channels, lat_dev * lon_dev)),
+        [pltpu.VMEM((basis_count, row_span, held + 16, 128), f32)],
         scalars=1,
+        mib=12,
     )
     q_shape = shape((basis_count, lat_dev, wide, channels), bf16)
     part = shape((basis_count, channels, channels // 2), f32)

time: 94.2 us -> 88.9 us (0.944)
  local copies, waits for them, and re-layouts: 14.2 us -> 9.41 us
  other arithmetic: 3.71 us -> 2.25 us
  blocking collectives: 46.4 us -> 45.3 us
  starting transfers between devices: 18.6 us -> 19.7 us
    reshape x2 -> x0, local copies, waits for them, and re-layouts: 3.52 us -> none  [tap_rows(): table.reshape(near, basis_count, (row_span + 1) * BLOCK * 2 // 128, 128)]
    rev x1 -> x0, local copies, waits for them, and re-layouts: 1.92 us -> none  [tap_rows(): table = jnp.flip(table, (2, 3)).astype(f32)]
    reshape x1 -> x0, other arithmetic: 1.29 us -> none  [tap_rows(): table.reshape(near, basis_count, (row_span + 1) * BLOCK * 2 // 128, 128)]
    all_to_all x3, blocking collectives: 46.4 us -> 45.3 us  [all_to_all(): return lax.all_to_all(x, axes, 0, 0, tiled=True)]
    unnamed x19 -> x30, local copies, waits for them, and re-layouts: 7.85 us -> 8.96 us
    ppermute x1, starting transfers between devices: 4.14 us -> 5.16 us  [reduce_all(): other = lax.ppermute(own, 'core', swap)]
  transfers between devices with their start and end apart: 6 -> 6, of which waited for: 1 -> 2; matrix products, arithmetic and copies ran while one was open for 10% -> 3% of each run, Pallas kernels for 5% -> 5%
where the time goes in v4:
time: 88.9 us; the launch traced here: 88.5 us
  blocking collectives  45.3 us (51%)
  starting transfers between devices  19.7 us (22%)
  local copies, waits for them, and re-layouts  9.41 us (11%)
  Pallas kernels  8.69 us (10%)
  waiting for transfers between devices  2.36 us (3%)
  other arithmetic  2.25 us (3%)
    all_to_all x3, blocking collectives, all_to_all(): return lax.all_to_all(x, axes, 0, 0, tiled=True)  45.3 us
    ppermute x4, starting transfers between devices, shift(): return lax.ppermute(x, axes, pairs)  14.4 us
    unnamed x30, local copies, waits for them, and re-layouts  8.96 us
    pallas_call x5, Pallas kernels, call(): pl.pallas_call(kernel, out_shape=out_shape, in_specs=[smem] * scalars + [...  8.69 us
    ppermute x1, starting transfers between devices, reduce_all(): other = lax.ppermute(own, 'core', swap)  5.16 us
  transfers between devices with their start and end apart: 6, of which 2 were waited for; matrix products, arithmetic and copies ran while one was open for 3% of the time, Pallas kernels for 5%

profile of v4, /device:TPU:1, one launch (start us, length us, event | category | flops | bytes accessed | tf_op | source)
XLA Modules:
  0.0 88.5 jit_solution(2485411377631932018)
XLA Ops:
  0.6 0.0 copy-start
  0.6 0.0 copy-start.12
  0.7 0.0 copy-start.11
  0.7 1.4 %copy.10 = bf16[256,8,128]{0,2,1:T(8,128)(2,1)S(1)} copy(bf16[256,8,128]{2,1,0:T(8,128)(2,1)} %param.6) | data formatting | bytes 1048576 | tf_op args[1]
  2.1 5.1 %collective-permute-start.1 = (bf16[3,128,256]{2,1,0:T(8,128)(2,1)S(1)}, bf16[3,128,256]{2,1,0:T(8,128)(2,1)S(1)}, u32[]{:S(2)}, u32[]{:S(2)}) collective-permute-start(bf16[3,128,256]{2,1,0:T(8,128)(2,1)S(1)} %get-tuple-element.28), channel_id=1, source_target_pairs={{16,0},{32,16},{48,32},{64,48},{80,64},{96,80},{112,96},{128,112},... | collective-permute-start | bytes 589832 | tf_op jit(solution)/shard_map/ppermute | solution.py:20
  7.3 1.9 %collective-permute-start = (bf16[3,128,256]{2,1,0:T(8,128)(2,1)S(1)}, bf16[3,128,256]{2,1,0:T(8,128)(2,1)S(1)}, u32[]{:S(2)}, u32[]{:S(2)}) collective-permute-start(bf16[3,128,256]{2,1,0:T(8,128)(2,1)S(1)} %get-tuple-element.29), channel_id=1, source_target_pairs={{0,16},{16,32},{32,48},{48,64},{64,80},{80,96},{96,112},{112,128},... | collective-permute-start | bytes 589832 | tf_op jit(solution)/shard_map/ppermute | solution.py:20
  9.2 0.0 copy-done.12
  9.2 0.1 dynamic_slice.6
  9.3 0.0 copy-done.11
  9.3 0.9 %copy.15 = bf16[32,8,8,128]{3,1,2,0:T(8,128)(2,1)} copy(bf16[32,8,8,128]{3,2,1,0:T(8,128)(2,1)S(1)} %bitcast.21) | data formatting | bytes 1048576
  10.2 0.0 copy-done
  10.2 0.2 constant_dynamic-slice_fusion
  10.5 0.5 copy.11
  10.9 0.0 copy-start.6
  11.0 0.1 broadcast_compare_fusion
  11.1 0.0 collective-permute-done.1.down
  11.1 0.0 copy-start.2
  11.1 0.7 collective-permute-done.up
  11.8 0.0 copy-start.4
  11.8 0.7 shard_map.69
  12.5 2.1 %collective-permute-start.2 = (bf16[14,16,256]{2,1,0:T(8,128)(2,1)}, bf16[14,16,256]{2,1,0:T(8,128)(2,1)}, u32[]{:S(2)}, u32[]{:S(2)}) collective-permute-start(bf16[14,16,256]{2,1,0:T(8,128)(2,1)} %get-tuple-element.15), channel_id=1, source_target_pairs={{0,1},{1,2},{2,3},{3,4},{4,5},{5,6},{6,7},{7,8},{8,9},{9,10},{10,1... | collective-permute-start | bytes 344072 | tf_op jit(solution)/shard_map/ppermute | solution.py:20
  14.6 5.3 %collective-permute-start.3 = (bf16[14,16,256]{2,1,0:T(8,128)(2,1)}, bf16[14,16,256]{2,1,0:T(8,128)(2,1)}, u32[]{:S(2)}, u32[]{:S(2)}) collective-permute-start(bf16[14,16,256]{2,1,0:T(8,128)(2,1)} %get-tuple-element.16), channel_id=1, source_target_pairs={{0,15},{1,0},{2,1},{3,2},{4,3},{5,4},{6,5},{7,6},{8,7},{9,8},{10,9... | collective-permute-start | bytes 344072 | tf_op jit(solution)/shard_map/ppermute | solution.py:20
  19.9 0.0 copy-done.2
  19.9 0.0 copy-done.4
  19.9 0.0 copy-done.6
  19.9 1.3 %shard_map.68 = (bf16[8,288,512]{2,1,0:T(8,128)(2,1)S(1)}, bf16[256,512]{1,0:T(8,128)(2,1)S(1)}, bf16[256,512]{1,0:T(8,128)(2,1)S(1)}) custom-call(s32[1]{0:T(128)} %bitcast.off_ref, bf16[9,7,16,33]{3,2,1,0:T(8,128)(2,1)S(1)} %select_bitcast_fusion.taps, bf16[256,1024]{1,0:T(8,128)(2,1)S(1)} %bitcast.17), custom_call_target="tpu_custom_call" | custom-call | flops 1000000000 | bytes 1000000 | tf_op jit(solution)/shard_map/pallas_call | solution.py:120
  21.2 0.0 copy-start.7
  21.3 0.7 copy-done.7
  21.9 0.0 copy-start.9
  21.9 0.7 copy-done.9
  22.6 0.0 copy-start.3
  22.7 0.9 %copy-done.3 = bf16[3,128,256]{2,1,0:T(8,128)(2,1)S(1)} copy-done((bf16[3,128,256]{2,1,0:T(8,128)(2,1)S(1)}, bf16[3,128,256]{2,1,0:T(8,128)(2,1)}, u32[]{:S(2)}) %copy-start.3) | copy-done | bytes 196632
  23.6 0.0 copy-start.5
  23.6 0.9 %copy-done.5 = bf16[3,128,256]{2,1,0:T(8,128)(2,1)S(1)} copy-done((bf16[3,128,256]{2,1,0:T(8,128)(2,1)S(1)}, bf16[3,128,256]{2,1,0:T(8,128)(2,1)}, u32[]{:S(2)}) %copy-start.5) | copy-done | bytes 196632
  24.5 0.0 copy-start.10
  24.5 0.9 %copy-done.10 = bf16[256,512]{1,0:T(8,128)(2,1)S(1)} copy-done((bf16[256,512]{1,0:T(8,128)(2,1)S(1)}, bf16[256,512]{1,0:T(8,128)(2,1)}, u32[]{:S(2)}) %copy-start.10) | copy-done | bytes 262168
  25.5 0.0 copy-start.8
  25.5 2.1 %shard_map.70 = (bf16[9,8,64,256]{3,2,1,0:T(8,128)(2,1)S(1)}, f32[9,256,256]{2,1,0:T(8,128)S(1)}) custom-call(bf16[8,288,512]{2,1,0:T(8,128)(2,1)S(1)} %get-tuple-element.14.band, bf16[8,128,256]{2,1,0:T(8,128)(2,1)S(1)} %bitcast.14, bf16[3,128,256]{2,1,0:T(8,128)(2,1)S(1)} %copy-done.5, bf16[3,128,256]{2,1,0:T(8,128)(2,1)S(1)} %copy-done.3, ...), custom_call_target="tpu_custom_call" | custom-call | flops 1000000000 | bytes 1000000 | tf_op jit(solution)/shard_map/pallas_call | solution.py:120
  27.6 0.0 collective-permute-done.2.left
  27.6 0.0 collective-permute-done.3.right
  27.6 0.0 copy-done.8
  27.6 3.1 %shard_map.71 = (bf16[9,8,64,256]{3,2,1,0:T(8,128)(2,1)S(1)}, f32[9,256,128]{2,1,0:T(8,128)S(1)}, f32[9,256,128]{2,1,0:T(8,128)S(1)}) custom-call(bf16[8,288,512]{2,1,0:T(8,128)(2,1)S(1)} %get-tuple-element.14.band, bf16[8,128,256]{2,1,0:T(8,128)(2,1)S(1)} %bitcast.15, bf16[3,128,256]{2,1,0:T(8,128)(2,1)S(1)} %copy-done.5, ...), custom_call_target="tpu_custom_call" | custom-call | flops 1000000000 | bytes 1000000 | tf_op jit(solution)/shard_map/pallas_call | solution.py:120
  30.7 0.0 copy-start.1
  30.7 0.1 broadcast_select_fusion.2
  30.9 0.1 collective-permute-start.4
  31.0 1.0 %copy-done.1 = bf16[9,256,256]{2,1,0:T(8,128)(2,1)S(1)} copy-done((bf16[9,256,256]{2,1,0:T(8,128)(2,1)S(1)}, bf16[9,256,256]{2,1,0:T(8,128)(2,1)}, u32[]{:S(2)}) %copy-start.1) | copy-done | bytes 1179672
  32.0 1.4 %shard_map.72 = bf16[256,1024]{1,0:T(8,128)(2,1)S(1)} custom-call(bf16[9,256,256]{2,1,0:T(8,128)(2,1)S(1)} %copy-done.1, bf16[9,8,64,256]{3,2,1,0:T(8,128)(2,1)S(1)} %get-tuple-element.22.mid_ref, bf16[9,8,64,256]{3,2,1,0:T(8,128)(2,1)S(1)} %get-tuple-element.23.edge_ref), custom_call_target="tpu_custom_call" | custom-call | flops 1000000000 | bytes 1000000 | tf_op jit(solution)/shard_map/pallas_call | solution.py:120
  33.4 0.9 %copy.13 = bf16[32,8,8,128]{3,2,1,0:T(8,128)(2,1)} copy(bf16[32,8,8,128]{3,1,2,0:T(8,128)(2,1)S(1)} %bitcast.16) | data formatting | bytes 1048576
  34.3 0.0 collective-permute-done.4
  34.3 0.2 add_convert_fusion
  34.5 17.5 %all_to_all.15 = bf16[16,144,128]{2,1,0:T(8,128)(2,1)S(1)} all-to-all(bf16[16,144,128]{2,1,0:T(8,128)(2,1)S(1)} %bitcast.18), channel_id=1, replica_groups=mesh['y'=4,'x_lo'=2,'core'=2,'z'=8,'x_hi'=2] {'y','x_hi','x_lo'}, dimensions={0} | all-to-all | bytes 1179648 | tf_op jit(solution)/shard_map/all_to_all | solution.py:146
  52.1 0.1 reduce_sum.21
  52.2 15.5 %all_to_all.16 = bf16[8,144,128]{2,1,0:T(8,128)(2,1)S(1)} all-to-all(bf16[8,144,128]{2,1,0:T(8,128)(2,1)S(1)} %broadcast_in_dim.32), channel_id=1, replica_groups=mesh['y'=4,'x_lo'=2,'core'=2,'z'=8,'x_hi'=2] {'z'}, dimensions={0} | all-to-all | bytes 589824 | tf_op jit(solution)/shard_map/all_to_all | solution.py:146
  67.8 0.1 broadcast_in_dim.33
  67.8 12.2 %all_to_all.17 = bf16[16,144,128]{2,1,0:T(8,128)(2,1)S(1)} all-to-all(bf16[16,144,128]{2,1,0:T(8,128)(2,1)S(1)} %broadcast_in_dim.33), channel_id=1, replica_groups=mesh['y'=4,'x_lo'=2,'core'=2,'z'=8,'x_hi'=2] {'y','x_hi','x_lo'}, dimensions={0} | all-to-all | bytes 1179648 | tf_op jit(solution)/shard_map/all_to_all | solution.py:146
  80.1 5.2 %collective-permute-start.5 = (bf16[9,256,128]{2,1,0:T(8,128)(2,1)S(1)}, bf16[9,256,128]{2,1,0:T(8,128)(2,1)S(1)}, u32[]{:S(2)}, u32[]{:S(2)}) collective-permute-start(bf16[9,256,128]{2,1,0:T(8,128)(2,1)S(1)} %bitcast.19), channel_id=1, source_target_pairs={{0,16},{16,0},{1,17},{17,1},{2,18},{18,2},{3,19},{19,3},{4,20},{20... | collective-permute-start | bytes 1769480 | tf_op jit(solution)/shard_map/ppermute | solution.py:168
  85.2 1.6 %collective-permute-done.5 = bf16[9,256,128]{2,1,0:T(8,128)(2,1)S(1)} collective-permute-done((bf16[9,256,128]{2,1,0:T(8,128)(2,1)S(1)}, bf16[9,256,128]{2,1,0:T(8,128)(2,1)S(1)}, u32[]{:S(2)}, u32[]{:S(2)}) %collective-permute-start.5) | collective-permute-done | bytes 589856 | tf_op jit(solution)/shard_map/ppermute | solution.py:168
  86.9 0.1 broadcast_select_fusion.1
  87.0 1.6 %maximum_convert_fusion = f32[9,256,256]{2,1,0:T(8,128)} fusion(bf16[9,256,128]{2,1,0:T(8,128)(2,1)S(1)} %get-tuple-element.27, bf16[9,256,128]{2,1,0:T(8,128)(2,1)S(1)} %get-tuple-element.26), kind=kLoop, calls=%fused_computation | loop fusion | flops 2359296 | bytes 3538944 | tf_op jit(solution)/shard_map/convert_element_type | solution.py:170
  (6 shorter events, 0.1 us)
Async XLA Ops:
  0.6 9.6 %copy-start = (bf16[9,128,7,33]{1,2,3,0:T(8,128)(2,1)S(1)}, bf16[9,128,7,33]{1,2,3,0:T(8,128)(2,1)}, u32[]{:S(2)}) copy-start(bf16[9,128,7,33]{1,2,3,0:T(8,128)(2,1)} %param.8) | copy-start | bytes 1596676
  0.6 8.6 %copy-start.12 = (s32[128]{0:T(128)S(1)}, s32[128]{0:T(128)}, u32[]{:S(2)}) copy-start(s32[128]{0:T(128)} %param.9) | copy-start | bytes 1540
  0.7 8.7 %copy-start.11 = (bf16[256,8,128]{2,1,0:T(8,128)(2,1)S(1)}, bf16[256,8,128]{2,1,0:T(8,128)(2,1)}, u32[]{:S(2)}) copy-start(bf16[256,8,128]{2,1,0:T(8,128)(2,1)} %param.5) | copy-start | bytes 1572868
  2.1 8.9 %collective-permute-start.1 = (bf16[3,128,256]{2,1,0:T(8,128)(2,1)S(1)}, bf16[3,128,256]{2,1,0:T(8,128)(2,1)S(1)}, u32[]{:S(2)}, u32[]{:S(2)}) collective-permute-start(bf16[3,128,256]{2,1,0:T(8,128)(2,1)S(1)} %get-tuple-element.28), channel_id=1, source_target_pairs={{16,0},{32,16},{48,32},{64,48},{80,64},{96,80},{112,96},{128,112},... | collective-permute-start | bytes 589832 | tf_op jit(solution)/shard_map/ppermute | solution.py:20
  7.3 4.5 %collective-permute-start = (bf16[3,128,256]{2,1,0:T(8,128)(2,1)S(1)}, bf16[3,128,256]{2,1,0:T(8,128)(2,1)S(1)}, u32[]{:S(2)}, u32[]{:S(2)}) collective-permute-start(bf16[3,128,256]{2,1,0:T(8,128)(2,1)S(1)} %get-tuple-element.29), channel_id=1, source_target_pairs={{0,16},{16,32},{32,48},{48,64},{64,80},{80,96},{96,112},{112,128},... | collective-permute-start | bytes 589832 | tf_op jit(solution)/shard_map/ppermute | solution.py:20
  10.9 9.0 %copy-start.6 = (bf16[32,8,8,128]{3,1,2,0:T(8,128)(2,1)S(1)}, bf16[32,8,8,128]{3,1,2,0:T(8,128)(2,1)}, u32[]{:S(2)}) copy-start(bf16[32,8,8,128]{3,1,2,0:T(8,128)(2,1)} %copy.15) | copy-start | bytes 1572868
  11.1 8.8 %copy-start.2 = (bf16[3,128,256]{2,1,0:T(8,128)(2,1)}, bf16[3,128,256]{2,1,0:T(8,128)(2,1)S(1)}, u32[]{:S(2)}) copy-start(bf16[3,128,256]{2,1,0:T(8,128)(2,1)S(1)} %collective-permute-done.1.down) | copy-start | bytes 589828
  11.8 8.1 %copy-start.4 = (bf16[3,128,256]{2,1,0:T(8,128)(2,1)}, bf16[3,128,256]{2,1,0:T(8,128)(2,1)S(1)}, u32[]{:S(2)}) copy-start(bf16[3,128,256]{2,1,0:T(8,128)(2,1)S(1)} %collective-permute-done.up) | copy-start | bytes 589828
  12.5 15.0 %collective-permute-start.2 = (bf16[14,16,256]{2,1,0:T(8,128)(2,1)}, bf16[14,16,256]{2,1,0:T(8,128)(2,1)}, u32[]{:S(2)}, u32[]{:S(2)}) collective-permute-start(bf16[14,16,256]{2,1,0:T(8,128)(2,1)} %get-tuple-element.15), channel_id=1, source_target_pairs={{0,1},{1,2},{2,3},{3,4},{4,5},{5,6},{6,7},{7,8},{8,9},{9,10},{10,1... | collective-permute-start | bytes 344072 | tf_op jit(solution)/shard_map/ppermute | solution.py:20
  14.6 13.0 %collective-permute-start.3 = (bf16[14,16,256]{2,1,0:T(8,128)(2,1)}, bf16[14,16,256]{2,1,0:T(8,128)(2,1)}, u32[]{:S(2)}, u32[]{:S(2)}) collective-permute-start(bf16[14,16,256]{2,1,0:T(8,128)(2,1)} %get-tuple-element.16), channel_id=1, source_target_pairs={{0,15},{1,0},{2,1},{3,2},{4,3},{5,4},{6,5},{7,6},{8,7},{9,8},{10,9... | collective-permute-start | bytes 344072 | tf_op jit(solution)/shard_map/ppermute | solution.py:20
  21.2 0.7 copy-start.7
  21.9 0.7 copy-start.9
  22.6 0.9 %copy-start.3 = (bf16[3,128,256]{2,1,0:T(8,128)(2,1)S(1)}, bf16[3,128,256]{2,1,0:T(8,128)(2,1)}, u32[]{:S(2)}) copy-start(bf16[3,128,256]{2,1,0:T(8,128)(2,1)} %copy-done.2) | copy-start | bytes 589828
  23.6 0.9 %copy-start.5 = (bf16[3,128,256]{2,1,0:T(8,128)(2,1)S(1)}, bf16[3,128,256]{2,1,0:T(8,128)(2,1)}, u32[]{:S(2)}) copy-start(bf16[3,128,256]{2,1,0:T(8,128)(2,1)} %copy-done.4) | copy-start | bytes 589828
  24.5 0.9 %copy-start.10 = (bf16[256,512]{1,0:T(8,128)(2,1)S(1)}, bf16[256,512]{1,0:T(8,128)(2,1)}, u32[]{:S(2)}) copy-start(bf16[256,512]{1,0:T(8,128)(2,1)} %copy-done.9) | copy-start | bytes 786436
  25.5 2.2 %copy-start.8 = (bf16[256,512]{1,0:T(8,128)(2,1)S(1)}, bf16[256,512]{1,0:T(8,128)(2,1)}, u32[]{:S(2)}) copy-start(bf16[256,512]{1,0:T(8,128)(2,1)} %copy-done.7) | copy-start | bytes 786436
  30.7 1.3 %copy-start.1 = (bf16[9,256,256]{2,1,0:T(8,128)(2,1)S(1)}, bf16[9,256,256]{2,1,0:T(8,128)(2,1)}, u32[]{:S(2)}) copy-start(bf16[9,256,256]{2,1,0:T(8,128)(2,1)} %w_ref.1) | copy-start | bytes 3538948
  30.9 3.4 %collective-permute-start.4 = (f32[9,256,128]{2,1,0:T(8,128)S(1)}, f32[9,256,128]{2,1,0:T(8,128)S(1)}, u32[]{:S(2)}, u32[]{:S(2)}) collective-permute-start(f32[9,256,128]{2,1,0:T(8,128)S(1)} %broadcast_select_fusion.2), channel_id=1, source_target_pairs={{0,16},{16,0},{1,17},{17,1},{2,18},{18,2},{3,19},{19,3},{4,20},{20... | collective-permute-start | bytes 3538952 | tf_op jit(solution)/shard_map/ppermute | solution.py:161
  80.1 6.8 %collective-permute-start.5 = (bf16[9,256,128]{2,1,0:T(8,128)(2,1)S(1)}, bf16[9,256,128]{2,1,0:T(8,128)(2,1)S(1)}, u32[]{:S(2)}, u32[]{:S(2)}) collective-permute-start(bf16[9,256,128]{2,1,0:T(8,128)(2,1)S(1)} %bitcast.19), channel_id=1, source_target_pairs={{0,16},{16,0},{1,17},{17,1},{2,18},{18,2},{3,19},{19,3},{4,20},{20... | collective-permute-start | bytes 1769480 | tf_op jit(solution)/shard_map/ppermute | solution.py:168

commit v5 on v4

--- a/solution.py
+++ b/solution.py
@@ -12,12 +12,18 @@
 bf16, f32 = jnp.bfloat16, jnp.float32
 
 
-def shift(x, axes, step, closed):
+def exchange(to_next, to_before, axes, closed):
     count = 1
     for axis in axes:
         count *= lax.axis_size(axis)
-    pairs = [(i, (i + step) % count) for i in range(count) if closed or 0 <= i + step < count]
-    return lax.ppermute(x, axes, pairs)
+    even = lax.axis_index(axes[-1]) % 2 == 0
+    near = [(i, i ^ 1) for i in range(count)]
+    far = [(i, (i + 1 - 2 * (i % 2 == 0)) % count) for i in range(count)]
+    if not closed:
+        far = far[1:-1]
+    came_near = lax.ppermute(jnp.where(even, to_next, to_before), axes, near)
+    came_far = lax.ppermute(jnp.where(even, to_before, to_next), axes, far)
+    return jnp.where(even, came_far, came_near), jnp.where(even, came_near, came_far)
 
 
 def tap_rows(basis_table, lon_reach, start, near):
@@ -178,12 +184,10 @@
     shape = jax.ShapeDtypeStruct
     core = lax.axis_index("core")
     main = jnp.transpose(grad_out, (1, 2, 0))
-    up = shift(main[lat_dev - half :], LAT, 1, False)
-    down = shift(main[:half], LAT, -1, False)
+    up, down = exchange(main[lat_dev - half :], main[:half], LAT, False)
     rim = shape((near, side, channels), bf16)
     tail, head = call(rim_kernel, (rim, rim), (main, up, down), flops=10**6, mib=4)
-    left = shift(tail, LON, 1, True)
-    right = shift(head, LON, -1, True)
+    left, right = exchange(tail, head, LON, True)
     above = lax.axis_index(LAT) * lat_dev - half
     held = min(16, nlat_all)
     start = jnp.clip(above, 0, nlat_all - held)

time: 88.9 us -> 88.9 us (level)
  waiting for transfers between devices: 2.36 us -> 5.53 us
  blocking collectives: 45.3 us -> 43 us
  other arithmetic: 2.25 us -> 4.09 us
  Pallas kernels: 8.69 us -> 7.02 us
  starting transfers between devices: 19.7 us -> 18.5 us
    ppermute x4, waiting for transfers between devices: 0.72 us -> 3.9 us  [the longest x2 3.89 us: exchange(): came_far = lax.ppermute(jnp.where(even, to_before, to_next), axes, far)]
    all_to_all x3, blocking collectives: 45.3 us -> 43 us  [all_to_all(): return lax.all_to_all(x, axes, 0, 0, tiled=True)]
    select_n x0 -> x4, other arithmetic: none -> 1.83 us  [the longest x2 1.01 us: exchange(): jnp.where(even, came_near, came_far)]
    pallas_call x5, Pallas kernels: 8.69 us -> 7.02 us  [call(): pl.pallas_call(kernel, out_shape=out_shape, in_specs=[smem] * scalars + [...]
    ppermute x4, starting transfers between devices: 14.4 us -> 13.3 us  [the longest x2 7.43 us: exchange(): came_far = lax.ppermute(jnp.where(even, to_before, to_next), axes, far)]
where the time goes in v5:
time: 88.9 us; the launch traced here: 88.5 us
  blocking collectives  43 us (48%)
  starting transfers between devices  18.5 us (21%)
  local copies, waits for them, and re-layouts  9.38 us (11%)
  Pallas kernels  7.02 us (8%)
  waiting for transfers between devices  5.53 us (6%)
  other arithmetic  4.09 us (5%)
  between operations  0.93 us (1%)
    all_to_all x3, blocking collectives, all_to_all(): return lax.all_to_all(x, axes, 0, 0, tiled=True)  43 us
    unnamed x30, local copies, waits for them, and re-layouts  8.96 us
    ppermute x2, starting transfers between devices, exchange(): came_far = lax.ppermute(jnp.where(even, to_before, to_next), axes, far)  7.43 us
    pallas_call x5, Pallas kernels, call(): pl.pallas_call(kernel, out_shape=out_shape, in_specs=[smem] * scalars + [...  7.02 us
    ppermute x2, starting transfers between devices, exchange(): came_near = lax.ppermute(jnp.where(even, to_next, to_before), axes, near)  5.86 us
    ppermute x1, starting transfers between devices, reduce_all(): other = lax.ppermute(own, 'core', swap)  5.16 us
    ppermute x2, waiting for transfers between devices, exchange(): came_far = lax.ppermute(jnp.where(even, to_before, to_next), axes, far)  3.89 us
  transfers between devices with their start and end apart: 6, of which 2 were waited for; matrix products, arithmetic and copies ran while one was open for 3% of the time, Pallas kernels for 5%

profile of v5, /device:TPU:1, one launch (start us, length us, event | category | flops | bytes accessed | tf_op | source)
XLA Modules:
  0.0 88.5 jit_solution(12634833945925017003)
XLA Ops:
  0.6 0.0 copy-start
  0.6 0.0 copy-start.12
  0.7 0.0 copy-start.11
  0.7 1.4 %copy.10 = bf16[256,8,128]{0,2,1:T(8,128)(2,1)S(1)} copy(bf16[256,8,128]{2,1,0:T(8,128)(2,1)} %param.6) | data formatting | bytes 1048576 | tf_op args[1]
  2.1 3.3 %collective-permute-start.1 = (bf16[3,128,256]{2,1,0:T(8,128)(2,1)S(1)}, bf16[3,128,256]{2,1,0:T(8,128)(2,1)S(1)}, u32[]{:S(2)}, u32[]{:S(2)}) collective-permute-start(bf16[3,128,256]{2,1,0:T(8,128)(2,1)S(1)} %get-tuple-element.28), channel_id=1, source_target_pairs={{0,16},{16,0},{32,48},{48,32},{64,80},{80,64},{96,112},{112,96},{1... | collective-permute-start | bytes 589832 | tf_op jit(solution)/shard_map/ppermute | solution.py:24
  5.5 1.9 %collective-permute-start = (bf16[3,128,256]{2,1,0:T(8,128)(2,1)S(1)}, bf16[3,128,256]{2,1,0:T(8,128)(2,1)S(1)}, u32[]{:S(2)}, u32[]{:S(2)}) collective-permute-start(bf16[3,128,256]{2,1,0:T(8,128)(2,1)S(1)} %get-tuple-element.29), channel_id=1, source_target_pairs={{16,32},{32,16},{48,64},{64,48},{80,96},{96,80},{112,128},{128,112... | collective-permute-start | bytes 589832 | tf_op jit(solution)/shard_map/ppermute | solution.py:25
  7.4 0.0 copy-done.12
  7.4 0.1 dynamic_slice.6
  7.5 0.0 copy-done.11
  7.5 0.9 %copy.15 = bf16[32,8,8,128]{3,1,2,0:T(8,128)(2,1)} copy(bf16[32,8,8,128]{3,2,1,0:T(8,128)(2,1)S(1)} %bitcast.21) | data formatting | bytes 1048576
  8.4 0.0 copy-done
  8.4 0.2 constant_dynamic-slice_fusion
  8.6 0.5 copy.11
  9.1 0.1 broadcast_compare_fusion
  9.2 0.0 copy-start.6
  9.3 0.0 collective-permute-done.1
  9.3 3.9 %collective-permute-done = bf16[3,128,256]{2,1,0:T(8,128)(2,1)S(1)} collective-permute-done((bf16[3,128,256]{2,1,0:T(8,128)(2,1)S(1)}, bf16[3,128,256]{2,1,0:T(8,128)(2,1)S(1)}, u32[]{:S(2)}, u32[]{:S(2)}) %collective-permute-start) | collective-permute-done | bytes 196640 | tf_op jit(solution)/shard_map/ppermute | solution.py:25
  13.2 0.0 copy-start.1
  13.2 0.0 copy-start.3
  13.2 0.8 broadcast_select_fusion.9
  14.0 2.5 %collective-permute-start.3 = (bf16[14,16,256]{2,1,0:T(8,128)(2,1)}, bf16[14,16,256]{2,1,0:T(8,128)(2,1)}, u32[]{:S(2)}, u32[]{:S(2)}) collective-permute-start(bf16[14,16,256]{2,1,0:T(8,128)(2,1)} %get-tuple-element.34), channel_id=1, source_target_pairs={{0,1},{1,0},{2,3},{3,2},{4,5},{5,4},{6,7},{7,6},{8,9},{9,8},{10,11... | collective-permute-start | bytes 344072 | tf_op jit(solution)/shard_map/ppermute | solution.py:24
  16.6 5.5 %collective-permute-start.2 = (bf16[14,16,256]{2,1,0:T(8,128)(2,1)}, bf16[14,16,256]{2,1,0:T(8,128)(2,1)}, u32[]{:S(2)}, u32[]{:S(2)}) collective-permute-start(bf16[14,16,256]{2,1,0:T(8,128)(2,1)} %get-tuple-element.35), channel_id=1, source_target_pairs={{0,15},{1,2},{2,1},{3,4},{4,3},{5,6},{6,5},{7,8},{8,7},{9,10},{10,... | collective-permute-start | bytes 344072 | tf_op jit(solution)/shard_map/ppermute | solution.py:25
  22.1 0.0 copy-done.1
  22.1 0.0 copy-done.3
  22.1 0.0 copy-done.6
  22.1 1.3 %shard_map.68 = (bf16[8,288,512]{2,1,0:T(8,128)(2,1)S(1)}, bf16[256,512]{1,0:T(8,128)(2,1)S(1)}, bf16[256,512]{1,0:T(8,128)(2,1)S(1)}) custom-call(s32[1]{0:T(128)} %bitcast.off_ref, bf16[9,7,16,33]{3,2,1,0:T(8,128)(2,1)S(1)} %select_bitcast_fusion.taps, bf16[256,1024]{1,0:T(8,128)(2,1)S(1)} %bitcast.17), custom_call_target="tpu_custom_call" | custom-call | flops 1000000000 | bytes 1000000 | tf_op jit(solution)/shard_map/pallas_call | solution.py:126
  23.4 0.0 copy-start.7
  23.4 0.7 copy-done.7
  24.1 0.0 copy-start.9
  24.1 0.7 copy-done.9
  24.8 0.0 copy-start.2
  24.8 0.9 %copy-done.2 = bf16[3,128,256]{2,1,0:T(8,128)(2,1)S(1)} copy-done((bf16[3,128,256]{2,1,0:T(8,128)(2,1)S(1)}, bf16[3,128,256]{2,1,0:T(8,128)(2,1)}, u32[]{:S(2)}) %copy-start.2) | copy-done | bytes 196632
  25.8 0.0 copy-start.4
  25.8 0.9 %copy-done.4 = bf16[3,128,256]{2,1,0:T(8,128)(2,1)S(1)} copy-done((bf16[3,128,256]{2,1,0:T(8,128)(2,1)S(1)}, bf16[3,128,256]{2,1,0:T(8,128)(2,1)}, u32[]{:S(2)}) %copy-start.4) | copy-done | bytes 196632
  26.7 0.0 copy-start.10
  26.7 0.9 %copy-done.10 = bf16[256,512]{1,0:T(8,128)(2,1)S(1)} copy-done((bf16[256,512]{1,0:T(8,128)(2,1)S(1)}, bf16[256,512]{1,0:T(8,128)(2,1)}, u32[]{:S(2)}) %copy-start.10) | copy-done | bytes 262168
  27.6 0.0 copy-start.8
  27.6 2.1 %shard_map.70 = (bf16[9,8,64,256]{3,2,1,0:T(8,128)(2,1)S(1)}, f32[9,256,256]{2,1,0:T(8,128)S(1)}) custom-call(bf16[8,288,512]{2,1,0:T(8,128)(2,1)S(1)} %get-tuple-element.14.band, bf16[8,128,256]{2,1,0:T(8,128)(2,1)S(1)} %bitcast.14, bf16[3,128,256]{2,1,0:T(8,128)(2,1)S(1)} %copy-done.4, bf16[3,128,256]{2,1,0:T(8,128)(2,1)S(1)} %copy-done.2, ...), custom_call_target="tpu_custom_call" | custom-call | flops 1000000000 | bytes 1000000 | tf_op jit(solution)/shard_map/pallas_call | solution.py:126
  29.8 0.0 collective-permute-done.3
  29.8 0.0 collective-permute-done.2
  29.8 1.0 %broadcast_select_fusion.7 = (bf16[14,16,256]{2,1,0:T(8,128)(2,1)S(1)}, bf16[14,16,256]{2,1,0:T(8,128)(2,1)S(1)}) fusion(bf16[14,16,256]{2,1,0:T(8,128)(2,1)} %collective-permute-done.3, bf16[14,16,256]{2,1,0:T(8,128)(2,1)} %collective-permute-done.2, pred[]{:T(512)S(6)} %eq.17), kind=kLoop, calls=%fused_computation.12 | loop fusion | flops 114688 | bytes 458753 | tf_op jit(solution)/shard_map/jit(_where)/select_n | solution.py:26
  30.8 0.0 copy-done.8
  30.8 2.1 %shard_map.71 = (bf16[9,8,64,256]{3,2,1,0:T(8,128)(2,1)S(1)}, f32[9,256,128]{2,1,0:T(8,128)S(1)}, f32[9,256,128]{2,1,0:T(8,128)S(1)}) custom-call(bf16[8,288,512]{2,1,0:T(8,128)(2,1)S(1)} %get-tuple-element.14.band, bf16[8,128,256]{2,1,0:T(8,128)(2,1)S(1)} %bitcast.15, bf16[3,128,256]{2,1,0:T(8,128)(2,1)S(1)} %copy-done.4, ...), custom_call_target="tpu_custom_call" | custom-call | flops 1000000000 | bytes 1000000 | tf_op jit(solution)/shard_map/pallas_call | solution.py:126
  32.9 0.0 copy-start.5
  32.9 0.1 broadcast_select_fusion.2
  33.1 0.1 collective-permute-start.4
  33.2 1.0 %copy-done.5 = bf16[9,256,256]{2,1,0:T(8,128)(2,1)S(1)} copy-done((bf16[9,256,256]{2,1,0:T(8,128)(2,1)S(1)}, bf16[9,256,256]{2,1,0:T(8,128)(2,1)}, u32[]{:S(2)}) %copy-start.5) | copy-done | bytes 1179672
  34.2 1.4 %shard_map.72 = bf16[256,1024]{1,0:T(8,128)(2,1)S(1)} custom-call(bf16[9,256,256]{2,1,0:T(8,128)(2,1)S(1)} %copy-done.5, bf16[9,8,64,256]{3,2,1,0:T(8,128)(2,1)S(1)} %get-tuple-element.22.mid_ref, bf16[9,8,64,256]{3,2,1,0:T(8,128)(2,1)S(1)} %get-tuple-element.23.edge_ref), custom_call_target="tpu_custom_call" | custom-call | flops 1000000000 | bytes 1000000 | tf_op jit(solution)/shard_map/pallas_call | solution.py:126
  35.6 0.9 %copy.13 = bf16[32,8,8,128]{3,2,1,0:T(8,128)(2,1)} copy(bf16[32,8,8,128]{3,1,2,0:T(8,128)(2,1)S(1)} %bitcast.16) | data formatting | bytes 1048576
  36.5 0.0 collective-permute-done.4
  36.5 0.2 add_convert_fusion
  36.8 16.5 %all_to_all.15 = bf16[16,144,128]{2,1,0:T(8,128)(2,1)S(1)} all-to-all(bf16[16,144,128]{2,1,0:T(8,128)(2,1)S(1)} %bitcast.18), channel_id=1, replica_groups=mesh['y'=4,'x_lo'=2,'core'=2,'z'=8,'x_hi'=2] {'y','x_hi','x_lo'}, dimensions={0} | all-to-all | bytes 1179648 | tf_op jit(solution)/shard_map/all_to_all | solution.py:152
  53.3 0.1 reduce_sum.21
  53.4 14.3 %all_to_all.16 = bf16[8,144,128]{2,1,0:T(8,128)(2,1)S(1)} all-to-all(bf16[8,144,128]{2,1,0:T(8,128)(2,1)S(1)} %broadcast_in_dim.32), channel_id=1, replica_groups=mesh['y'=4,'x_lo'=2,'core'=2,'z'=8,'x_hi'=2] {'z'}, dimensions={0} | all-to-all | bytes 589824 | tf_op jit(solution)/shard_map/all_to_all | solution.py:152
  67.7 0.1 broadcast_in_dim.33
  67.8 12.2 %all_to_all.17 = bf16[16,144,128]{2,1,0:T(8,128)(2,1)S(1)} all-to-all(bf16[16,144,128]{2,1,0:T(8,128)(2,1)S(1)} %broadcast_in_dim.33), channel_id=1, replica_groups=mesh['y'=4,'x_lo'=2,'core'=2,'z'=8,'x_hi'=2] {'y','x_hi','x_lo'}, dimensions={0} | all-to-all | bytes 1179648 | tf_op jit(solution)/shard_map/all_to_all | solution.py:152
  80.1 5.2 %collective-permute-start.5 = (bf16[9,256,128]{2,1,0:T(8,128)(2,1)S(1)}, bf16[9,256,128]{2,1,0:T(8,128)(2,1)S(1)}, u32[]{:S(2)}, u32[]{:S(2)}) collective-permute-start(bf16[9,256,128]{2,1,0:T(8,128)(2,1)S(1)} %bitcast.19), channel_id=1, source_target_pairs={{0,16},{16,0},{1,17},{17,1},{2,18},{18,2},{3,19},{19,3},{4,20},{20... | collective-permute-start | bytes 1769480 | tf_op jit(solution)/shard_map/ppermute | solution.py:174
  85.2 1.6 %collective-permute-done.5 = bf16[9,256,128]{2,1,0:T(8,128)(2,1)S(1)} collective-permute-done((bf16[9,256,128]{2,1,0:T(8,128)(2,1)S(1)}, bf16[9,256,128]{2,1,0:T(8,128)(2,1)S(1)}, u32[]{:S(2)}, u32[]{:S(2)}) %collective-permute-start.5) | collective-permute-done | bytes 589856 | tf_op jit(solution)/shard_map/ppermute | solution.py:174
  86.9 0.1 broadcast_select_fusion.1
  87.0 1.6 %maximum_convert_fusion = f32[9,256,256]{2,1,0:T(8,128)} fusion(bf16[9,256,128]{2,1,0:T(8,128)(2,1)S(1)} %get-tuple-element.27, bf16[9,256,128]{2,1,0:T(8,128)(2,1)S(1)} %get-tuple-element.26), kind=kLoop, calls=%fused_computation | loop fusion | flops 2359296 | bytes 3538944 | tf_op jit(solution)/shard_map/convert_element_type | solution.py:176
  (8 shorter events, 0.2 us)
Async XLA Ops:
  0.6 7.8 %copy-start = (bf16[9,128,7,33]{1,2,3,0:T(8,128)(2,1)S(1)}, bf16[9,128,7,33]{1,2,3,0:T(8,128)(2,1)}, u32[]{:S(2)}) copy-start(bf16[9,128,7,33]{1,2,3,0:T(8,128)(2,1)} %param.8) | copy-start | bytes 1596676
  0.6 6.8 %copy-start.12 = (s32[128]{0:T(128)S(1)}, s32[128]{0:T(128)}, u32[]{:S(2)}) copy-start(s32[128]{0:T(128)} %param.9) | copy-start | bytes 1540
  0.7 6.9 %copy-start.11 = (bf16[256,8,128]{2,1,0:T(8,128)(2,1)S(1)}, bf16[256,8,128]{2,1,0:T(8,128)(2,1)}, u32[]{:S(2)}) copy-start(bf16[256,8,128]{2,1,0:T(8,128)(2,1)} %param.5) | copy-start | bytes 1572868
  2.1 7.1 %collective-permute-start.1 = (bf16[3,128,256]{2,1,0:T(8,128)(2,1)S(1)}, bf16[3,128,256]{2,1,0:T(8,128)(2,1)S(1)}, u32[]{:S(2)}, u32[]{:S(2)}) collective-permute-start(bf16[3,128,256]{2,1,0:T(8,128)(2,1)S(1)} %get-tuple-element.28), channel_id=1, source_target_pairs={{0,16},{16,0},{32,48},{48,32},{64,80},{80,64},{96,112},{112,96},{1... | collective-permute-start | bytes 589832 | tf_op jit(solution)/shard_map/ppermute | solution.py:24
  5.5 7.7 %collective-permute-start = (bf16[3,128,256]{2,1,0:T(8,128)(2,1)S(1)}, bf16[3,128,256]{2,1,0:T(8,128)(2,1)S(1)}, u32[]{:S(2)}, u32[]{:S(2)}) collective-permute-start(bf16[3,128,256]{2,1,0:T(8,128)(2,1)S(1)} %get-tuple-element.29), channel_id=1, source_target_pairs={{16,32},{32,16},{48,64},{64,48},{80,96},{96,80},{112,128},{128,112... | collective-permute-start | bytes 589832 | tf_op jit(solution)/shard_map/ppermute | solution.py:25
  9.2 12.9 %copy-start.6 = (bf16[32,8,8,128]{3,1,2,0:T(8,128)(2,1)S(1)}, bf16[32,8,8,128]{3,1,2,0:T(8,128)(2,1)}, u32[]{:S(2)}) copy-start(bf16[32,8,8,128]{3,1,2,0:T(8,128)(2,1)} %copy.15) | copy-start | bytes 1572868
  13.2 8.9 %copy-start.1 = (bf16[3,128,256]{2,1,0:T(8,128)(2,1)}, bf16[3,128,256]{2,1,0:T(8,128)(2,1)S(1)}, u32[]{:S(2)}) copy-start(bf16[3,128,256]{2,1,0:T(8,128)(2,1)S(1)} %get-tuple-element.30.down) | copy-start | bytes 589828
  13.2 8.9 %copy-start.3 = (bf16[3,128,256]{2,1,0:T(8,128)(2,1)}, bf16[3,128,256]{2,1,0:T(8,128)(2,1)S(1)}, u32[]{:S(2)}) copy-start(bf16[3,128,256]{2,1,0:T(8,128)(2,1)S(1)} %get-tuple-element.31.up) | copy-start | bytes 589828
  14.0 15.7 %collective-permute-start.3 = (bf16[14,16,256]{2,1,0:T(8,128)(2,1)}, bf16[14,16,256]{2,1,0:T(8,128)(2,1)}, u32[]{:S(2)}, u32[]{:S(2)}) collective-permute-start(bf16[14,16,256]{2,1,0:T(8,128)(2,1)} %get-tuple-element.34), channel_id=1, source_target_pairs={{0,1},{1,0},{2,3},{3,2},{4,5},{5,4},{6,7},{7,6},{8,9},{9,8},{10,11... | collective-permute-start | bytes 344072 | tf_op jit(solution)/shard_map/ppermute | solution.py:24
  16.6 13.2 %collective-permute-start.2 = (bf16[14,16,256]{2,1,0:T(8,128)(2,1)}, bf16[14,16,256]{2,1,0:T(8,128)(2,1)}, u32[]{:S(2)}, u32[]{:S(2)}) collective-permute-start(bf16[14,16,256]{2,1,0:T(8,128)(2,1)} %get-tuple-element.35), channel_id=1, source_target_pairs={{0,15},{1,2},{2,1},{3,4},{4,3},{5,6},{6,5},{7,8},{8,7},{9,10},{10,... | collective-permute-start | bytes 344072 | tf_op jit(solution)/shard_map/ppermute | solution.py:25
  23.4 0.7 copy-start.7
  24.1 0.7 copy-start.9
  24.8 0.9 %copy-start.2 = (bf16[3,128,256]{2,1,0:T(8,128)(2,1)S(1)}, bf16[3,128,256]{2,1,0:T(8,128)(2,1)}, u32[]{:S(2)}) copy-start(bf16[3,128,256]{2,1,0:T(8,128)(2,1)} %copy-done.1) | copy-start | bytes 589828
  25.8 0.9 %copy-start.4 = (bf16[3,128,256]{2,1,0:T(8,128)(2,1)S(1)}, bf16[3,128,256]{2,1,0:T(8,128)(2,1)}, u32[]{:S(2)}) copy-start(bf16[3,128,256]{2,1,0:T(8,128)(2,1)} %copy-done.3) | copy-start | bytes 589828
  26.7 0.9 %copy-start.10 = (bf16[256,512]{1,0:T(8,128)(2,1)S(1)}, bf16[256,512]{1,0:T(8,128)(2,1)}, u32[]{:S(2)}) copy-start(bf16[256,512]{1,0:T(8,128)(2,1)} %copy-done.9) | copy-start | bytes 786436
  27.6 3.1 %copy-start.8 = (bf16[256,512]{1,0:T(8,128)(2,1)S(1)}, bf16[256,512]{1,0:T(8,128)(2,1)}, u32[]{:S(2)}) copy-start(bf16[256,512]{1,0:T(8,128)(2,1)} %copy-done.7) | copy-start | bytes 786436
  32.9 1.3 %copy-start.5 = (bf16[9,256,256]{2,1,0:T(8,128)(2,1)S(1)}, bf16[9,256,256]{2,1,0:T(8,128)(2,1)}, u32[]{:S(2)}) copy-start(bf16[9,256,256]{2,1,0:T(8,128)(2,1)} %w_ref.1) | copy-start | bytes 3538948
  33.1 3.4 %collective-permute-start.4 = (f32[9,256,128]{2,1,0:T(8,128)S(1)}, f32[9,256,128]{2,1,0:T(8,128)S(1)}, u32[]{:S(2)}, u32[]{:S(2)}) collective-permute-start(f32[9,256,128]{2,1,0:T(8,128)S(1)} %broadcast_select_fusion.2), channel_id=1, source_target_pairs={{0,16},{16,0},{1,17},{17,1},{2,18},{18,2},{3,19},{19,3},{4,20},{20... | collective-permute-start | bytes 3538952 | tf_op jit(solution)/shard_map/ppermute | solution.py:167
  80.1 6.8 %collective-permute-start.5 = (bf16[9,256,128]{2,1,0:T(8,128)(2,1)S(1)}, bf16[9,256,128]{2,1,0:T(8,128)(2,1)S(1)}, u32[]{:S(2)}, u32[]{:S(2)}) collective-permute-start(bf16[9,256,128]{2,1,0:T(8,128)(2,1)S(1)} %bitcast.19), channel_id=1, source_target_pairs={{0,16},{16,0},{1,17},{17,1},{2,18},{18,2},{3,19},{19,3},{4,20},{20... | collective-permute-start | bytes 1769480 | tf_op jit(solution)/shard_map/ppermute | solution.py:174

commit v6 on v5

v6 whole, which is shorter than its diff:
```python
import jax
import jax.numpy as jnp
from jax import lax
from jax.experimental import pallas as pl
from jax.experimental.pallas import tpu as pltpu
from jax.sharding import Mesh, PartitionSpec as P

LAT = ("y", "x_lo", "core")
LON = ("z", "x_hi")
PLANE = ("y", "x_hi", "x_lo")
BLOCK = 32
bf16, f32 = jnp.bfloat16, jnp.float32


def exchange(first, second, axes, closed):
    count = 1
    for axis in axes:
        count *= lax.axis_size(axis)
    near = [(i, i ^ 1) for i in range(count)]
    far = [(i, (i + 1 - 2 * (i % 2 == 0)) % count) for i in range(count)]
    if not closed:
        far = far[1:-1]
    return lax.ppermute(first, axes, near), lax.ppermute(second, axes, far)


def tap_rows(basis_table, lon_reach, start, near):
    tap_count = basis_table.shape[3]
    table = lax.dynamic_slice_in_dim(basis_table, start, near, 1)
    reach = lax.dynamic_slice_in_dim(lon_reach, start, near, 0)
    offset = jnp.abs(lax.iota(jnp.int32, tap_count) - tap_count // 2)
    table = jnp.where((offset[None, :] <= reach[:, None])[None, :, None, :], table, jnp.zeros_like(table))
    return jnp.transpose(table, (0, 2, 1, 3))


def rim_kernel(flags, main, near, far, first, second):
    lat_dev, lon_dev, _ = main.shape
    half, side = near.shape[0], first.shape[1]
    for even in (0, 1):
        last = lon_dev - side

        @pl.when(flags[2] == even)
        def _():
            for ref, at in ((first, last if even else 0), (second, 0 if even else last)):
                ref[half : half + lat_dev] = main[:, at : at + side, :]
                for upper in (0, 1):

                    @pl.when(flags[1] == upper)
                    def _():
                        up, down = (far, near) if upper else (near, far)
                        ref[:half] = up[:, at : at + side, :]
                        ref[half + lat_dev :] = down[:, at : at + side, :]


def convolve(band, ext, place, q_ref):
    basis_count, lat_dev, columns, _ = q_ref.shape
    row_span = ext.shape[0] - lat_dev + 1
    for i in range(lat_dev):
        for j in range(columns // BLOCK):
            parts = [ext[(i + row_span - 1 - s,) + place(j)] for s in range(row_span)]
            window = jnp.concatenate(parts + [jnp.zeros_like(parts[0])], axis=0)
            out = jnp.dot(band[i], window, preferred_element_type=f32).astype(bf16)
            for k in range(basis_count):
                q_ref[k, i, j * BLOCK : (j + 1) * BLOCK, :] = out[k * BLOCK : (k + 1) * BLOCK, :]


def build_band(off, taps, band, lines):
    basis_count, row_span, near, tap_count = taps.shape
    lat_dev = band.shape[0]
    wide = 2 * BLOCK
    tap = lax.broadcasted_iota(jnp.int32, (tap_count, 128), 0)
    lane = lax.broadcasted_iota(jnp.int32, (tap_count, 128), 1)
    lines[...] = jnp.zeros_like(lines)
    for s in range(row_span):
        turn = (lane == s % 2 * wide + tap_count - 1 - tap).astype(bf16)
        for k in range(basis_count):
            lines[k, s, 8 : 8 + near, :] = jnp.dot(taps[k, s], turn, preferred_element_type=f32)
    base = off + 8 + row_span - 1
    for k in range(basis_count):
        for p in range((row_span + 1) // 2):
            pair = lines[k, 2 * p, pl.ds(base - 2 * p, lat_dev), :]
            if 2 * p + 1 < row_span:
                pair = pair + lines[k, 2 * p + 1, pl.ds(base - 2 * p - 1, lat_dev), :]
            for i in range(lat_dev):
                line = jnp.broadcast_to(pair[i : i + 1, :], (BLOCK, 128))
                line = pltpu.roll(line, 0, 1, stride=1, stride_axis=0)
                band[i, k * BLOCK : (k + 1) * BLOCK, p * 128 : (p + 1) * 128] = line.astype(bf16)


def cut_fields(f_ref, f_mid, f_edge):
    wide = 2 * BLOCK
    lane = lax.broadcasted_iota(jnp.int32, (1, 128), 1)
    for i in range(0, f_ref.shape[1] // 128, 2):
        even = f_ref[:, i * 128 : (i + 1) * 128].astype(f32)
        odd = f_ref[:, (i + 1) * 128 : (i + 2) * 128].astype(f32)
        back = lambda x: pltpu.roll(x, 128 - BLOCK, 1)
        ahead = lambda x: pltpu.roll(x, BLOCK, 1)
        at = slice(i * wide, (i + 2) * wide)
        f_mid[:, at] = jnp.where(lane < wide, back(even), ahead(odd)).astype(bf16)
        f_edge[:, at] = jnp.where(lane < wide, ahead(even), back(odd)).astype(bf16)


def middle_kernel(flags, taps, f_ref, main, near, far, band, f_edge, q_ref, total, window, lines, f_mid, ext):
    lat_dev, lon_dev, channels = main.shape
    half, side = near.shape[0], BLOCK // 2
    inner = window.shape[2]
    build_band(flags[0], taps, band, lines)
    cut_fields(f_ref, f_mid, f_edge)
    ext[half : half + lat_dev] = main[...]
    for upper in (0, 1):

        @pl.when(flags[1] == upper)
        def _():
            ext[:half] = (far if upper else near)[...]
            ext[half + lat_dev :] = (near if upper else far)[...]

    window[:, 0] = ext[:, lon_dev - inner :, :]
    window[:, 1] = ext[:, :inner, :]
    convolve(band, ext, lambda j: (slice(side + j * BLOCK, side + (j + 2) * BLOCK),), q_ref)
    for k in range(q_ref.shape[0]):
        cells = q_ref[k].reshape(f_mid.shape[1], channels)
        total[k] = jnp.dot(f_mid[...], cells, preferred_element_type=f32)


def edge_kernel(flags, band, window, near, far, f_ref, total, q_ref, low, high, ext):
    channels = window.shape[3]
    side, inner = near.shape[1], window.shape[2]
    ext[:, 0, :inner, :] = window[:, 0]
    ext[:, 1, side:, :] = window[:, 1]
    for even in (0, 1):

        @pl.when(flags[2] == even)
        def _():
            ext[:, 0, inner:, :] = (near if even else far)[...]
            ext[:, 1, :side, :] = (far if even else near)[...]

    convolve(band, ext, lambda j: (j,), q_ref)
    for k in range(q_ref.shape[0]):
        cells = q_ref[k].reshape(f_ref.shape[1], channels)
        out = total[k] + jnp.dot(f_ref[...], cells, preferred_element_type=f32)
        low[k] = out[:, : channels // 2]
        high[k] = out[:, channels // 2 :]


def call(kernel, out_shape, operands, scratch=(), scalars=0, flops=10**9, mib=16):
    vmem = pl.BlockSpec(memory_space=pltpu.VMEM)
    smem = pl.BlockSpec(memory_space=pltpu.SMEM)
    return pl.pallas_call(
        kernel,
        out_shape=out_shape,
        in_specs=[smem] * scalars + [vmem] * (len(operands) - scalars),
        out_specs=jax.tree.map(lambda _: vmem, out_shape),
        scratch_shapes=list(scratch),
        compiler_params=pltpu.CompilerParams(vmem_limit_bytes=mib * 1024 * 1024),
        cost_estimate=pl.CostEstimate(flops=flops, bytes_accessed=10**6, transcendentals=0),
    )(*operands)


def mix_kernel(w_ref, mid_ref, edge_ref, out_ref):
    basis_count, lat_dev, columns, channels = mid_ref.shape
    for i in range(0, lat_dev, 2):
        total = jnp.zeros((channels, 4 * columns), f32)
        for k in range(basis_count):
            parts = []
            for row in (i, i + 1):
                parts += [edge_ref[k, row, BLOCK:], mid_ref[k, row], edge_ref[k, row, :BLOCK]]
            total += lax.dot_general(
                w_ref[k], jnp.concatenate(parts, axis=0), (((1,), (1,)), ((), ())), preferred_element_type=f32
            )
        out_ref[:, i * 2 * columns : (i + 2) * 2 * columns] = total.astype(bf16)


def all_to_all(x, axes):
    return lax.all_to_all(x, axes, 0, 0, tiled=True)


def to_all(x, count):
    return jnp.broadcast_to(x[None], (count,) + x.shape)


def reduce_all(low, high, core, scale, beside):
    swap = [(0, 1), (1, 0)]
    basis_count, channels, half = low.shape
    plane = 1
    for axis in PLANE:
        plane *= lax.axis_size(axis)
    depth = lax.axis_size("z")
    keep, send = jnp.where(core == 0, low, high), jnp.where(core == 0, high, low)
    came, beside = lax.optimization_barrier((lax.ppermute(send, "core", swap), beside))
    own = keep + came
    own = own.reshape(plane, -1, half).astype(bf16)
    own = jnp.sum(all_to_all(own, PLANE).astype(f32), axis=0).astype(bf16)
    own = jnp.sum(all_to_all(to_all(own, depth), ("z",)).astype(f32), axis=0)
    own = (own * scale).astype(bf16)
    own = all_to_all(to_all(own, plane), PLANE).reshape(basis_count, channels, half)
    other = lax.ppermute(own, "core", swap)
    low, high = jnp.where(core == 0, own, other), jnp.where(core == 0, other, own)
    return jnp.concatenate([low, high], axis=2).astype(f32), beside


def local(fields, grad_out, weight, basis_table, lon_reach):
    channels, lat_dev, lon_dev = fields.shape
    basis_count, nlat_all, row_span, tap_count = basis_table.shape
    half, side = row_span // 2, tap_count // 2
    near, wide = lat_dev + 2 * half, 2 * BLOCK
    shape = jax.ShapeDtypeStruct
    core = lax.axis_index("core")
    above = lax.axis_index(LAT) * lat_dev - half
    held = min(16, nlat_all)
    start = jnp.clip(above, 0, nlat_all - held)
    upper = core == 0
    even = lax.axis_index(LON) % 2 == 0
    flags = jnp.stack([above - start, upper.astype(jnp.int32), even.astype(jnp.int32)])
    main = jnp.transpose(grad_out, (1, 2, 0))
    last, first = main[lat_dev - half :], main[:half]
    near_lat, far_lat = exchange(jnp.where(upper, last, first), jnp.where(upper, first, last), LAT, False)
    rim = shape((near, side, channels), bf16)
    rims = call(rim_kernel, (rim, rim), (flags, main, near_lat, far_lat), scalars=1, flops=10**6, mib=4)
    near_lon, far_lon = exchange(*rims, LON, True)
    taps = tap_rows(basis_table, lon_reach, start, held)
    q_shape = shape((basis_count, lat_dev, wide, channels), bf16)
    columns = shape((channels, lat_dev * wide), bf16)
    part = shape((basis_count, channels, channels // 2), f32)
    band, f_edge, q_mid, total, window = call(
        middle_kernel,
        (
            shape((lat_dev, basis_count * BLOCK, (row_span + 1) * wide), bf16),
            columns,
            q_shape,
            shape((basis_count, channels, channels), f32),
            shape((near, 2, wide - side, channels), bf16),
        ),
        (flags, taps, fields.reshape(channels, lat_dev * lon_dev), main, near_lat, far_lat),
        [
            pltpu.VMEM((basis_count, row_span, held + 16, 128), f32),
            pltpu.VMEM(columns.shape, bf16),
            pltpu.VMEM((near, lon_dev, channels), bf16),
        ],
        scalars=1,
    )
    q_edge, low, high = call(
        edge_kernel,
        (q_shape, part, part),
        (flags, band, window, near_lon, far_lon, f_edge, total),
        [pltpu.VMEM((near, 2, wide, channels), bf16)],
        scalars=1,
    )
    mixed = call(mix_kernel, shape((channels, lat_dev * lon_dev), bf16), (weight, q_mid, q_edge))
    field_grad = mixed.reshape(channels, lat_dev, lon_dev)
    weight_grad, field_grad = reduce_all(low, high, core, 1.0 / nlat_all, field_grad)
    return field_grad, weight_grad


def solution(mesh):
    fine = Mesh(mesh.devices.reshape(4, 2, 2, 8, 2), ("y", "x_lo", "core", "z", "x_hi"))
    split = P(None, LAT, LON)
    return jax.shard_map(
        local,
        mesh=fine,
        in_specs=(split, split, P(), P(), P()),
        out_specs=(split, P()),
        check_vma=False,
    )
```

time: 88.9 us -> 85.2 us (0.958)
  local copies, waits for them, and re-layouts: 9.38 us -> 4.33 us
  blocking collectives: 43 us -> 45.5 us
  other arithmetic: 4.09 us -> 2.36 us
  Pallas kernels: 7.02 us -> 8.69 us
    unnamed x30 -> x12, local copies, waits for them, and re-layouts: 8.96 us -> 3.91 us
    all_to_all x3, blocking collectives: 43 us -> 45.5 us  [all_to_all(): return lax.all_to_all(x, axes, 0, 0, tiled=True)]
    select_n x4 -> x1, other arithmetic: 1.83 us -> 0.03 us  [local(): jnp.where(upper, first, last)]
    pallas_call x5 -> x4, Pallas kernels: 7.02 us -> 8.69 us  [call(): pl.pallas_call(kernel, out_shape=out_shape, in_specs=[smem] * scalars + [...]
  transfers between devices with their start and end apart: 6 -> 6, of which waited for: 2 -> 2; matrix products, arithmetic and copies ran while one was open for 3% -> 2% of each run, Pallas kernels for 5% -> 6%
where the time goes in v6:
time: 85.2 us; the launch traced here: 85 us
  blocking collectives  45.5 us (53%)
  starting transfers between devices  18.2 us (21%)
  Pallas kernels  8.69 us (10%)
  waiting for transfers between devices  5 us (6%)
  local copies, waits for them, and re-layouts  4.33 us (5%)
  other arithmetic  2.36 us (3%)
  between operations  0.88 us (1%)
    all_to_all x3, blocking collectives, all_to_all(): return lax.all_to_all(x, axes, 0, 0, tiled=True)  45.5 us
    ppermute x4, starting transfers between devices, exchange(): return (lax.ppermute(first, axes, near), lax.ppermute(second, axes, far))  13 us
    pallas_call x4, Pallas kernels, call(): pl.pallas_call(kernel, out_shape=out_shape, in_specs=[smem] * scalars + [...  8.69 us
    ppermute x1, starting transfers between devices, reduce_all(): other = lax.ppermute(own, 'core', swap)  5.17 us
    unnamed x12, local copies, waits for them, and re-layouts  3.91 us
    ppermute x4, waiting for transfers between devices, exchange(): return (lax.ppermute(first, axes, near), lax.ppermute(second, axes, far))  3.37 us
  transfers between devices with their start and end apart: 6, of which 2 were waited for; matrix products, arithmetic and copies ran while one was open for 2% of the time, Pallas kernels for 6%

profile of v6, /device:TPU:1, one launch (start us, length us, event | category | flops | bytes accessed | tf_op | source)
XLA Modules:
  0.0 85.0 jit_solution(10752461386024330576)
XLA Ops:
  0.6 0.0 copy-start
  0.6 0.0 copy-start.3
  0.7 1.4 %copy.10 = bf16[256,8,128]{0,2,1:T(8,128)(2,1)S(1)} copy(bf16[256,8,128]{2,1,0:T(8,128)(2,1)} %param.6) | data formatting | bytes 1048576 | tf_op args[1]
  2.1 4.5 %collective-permute-start.1 = (bf16[3,128,256]{2,1,0:T(8,128)(2,1)S(1)}, bf16[3,128,256]{2,1,0:T(8,128)(2,1)S(1)}, u32[]{:S(2)}, u32[]{:S(2)}) collective-permute-start(bf16[3,128,256]{2,1,0:T(8,128)(2,1)S(1)} %get-tuple-element.28), channel_id=1, source_target_pairs={{16,32},{32,16},{48,64},{64,48},{80,96},{96,80},{112,128},{128,112... | collective-permute-start | bytes 589832 | tf_op jit(solution)/shard_map/ppermute | solution.py:23
  6.6 0.1 collective-permute-start
  6.8 0.0 copy-done.3
  6.8 0.1 dynamic_slice.6
  6.8 0.0 copy-done
  6.8 0.2 constant_dynamic-slice_fusion
  7.1 0.0 copy-start.2
  7.1 0.5 copy.11
  7.6 0.1 pad_add_fusion.flags
  7.7 0.1 broadcast_compare_fusion
  7.7 3.4 %collective-permute-done.1.far = bf16[3,128,256]{2,1,0:T(8,128)(2,1)S(1)} collective-permute-done((bf16[3,128,256]{2,1,0:T(8,128)(2,1)S(1)}, bf16[3,128,256]{2,1,0:T(8,128)(2,1)S(1)}, u32[]{:S(2)}, u32[]{:S(2)}) %collective-permute-start.1) | collective-permute-done | bytes 196640 | tf_op jit(solution)/shard_map/ppermute | solution.py:23
  11.1 0.0 collective-permute-done.near
  11.1 0.6 shard_map.69
  11.7 2.7 %collective-permute-start.2 = (bf16[14,16,256]{2,1,0:T(8,128)(2,1)S(1)}, bf16[14,16,256]{2,1,0:T(8,128)(2,1)S(1)}, u32[]{:S(2)}, u32[]{:S(2)}) collective-permute-start(bf16[14,16,256]{2,1,0:T(8,128)(2,1)S(1)} %get-tuple-element.16), channel_id=1, source_target_pairs={{0,1},{1,0},{2,3},{3,2},{4,5},{5,4},{6,7},{7,6},{8,9},{9,8},{10,11... | collective-permute-start | bytes 344072 | tf_op jit(solution)/shard_map/ppermute | solution.py:23
  14.4 5.6 %collective-permute-start.3 = (bf16[14,16,256]{2,1,0:T(8,128)(2,1)S(1)}, bf16[14,16,256]{2,1,0:T(8,128)(2,1)S(1)}, u32[]{:S(2)}, u32[]{:S(2)}) collective-permute-start(bf16[14,16,256]{2,1,0:T(8,128)(2,1)S(1)} %get-tuple-element.17), channel_id=1, source_target_pairs={{0,15},{1,2},{2,1},{3,4},{4,3},{5,6},{6,5},{7,8},{8,7},{9,10},{10,... | collective-permute-start | bytes 344072 | tf_op jit(solution)/shard_map/ppermute | solution.py:23
  20.1 0.0 copy-done.2
  20.1 0.1 copy.15
  20.2 3.9 %shard_map.68 = (bf16[8,288,512]{2,1,0:T(8,128)(2,1)S(1)}, bf16[256,512]{1,0:T(8,128)(2,1)S(1)}, bf16[9,8,64,256]{3,2,1,0:T(8,128)(2,1)S(1)}, f32[9,256,256]{2,1,0:T(8,128)S(1)}, bf16[14,2,48,256]{3,2,1,0:T(8,128)(2,1)S(1)}) custom-call(s32[3]{0:T(128)S(1)} %pad_add_fusion.flags, bf16[9,7,16,33]{3,2,1,0:T(8,128)(2,1)S(1)} %select_bitcast_fusion.taps, ...), custom_call_target="tpu_custom_call" | custom-call | flops 1000000000 | bytes 1000000 | tf_op jit(solution)/shard_map/pallas_call | solution.py:147
  24.1 0.0 collective-permute-done.2.near
  24.1 0.0 collective-permute-done.3.far
  24.1 2.8 %shard_map.70 = (bf16[9,8,64,256]{3,2,1,0:T(8,128)(2,1)S(1)}, f32[9,256,128]{2,1,0:T(8,128)S(1)}, f32[9,256,128]{2,1,0:T(8,128)S(1)}) custom-call(s32[3]{0:T(128)S(1)} %pad_add_fusion.flags, bf16[8,288,512]{2,1,0:T(8,128)(2,1)S(1)} %get-tuple-element.14.band, bf16[14,2,48,256]{3,2,1,0:T(8,128)(2,1)S(1)} %get-tuple-element.15.window, ...), custom_call_target="tpu_custom_call" | custom-call | flops 1000000000 | bytes 1000000 | tf_op jit(solution)/shard_map/pallas_call | solution.py:147
  26.9 0.0 copy-start.1
  26.9 0.1 broadcast_select_fusion.2
  27.0 0.1 collective-permute-start.4
  27.1 1.0 %copy-done.1 = bf16[9,256,256]{2,1,0:T(8,128)(2,1)S(1)} copy-done((bf16[9,256,256]{2,1,0:T(8,128)(2,1)S(1)}, bf16[9,256,256]{2,1,0:T(8,128)(2,1)}, u32[]{:S(2)}) %copy-start.1) | copy-done | bytes 1179672
  28.2 1.4 %shard_map.71 = bf16[256,1024]{1,0:T(8,128)(2,1)S(1)} custom-call(bf16[9,256,256]{2,1,0:T(8,128)(2,1)S(1)} %copy-done.1, bf16[9,8,64,256]{3,2,1,0:T(8,128)(2,1)S(1)} %get-tuple-element.22.mid_ref, bf16[9,8,64,256]{3,2,1,0:T(8,128)(2,1)S(1)} %get-tuple-element.23.edge_ref), custom_call_target="tpu_custom_call" | custom-call | flops 1000000000 | bytes 1000000 | tf_op jit(solution)/shard_map/pallas_call | solution.py:147
  29.6 0.9 %copy.13 = bf16[32,8,8,128]{3,2,1,0:T(8,128)(2,1)} copy(bf16[32,8,8,128]{3,1,2,0:T(8,128)(2,1)S(1)} %bitcast.17) | data formatting | bytes 1048576
  30.5 0.0 collective-permute-done.4
  30.5 0.2 add_convert_fusion
  30.7 18.0 %all_to_all.15 = bf16[16,144,128]{2,1,0:T(8,128)(2,1)S(1)} all-to-all(bf16[16,144,128]{2,1,0:T(8,128)(2,1)S(1)} %bitcast.19), channel_id=1, replica_groups=mesh['y'=4,'x_lo'=2,'core'=2,'z'=8,'x_hi'=2] {'y','x_hi','x_lo'}, dimensions={0} | all-to-all | bytes 1179648 | tf_op jit(solution)/shard_map/all_to_all | solution.py:173
  48.7 0.1 reduce_sum.21
  48.9 15.3 %all_to_all.16 = bf16[8,144,128]{2,1,0:T(8,128)(2,1)S(1)} all-to-all(bf16[8,144,128]{2,1,0:T(8,128)(2,1)S(1)} %broadcast_in_dim.16), channel_id=1, replica_groups=mesh['y'=4,'x_lo'=2,'core'=2,'z'=8,'x_hi'=2] {'z'}, dimensions={0} | all-to-all | bytes 589824 | tf_op jit(solution)/shard_map/all_to_all | solution.py:173
  64.2 0.1 broadcast_in_dim.17
  64.3 12.2 %all_to_all.17 = bf16[16,144,128]{2,1,0:T(8,128)(2,1)S(1)} all-to-all(bf16[16,144,128]{2,1,0:T(8,128)(2,1)S(1)} %broadcast_in_dim.17), channel_id=1, replica_groups=mesh['y'=4,'x_lo'=2,'core'=2,'z'=8,'x_hi'=2] {'y','x_hi','x_lo'}, dimensions={0} | all-to-all | bytes 1179648 | tf_op jit(solution)/shard_map/all_to_all | solution.py:173
  76.5 5.2 %collective-permute-start.5 = (bf16[9,256,128]{2,1,0:T(8,128)(2,1)S(1)}, bf16[9,256,128]{2,1,0:T(8,128)(2,1)S(1)}, u32[]{:S(2)}, u32[]{:S(2)}) collective-permute-start(bf16[9,256,128]{2,1,0:T(8,128)(2,1)S(1)} %bitcast.20), channel_id=1, source_target_pairs={{0,16},{16,0},{1,17},{17,1},{2,18},{18,2},{3,19},{19,3},{4,20},{20... | collective-permute-start | bytes 1769480 | tf_op jit(solution)/shard_map/ppermute | solution.py:195
  81.7 1.6 %collective-permute-done.5 = bf16[9,256,128]{2,1,0:T(8,128)(2,1)S(1)} collective-permute-done((bf16[9,256,128]{2,1,0:T(8,128)(2,1)S(1)}, bf16[9,256,128]{2,1,0:T(8,128)(2,1)S(1)}, u32[]{:S(2)}, u32[]{:S(2)}) %collective-permute-start.5) | collective-permute-done | bytes 589856 | tf_op jit(solution)/shard_map/ppermute | solution.py:195
  83.3 0.1 broadcast_select_fusion.1
  83.4 1.6 %maximum_convert_fusion = f32[9,256,256]{2,1,0:T(8,128)} fusion(bf16[9,256,128]{2,1,0:T(8,128)(2,1)S(1)} %get-tuple-element.27, bf16[9,256,128]{2,1,0:T(8,128)(2,1)S(1)} %get-tuple-element.26), kind=kLoop, calls=%fused_computation | loop fusion | flops 2359296 | bytes 3538944 | tf_op jit(solution)/shard_map/convert_element_type | solution.py:197
  (6 shorter events, 0.1 us)
Async XLA Ops:
  0.6 6.2 %copy-start = (bf16[9,128,7,33]{1,2,3,0:T(8,128)(2,1)S(1)}, bf16[9,128,7,33]{1,2,3,0:T(8,128)(2,1)}, u32[]{:S(2)}) copy-start(bf16[9,128,7,33]{1,2,3,0:T(8,128)(2,1)} %param.8) | copy-start | bytes 1596676
  0.6 6.1 %copy-start.3 = (s32[128]{0:T(128)S(1)}, s32[128]{0:T(128)}, u32[]{:S(2)}) copy-start(s32[128]{0:T(128)} %param.9) | copy-start | bytes 1540
  2.1 9.0 %collective-permute-start.1 = (bf16[3,128,256]{2,1,0:T(8,128)(2,1)S(1)}, bf16[3,128,256]{2,1,0:T(8,128)(2,1)S(1)}, u32[]{:S(2)}, u32[]{:S(2)}) collective-permute-start(bf16[3,128,256]{2,1,0:T(8,128)(2,1)S(1)} %get-tuple-element.28), channel_id=1, source_target_pairs={{16,32},{32,16},{48,64},{64,48},{80,96},{96,80},{112,128},{128,112... | collective-permute-start | bytes 589832 | tf_op jit(solution)/shard_map/ppermute | solution.py:23
  6.6 4.5 %collective-permute-start = (bf16[3,128,256]{2,1,0:T(8,128)(2,1)S(1)}, bf16[3,128,256]{2,1,0:T(8,128)(2,1)S(1)}, u32[]{:S(2)}, u32[]{:S(2)}) collective-permute-start(bf16[3,128,256]{2,1,0:T(8,128)(2,1)S(1)} %get-tuple-element.29), channel_id=1, source_target_pairs={{0,16},{16,0},{32,48},{48,32},{64,80},{80,64},{96,112},{112,96},{1... | collective-permute-start | bytes 589832 | tf_op jit(solution)/shard_map/ppermute | solution.py:23
  7.1 13.0 %copy-start.2 = (bf16[256,8,128]{2,1,0:T(8,128)(2,1)S(1)}, bf16[256,8,128]{2,1,0:T(8,128)(2,1)}, u32[]{:S(2)}) copy-start(bf16[256,8,128]{2,1,0:T(8,128)(2,1)} %param.5) | copy-start | bytes 1572868
  11.7 12.4 %collective-permute-start.2 = (bf16[14,16,256]{2,1,0:T(8,128)(2,1)S(1)}, bf16[14,16,256]{2,1,0:T(8,128)(2,1)S(1)}, u32[]{:S(2)}, u32[]{:S(2)}) collective-permute-start(bf16[14,16,256]{2,1,0:T(8,128)(2,1)S(1)} %get-tuple-element.16), channel_id=1, source_target_pairs={{0,1},{1,0},{2,3},{3,2},{4,5},{5,4},{6,7},{7,6},{8,9},{9,8},{10,11... | collective-permute-start | bytes 344072 | tf_op jit(solution)/shard_map/ppermute | solution.py:23
  14.4 9.7 %collective-permute-start.3 = (bf16[14,16,256]{2,1,0:T(8,128)(2,1)S(1)}, bf16[14,16,256]{2,1,0:T(8,128)(2,1)S(1)}, u32[]{:S(2)}, u32[]{:S(2)}) collective-permute-start(bf16[14,16,256]{2,1,0:T(8,128)(2,1)S(1)} %get-tuple-element.17), channel_id=1, source_target_pairs={{0,15},{1,2},{2,1},{3,4},{4,3},{5,6},{6,5},{7,8},{8,7},{9,10},{10,... | collective-permute-start | bytes 344072 | tf_op jit(solution)/shard_map/ppermute | solution.py:23
  26.9 1.3 %copy-start.1 = (bf16[9,256,256]{2,1,0:T(8,128)(2,1)S(1)}, bf16[9,256,256]{2,1,0:T(8,128)(2,1)}, u32[]{:S(2)}) copy-start(bf16[9,256,256]{2,1,0:T(8,128)(2,1)} %w_ref.1) | copy-start | bytes 3538948
  27.0 3.4 %collective-permute-start.4 = (f32[9,256,128]{2,1,0:T(8,128)S(1)}, f32[9,256,128]{2,1,0:T(8,128)S(1)}, u32[]{:S(2)}, u32[]{:S(2)}) collective-permute-start(f32[9,256,128]{2,1,0:T(8,128)S(1)} %broadcast_select_fusion.2), channel_id=1, source_target_pairs={{0,16},{16,0},{1,17},{17,1},{2,18},{18,2},{3,19},{19,3},{4,20},{20... | collective-permute-start | bytes 3538952 | tf_op jit(solution)/shard_map/ppermute | solution.py:188
  76.5 6.8 %collective-permute-start.5 = (bf16[9,256,128]{2,1,0:T(8,128)(2,1)S(1)}, bf16[9,256,128]{2,1,0:T(8,128)(2,1)S(1)}, u32[]{:S(2)}, u32[]{:S(2)}) collective-permute-start(bf16[9,256,128]{2,1,0:T(8,128)(2,1)S(1)} %bitcast.20), channel_id=1, source_target_pairs={{0,16},{16,0},{1,17},{17,1},{2,18},{18,2},{3,19},{19,3},{4,20},{20... | collective-permute-start | bytes 1769480 | tf_op jit(solution)/shard_map/ppermute | solution.py:195

commit v7 on v6

--- a/solution.py
+++ b/solution.py
@@ -1,3 +1,5 @@
+import functools
+
 import jax
 import jax.numpy as jnp
 from jax import lax
@@ -23,6 +25,16 @@
     return lax.ppermute(first, axes, near), lax.ppermute(second, axes, far)
 
 
+def parity(axes):
+    return lax.rem(lax.axis_index(axes[-1]), 2)
+
+
+def held_rows(lat_dev, half, nlat_all):
+    above = lax.axis_index(LAT) * lat_dev - half
+    held = min(16, nlat_all)
+    return above, jnp.clip(above, 0, nlat_all - held), held
+
+
 def tap_rows(basis_table, lon_reach, start, near):
     tap_count = basis_table.shape[3]
     table = lax.dynamic_slice_in_dim(basis_table, start, near, 1)
@@ -32,19 +44,20 @@
     return jnp.transpose(table, (0, 2, 1, 3))
 
 
-def rim_kernel(flags, main, near, far, first, second):
+def rim_kernel(main, near, far, first, second):
     lat_dev, lon_dev, _ = main.shape
     half, side = near.shape[0], first.shape[1]
+    odd_lon, odd_lat = parity(LON), parity(LAT)
     for even in (0, 1):
         last = lon_dev - side
 
-        @pl.when(flags[2] == even)
+        @pl.when(odd_lon != even)
         def _():
             for ref, at in ((first, last if even else 0), (second, 0 if even else last)):
                 ref[half : half + lat_dev] = main[:, at : at + side, :]
                 for upper in (0, 1):
 
-                    @pl.when(flags[1] == upper)
+                    @pl.when(odd_lat != upper)
                     def _():
                         up, down = (far, near) if upper else (near, far)
                         ref[:half] = up[:, at : at + side, :]
@@ -99,16 +112,18 @@
         f_edge[:, at] = jnp.where(lane < wide, ahead(even), back(odd)).astype(bf16)
 
 
-def middle_kernel(flags, taps, f_ref, main, near, far, band, f_edge, q_ref, total, window, lines, f_mid, ext):
+def middle_kernel(nlat_all, taps, f_ref, main, near, far, band, f_edge, q_ref, total, window, lines, f_mid, ext):
     lat_dev, lon_dev, channels = main.shape
     half, side = near.shape[0], BLOCK // 2
     inner = window.shape[2]
-    build_band(flags[0], taps, band, lines)
+    above, start, _ = held_rows(lat_dev, half, nlat_all)
+    build_band(above - start, taps, band, lines)
     cut_fields(f_ref, f_mid, f_edge)
     ext[half : half + lat_dev] = main[...]
+    odd_lat = parity(LAT)
     for upper in (0, 1):
 
-        @pl.when(flags[1] == upper)
+        @pl.when(odd_lat != upper)
         def _():
             ext[:half] = (far if upper else near)[...]
             ext[half + lat_dev :] = (near if upper else far)[...]
@@ -121,14 +136,17 @@
         total[k] = jnp.dot(f_mid[...], cells, preferred_element_type=f32)
 
 
-def edge_kernel(flags, band, window, near, far, f_ref, total, q_ref, low, high, ext):
+def edge_kernel(band, window, near, far, f_ref, total, w_ref, q_ref, low, high, w_out, ext, sem):
+    fetch = pltpu.make_async_copy(w_ref, w_out, sem)
+    fetch.start()
     channels = window.shape[3]
     side, inner = near.shape[1], window.shape[2]
     ext[:, 0, :inner, :] = window[:, 0]
     ext[:, 1, side:, :] = window[:, 1]
+    odd_lon = parity(LON)
     for even in (0, 1):
 
-        @pl.when(flags[2] == even)
+        @pl.when(odd_lon != even)
         def _():
             ext[:, 0, inner:, :] = (near if even else far)[...]
             ext[:, 1, :side, :] = (far if even else near)[...]
@@ -139,15 +157,15 @@
         out = total[k] + jnp.dot(f_ref[...], cells, preferred_element_type=f32)
         low[k] = out[:, : channels // 2]
         high[k] = out[:, channels // 2 :]
-
-
-def call(kernel, out_shape, operands, scratch=(), scalars=0, flops=10**9, mib=16):
+    fetch.wait()
+
+
+def call(kernel, out_shape, operands, scratch=(), hbm=0, flops=10**9, mib=16):
     vmem = pl.BlockSpec(memory_space=pltpu.VMEM)
-    smem = pl.BlockSpec(memory_space=pltpu.SMEM)
     return pl.pallas_call(
         kernel,
         out_shape=out_shape,
-        in_specs=[smem] * scalars + [vmem] * (len(operands) - scalars),
+        in_specs=[vmem] * (len(operands) - hbm) + [pl.BlockSpec(memory_space=pl.ANY)] * hbm,
         out_specs=jax.tree.map(lambda _: vmem, out_shape),
         scratch_shapes=list(scratch),
         compiler_params=pltpu.CompilerParams(vmem_limit_bytes=mib * 1024 * 1024),
@@ -169,6 +187,39 @@
         out_ref[:, i * 2 * columns : (i + 2) * 2 * columns] = total.astype(bf16)
 
 
+def place_kernel(own, half_ref, *refs):
+    out, wide, sems = refs[-3:]
+    basis_count, _, columns = half_ref.shape
+    at = lax.axis_index("core") if own else 1 - lax.axis_index("core")
+    at = pl.ds(pl.multiple_of(at * columns, columns), columns)
+    parts = sems.shape[0]
+    size = basis_count // parts
+    copies = []
+    for part in range(parts):
+        rows = slice(part * size, (part + 1) * size)
+        wide[rows] = half_ref[rows].astype(f32)
+        copies.append(pltpu.make_async_copy(wide.at[rows], out.at[rows, :, at], sems.at[part]))
+        copies[-1].start()
+    for copy in copies:
+        copy.wait()
+
+
+def place(half, own, into=None):
+    basis_count, channels, columns = half.shape
+    hbm = pl.BlockSpec(memory_space=pl.ANY)
+    operands = (half,) if into is None else (half, into)
+    return pl.pallas_call(
+        functools.partial(place_kernel, own),
+        out_shape=jax.ShapeDtypeStruct((basis_count, channels, 2 * columns), f32),
+        in_specs=[pl.BlockSpec(memory_space=pltpu.VMEM)] + [hbm] * (len(operands) - 1),
+        out_specs=hbm,
+        scratch_shapes=[pltpu.VMEM(half.shape, f32), pltpu.SemaphoreType.DMA((3,))],
+        input_output_aliases={} if into is None else {1: 0},
+        compiler_params=pltpu.CompilerParams(vmem_limit_bytes=4 * 1024 * 1024),
+        cost_estimate=pl.CostEstimate(flops=10**6, bytes_accessed=10**6, transcendentals=0),
+    )(*operands)
+
+
 def all_to_all(x, axes):
     return lax.all_to_all(x, axes, 0, 0, tiled=True)
 
@@ -177,7 +228,7 @@
     return jnp.broadcast_to(x[None], (count,) + x.shape)
 
 
-def reduce_all(low, high, core, scale, beside):
+def reduce_all(low, high, core, scale, beside, finish):
     swap = [(0, 1), (1, 0)]
     basis_count, channels, half = low.shape
     plane = 1
@@ -192,9 +243,9 @@
     own = jnp.sum(all_to_all(to_all(own, depth), ("z",)).astype(f32), axis=0)
     own = (own * scale).astype(bf16)
     own = all_to_all(to_all(own, plane), PLANE).reshape(basis_count, channels, half)
-    other = lax.ppermute(own, "core", swap)
-    low, high = jnp.where(core == 0, own, other), jnp.where(core == 0, other, own)
-    return jnp.concatenate([low, high], axis=2).astype(f32), beside
+    beside = finish(beside)
+    other, summed, beside = lax.optimization_barrier((lax.ppermute(own, "core", swap), place(own, True), beside))
+    return place(other, False, summed), beside
 
 
 def local(fields, grad_out, weight, basis_table, lon_reach):
@@ -204,24 +255,20 @@
     near, wide = lat_dev + 2 * half, 2 * BLOCK
     shape = jax.ShapeDtypeStruct
     core = lax.axis_index("core")
-    above = lax.axis_index(LAT) * lat_dev - half
-    held = min(16, nlat_all)
-    start = jnp.clip(above, 0, nlat_all - held)
+    _, start, held = held_rows(lat_dev, half, nlat_all)
     upper = core == 0
-    even = lax.axis_index(LON) % 2 == 0
-    flags = jnp.stack([above - start, upper.astype(jnp.int32), even.astype(jnp.int32)])
     main = jnp.transpose(grad_out, (1, 2, 0))
     last, first = main[lat_dev - half :], main[:half]
     near_lat, far_lat = exchange(jnp.where(upper, last, first), jnp.where(upper, first, last), LAT, False)
     rim = shape((near, side, channels), bf16)
-    rims = call(rim_kernel, (rim, rim), (flags, main, near_lat, far_lat), scalars=1, flops=10**6, mib=4)
+    rims = call(rim_kernel, (rim, rim), (main, near_lat, far_lat), flops=10**6, mib=4)
     near_lon, far_lon = exchange(*rims, LON, True)
     taps = tap_rows(basis_table, lon_reach, start, held)
     q_shape = shape((basis_count, lat_dev, wide, channels), bf16)
     columns = shape((channels, lat_dev * wide), bf16)
     part = shape((basis_count, channels, channels // 2), f32)
     band, f_edge, q_mid, total, window = call(
-        middle_kernel,
+        functools.partial(middle_kernel, nlat_all),
         (
             shape((lat_dev, basis_count * BLOCK, (row_span + 1) * wide), bf16),
             columns,
@@ -229,24 +276,24 @@
             shape((basis_count, channels, channels), f32),
             shape((near, 2, wide - side, channels), bf16),
         ),
-        (flags, taps, fields.reshape(channels, lat_dev * lon_dev), main, near_lat, far_lat),
+        (taps, fields.reshape(channels, lat_dev * lon_dev), main, near_lat, far_lat),
         [
             pltpu.VMEM((basis_count, row_span, held + 16, 128), f32),
             pltpu.VMEM(columns.shape, bf16),
             pltpu.VMEM((near, lon_dev, channels), bf16),
         ],
-        scalars=1,
     )
-    q_edge, low, high = call(
+    q_edge, low, high, weight = call(
         edge_kernel,
-        (q_shape, part, part),
-        (flags, band, window, near_lon, far_lon, f_edge, total),
-        [pltpu.VMEM((near, 2, wide, channels), bf16)],
-        scalars=1,
+        (q_shape, part, part, shape(weight.shape, bf16)),
+        (band, window, near_lon, far_lon, f_edge, total, weight),
+        [pltpu.VMEM((near, 2, wide, channels), bf16), pltpu.SemaphoreType.DMA],
+        hbm=1,
     )
     mixed = call(mix_kernel, shape((channels, lat_dev * lon_dev), bf16), (weight, q_mid, q_edge))
-    field_grad = mixed.reshape(channels, lat_dev, lon_dev)
-    weight_grad, field_grad = reduce_all(low, high, core, 1.0 / nlat_all, field_grad)
+    weight_grad, field_grad = reduce_all(
+        low, high, core, 1.0 / nlat_all, mixed, lambda x: x.reshape(channels, lat_dev, lon_dev)
+    )
     return field_grad, weight_grad
 
 

time: 85.2 us -> 84.8 us (level)
  blocking collectives: 45.5 us -> 47.7 us
  other arithmetic: 2.36 us -> 0.62 us
  local copies, waits for them, and re-layouts: 4.33 us -> 3.31 us
    all_to_all x3, blocking collectives: 45.5 us -> 47.7 us  [all_to_all(): return lax.all_to_all(x, axes, 0, 0, tiled=True)]
    ppermute x1, waiting for transfers between devices: 1.63 us -> 0.01 us  [reduce_all(): lax.ppermute(own, 'core', swap)]
    convert_element_type x1 -> x0, other arithmetic: 1.57 us -> none  [reduce_all(): return (jnp.concatenate([low, high], axis=2).astype(f32), beside)]
    ppermute x1, waiting for transfers between devices: 0.01 us -> 1.42 us  [reduce_all(): lax.ppermute(send, 'core', swap)]
    unnamed x12, local copies, waits for them, and re-layouts: 3.91 us -> 2.88 us
    pallas_call x4 -> x6, Pallas kernels: 8.69 us -> 9.46 us  [the longest x4 7.34 us: call(): pl.pallas_call(kernel, out_shape=out_shape, in_specs=[vmem] * (len(operan...]
  transfers between devices with their start and end apart: 6 -> 6, of which waited for: 2 -> 2; matrix products, arithmetic and copies ran while one was open for 2% -> 2% of each run, Pallas kernels for 6% -> 7%
where the time goes in v7:
time: 84.8 us; the launch traced here: 84.6 us
  blocking collectives  47.7 us (56%)
  starting transfers between devices  17.7 us (21%)
  Pallas kernels  9.46 us (11%)
  waiting for transfers between devices  4.88 us (6%)
  local copies, waits for them, and re-layouts  3.31 us (4%)
  between operations  0.88 us (1%)
    all_to_all x3, blocking collectives, all_to_all(): return lax.all_to_all(x, axes, 0, 0, tiled=True)  47.7 us
    ppermute x4, starting transfers between devices, exchange(): return (lax.ppermute(first, axes, near), lax.ppermute(second, axes, far))  13 us
    pallas_call x4, Pallas kernels, call(): pl.pallas_call(kernel, out_shape=out_shape, in_specs=[vmem] * (len(operan...  7.34 us
    ppermute x1, starting transfers between devices, reduce_all(): lax.ppermute(own, 'core', swap)  4.68 us
    ppermute x4, waiting for transfers between devices, exchange(): return (lax.ppermute(first, axes, near), lax.ppermute(second, axes, far))  3.46 us
    unnamed x12, local copies, waits for them, and re-layouts  2.88 us
    pallas_call x2, Pallas kernels, place(): pl.pallas_call(functools.partial(place_kernel, own), out_shape=jax.ShapeD...  2.12 us
  transfers between devices with their start and end apart: 6, of which 2 were waited for; matrix products, arithmetic and copies ran while one was open for 2% of the time, Pallas kernels for 7%

profile of v7, /device:TPU:1, one launch (start us, length us, event | category | flops | bytes accessed | tf_op | source)
XLA Modules:
  0.0 84.6 jit_solution(16244812651330389667)
XLA Ops:
  0.6 0.0 copy-start
  0.6 0.0 copy-start.3
  0.7 1.4 %copy.11 = bf16[256,8,128]{0,2,1:T(8,128)(2,1)S(1)} copy(bf16[256,8,128]{2,1,0:T(8,128)(2,1)} %param.6) | data formatting | bytes 1048576 | tf_op args[1]
  2.1 4.5 %collective-permute-start.1 = (bf16[3,128,256]{2,1,0:T(8,128)(2,1)S(1)}, bf16[3,128,256]{2,1,0:T(8,128)(2,1)S(1)}, u32[]{:S(2)}, u32[]{:S(2)}) collective-permute-start(bf16[3,128,256]{2,1,0:T(8,128)(2,1)S(1)} %get-tuple-element.34), channel_id=1, source_target_pairs={{16,32},{32,16},{48,64},{64,48},{80,96},{96,80},{112,128},{128,112... | collective-permute-start | bytes 589832 | tf_op jit(solution)/shard_map/ppermute | solution.py:25
  6.6 0.1 collective-permute-start
  6.7 0.0 copy-done.3
  6.7 0.1 dynamic_slice.6
  6.8 0.0 copy-done
  6.8 0.2 constant_dynamic-slice_fusion
  7.1 0.0 copy-start.2
  7.1 0.5 copy.12
  7.6 0.1 broadcast_compare_fusion
  7.6 3.5 %collective-permute-done.1.far = bf16[3,128,256]{2,1,0:T(8,128)(2,1)S(1)} collective-permute-done((bf16[3,128,256]{2,1,0:T(8,128)(2,1)S(1)}, bf16[3,128,256]{2,1,0:T(8,128)(2,1)S(1)}, u32[]{:S(2)}, u32[]{:S(2)}) %collective-permute-start.1) | collective-permute-done | bytes 196640 | tf_op jit(solution)/shard_map/ppermute | solution.py:25
  11.1 0.0 collective-permute-done.near
  11.1 2.8 %collective-permute-start.2 = (bf16[14,16,256]{2,1,0:T(8,128)(2,1)S(1)}, bf16[14,16,256]{2,1,0:T(8,128)(2,1)S(1)}, u32[]{:S(2)}, u32[]{:S(2)}) collective-permute-start(bf16[14,16,256]{2,1,0:T(8,128)(2,1)S(1)} %get-tuple-element.20), channel_id=1, source_target_pairs={{0,1},{1,0},{2,3},{3,2},{4,5},{5,4},{6,7},{7,6},{8,9},{9,8},{10,11... | collective-permute-start | bytes 344072 | tf_op jit(solution)/shard_map/ppermute | solution.py:25
  13.9 5.6 %collective-permute-start.3 = (bf16[14,16,256]{2,1,0:T(8,128)(2,1)S(1)}, bf16[14,16,256]{2,1,0:T(8,128)(2,1)S(1)}, u32[]{:S(2)}, u32[]{:S(2)}) collective-permute-start(bf16[14,16,256]{2,1,0:T(8,128)(2,1)S(1)} %get-tuple-element.21), channel_id=1, source_target_pairs={{0,15},{1,2},{2,1},{3,4},{4,3},{5,6},{6,5},{7,8},{8,7},{9,10},{10,... | collective-permute-start | bytes 344072 | tf_op jit(solution)/shard_map/ppermute | solution.py:25
  19.5 0.0 copy-done.2
  19.5 0.1 copy.16
  19.6 0.0 copy-start.1
  19.6 3.4 %shard_map.68 = (bf16[8,288,512]{2,1,0:T(8,128)(2,1)S(1)}, bf16[256,512]{1,0:T(8,128)(2,1)S(1)}, bf16[9,8,64,256]{3,2,1,0:T(8,128)(2,1)S(1)}, f32[9,256,256]{2,1,0:T(8,128)S(1)}, bf16[14,2,48,256]{3,2,1,0:T(8,128)(2,1)S(1)}) custom-call(bf16[9,7,16,33]{3,2,1,0:T(8,128)(2,1)S(1)} %select_bitcast_fusion.taps, bf16[256,1024]{1,0:T(8,128)(2,1)S(1)} %bitcast.17, ...), custom_call_target="tpu_custom_call" | custom-call | flops 1000000000 | bytes 1000000 | tf_op jit(solution)/shard_map/pallas_call | solution.py:165
  23.1 0.0 collective-permute-done.2.near
  23.1 0.0 collective-permute-done.3.far
  23.1 0.0 copy-done.1
  23.1 2.5 %shard_map.70 = (bf16[9,8,64,256]{3,2,1,0:T(8,128)(2,1)S(1)}, f32[9,256,128]{2,1,0:T(8,128)S(1)}, f32[9,256,128]{2,1,0:T(8,128)S(1)}, bf16[9,256,256]{2,1,0:T(8,128)(2,1)S(1)}) custom-call(bf16[8,288,512]{2,1,0:T(8,128)(2,1)S(1)} %get-tuple-element.18.band, bf16[14,2,48,256]{3,2,1,0:T(8,128)(2,1)S(1)} %get-tuple-element.19.window, ...), custom_call_target="tpu_custom_call" | custom-call | flops 1000000000 | bytes 1000000 | tf_op jit(solution)/shard_map/pallas_call | solution.py:165
  25.6 0.1 broadcast_select_fusion
  25.7 0.1 collective-permute-start.4
  25.8 1.4 %shard_map.71 = bf16[256,1024]{1,0:T(8,128)(2,1)S(1)} custom-call(bf16[9,256,256]{2,1,0:T(8,128)(2,1)S(1)} %get-tuple-element.26.w_ref, bf16[9,8,64,256]{3,2,1,0:T(8,128)(2,1)S(1)} %get-tuple-element.27.mid_ref, bf16[9,8,64,256]{3,2,1,0:T(8,128)(2,1)S(1)} %get-tuple-element.28.edge_ref), custom_call_target="tpu_custom_call" | custom-call | flops 1000000000 | bytes 1000000 | tf_op jit(solution)/shard_map/pallas_call | solution.py:165
  27.2 1.4 %collective-permute-done.4 = f32[9,256,128]{2,1,0:T(8,128)S(1)} collective-permute-done((f32[9,256,128]{2,1,0:T(8,128)S(1)}, f32[9,256,128]{2,1,0:T(8,128)S(1)}, u32[]{:S(2)}, u32[]{:S(2)}) %collective-permute-start.4) | collective-permute-done | bytes 1179680 | tf_op jit(solution)/shard_map/ppermute | solution.py:239
  28.6 0.2 add_convert_fusion
  28.9 18.2 %all_to_all.15 = bf16[16,144,128]{2,1,0:T(8,128)(2,1)S(1)} all-to-all(bf16[16,144,128]{2,1,0:T(8,128)(2,1)S(1)} %bitcast.18), channel_id=1, replica_groups=mesh['y'=4,'x_lo'=2,'core'=2,'z'=8,'x_hi'=2] {'y','x_hi','x_lo'}, dimensions={0} | all-to-all | bytes 1179648 | tf_op jit(solution)/shard_map/all_to_all | solution.py:224
  47.0 0.1 reduce_sum.21
  47.2 16.0 %all_to_all.16 = bf16[8,144,128]{2,1,0:T(8,128)(2,1)S(1)} all-to-all(bf16[8,144,128]{2,1,0:T(8,128)(2,1)S(1)} %broadcast_in_dim.16), channel_id=1, replica_groups=mesh['y'=4,'x_lo'=2,'core'=2,'z'=8,'x_hi'=2] {'z'}, dimensions={0} | all-to-all | bytes 589824 | tf_op jit(solution)/shard_map/all_to_all | solution.py:224
  63.2 0.1 broadcast_in_dim.17
  63.3 13.5 %all_to_all.17 = bf16[16,144,128]{2,1,0:T(8,128)(2,1)S(1)} all-to-all(bf16[16,144,128]{2,1,0:T(8,128)(2,1)S(1)} %broadcast_in_dim.17), channel_id=1, replica_groups=mesh['y'=4,'x_lo'=2,'core'=2,'z'=8,'x_hi'=2] {'y','x_hi','x_lo'}, dimensions={0} | all-to-all | bytes 1179648 | tf_op jit(solution)/shard_map/all_to_all | solution.py:224
  76.9 4.7 %collective-permute-start.5 = (bf16[9,256,128]{2,1,0:T(8,128)(2,1)S(1)}, bf16[9,256,128]{2,1,0:T(8,128)(2,1)S(1)}, u32[]{:S(2)}, u32[]{:S(2)}) collective-permute-start(bf16[9,256,128]{2,1,0:T(8,128)(2,1)S(1)} %bitcast.14), channel_id=1, source_target_pairs={{0,16},{16,0},{1,17},{17,1},{2,18},{18,2},{3,19},{19,3},{4,20},{20... | collective-permute-start | bytes 1769480 | tf_op jit(solution)/shard_map/ppermute | solution.py:247
  81.5 0.9 %copy.14 = bf16[32,8,8,128]{3,2,1,0:T(8,128)(2,1)} copy(bf16[32,8,8,128]{3,1,2,0:T(8,128)(2,1)S(1)} %bitcast.16) | data formatting | bytes 1048576
  82.4 1.1 %shard_map.72.refs_0_ = f32[9,256,256]{2,1,0:T(8,128)} custom-call(bf16[9,256,128]{2,1,0:T(8,128)(2,1)S(1)} %bitcast.15), custom_call_target="tpu_custom_call" | custom-call | flops 1000000 | bytes 1000000 | tf_op jit(solution)/shard_map/pallas_call | solution.py:211
  83.5 0.0 collective-permute-done.5.half_ref
  83.5 1.1 %shard_map.73 = f32[9,256,256]{2,1,0:T(8,128)} custom-call(bf16[9,256,128]{2,1,0:T(8,128)(2,1)S(1)} %collective-permute-done.5.half_ref, f32[9,256,256]{2,1,0:T(8,128)} %shard_map.72.refs_0_), custom_call_target="tpu_custom_call", output_to_operand_aliasing={{}: (1, {})} | custom-call | flops 1000000 | bytes 1000000 | tf_op jit(solution)/shard_map/pallas_call | solution.py:211
  (7 shorter events, 0.2 us)
Async XLA Ops:
  0.6 6.2 %copy-start = (bf16[9,128,7,33]{1,2,3,0:T(8,128)(2,1)S(1)}, bf16[9,128,7,33]{1,2,3,0:T(8,128)(2,1)}, u32[]{:S(2)}) copy-start(bf16[9,128,7,33]{1,2,3,0:T(8,128)(2,1)} %param.8) | copy-start | bytes 1596676
  0.6 6.1 %copy-start.3 = (s32[128]{0:T(128)S(1)}, s32[128]{0:T(128)}, u32[]{:S(2)}) copy-start(s32[128]{0:T(128)} %param.9) | copy-start | bytes 1540
  2.1 9.0 %collective-permute-start.1 = (bf16[3,128,256]{2,1,0:T(8,128)(2,1)S(1)}, bf16[3,128,256]{2,1,0:T(8,128)(2,1)S(1)}, u32[]{:S(2)}, u32[]{:S(2)}) collective-permute-start(bf16[3,128,256]{2,1,0:T(8,128)(2,1)S(1)} %get-tuple-element.34), channel_id=1, source_target_pairs={{16,32},{32,16},{48,64},{64,48},{80,96},{96,80},{112,128},{128,112... | collective-permute-start | bytes 589832 | tf_op jit(solution)/shard_map/ppermute | solution.py:25
  6.6 4.5 %collective-permute-start = (bf16[3,128,256]{2,1,0:T(8,128)(2,1)S(1)}, bf16[3,128,256]{2,1,0:T(8,128)(2,1)S(1)}, u32[]{:S(2)}, u32[]{:S(2)}) collective-permute-start(bf16[3,128,256]{2,1,0:T(8,128)(2,1)S(1)} %get-tuple-element.35), channel_id=1, source_target_pairs={{0,16},{16,0},{32,48},{48,32},{64,80},{80,64},{96,112},{112,96},{1... | collective-permute-start | bytes 589832 | tf_op jit(solution)/shard_map/ppermute | solution.py:25
  7.1 12.4 %copy-start.2 = (bf16[256,8,128]{2,1,0:T(8,128)(2,1)S(1)}, bf16[256,8,128]{2,1,0:T(8,128)(2,1)}, u32[]{:S(2)}) copy-start(bf16[256,8,128]{2,1,0:T(8,128)(2,1)} %param.5) | copy-start | bytes 1572868
  11.1 11.9 %collective-permute-start.2 = (bf16[14,16,256]{2,1,0:T(8,128)(2,1)S(1)}, bf16[14,16,256]{2,1,0:T(8,128)(2,1)S(1)}, u32[]{:S(2)}, u32[]{:S(2)}) collective-permute-start(bf16[14,16,256]{2,1,0:T(8,128)(2,1)S(1)} %get-tuple-element.20), channel_id=1, source_target_pairs={{0,1},{1,0},{2,3},{3,2},{4,5},{5,4},{6,7},{7,6},{8,9},{9,8},{10,11... | collective-permute-start | bytes 344072 | tf_op jit(solution)/shard_map/ppermute | solution.py:25
  13.9 9.2 %collective-permute-start.3 = (bf16[14,16,256]{2,1,0:T(8,128)(2,1)S(1)}, bf16[14,16,256]{2,1,0:T(8,128)(2,1)S(1)}, u32[]{:S(2)}, u32[]{:S(2)}) collective-permute-start(bf16[14,16,256]{2,1,0:T(8,128)(2,1)S(1)} %get-tuple-element.21), channel_id=1, source_target_pairs={{0,15},{1,2},{2,1},{3,4},{4,3},{5,6},{6,5},{7,8},{8,7},{9,10},{10,... | collective-permute-start | bytes 344072 | tf_op jit(solution)/shard_map/ppermute | solution.py:25
  19.6 3.5 %copy-start.1 = (bf16[9,256,256]{2,1,0:T(8,128)(2,1)S(1)}, bf16[9,256,256]{2,1,0:T(8,128)(2,1)}, u32[]{:S(2)}) copy-start(bf16[9,256,256]{2,1,0:T(8,128)(2,1)} %w_ref.1) | copy-start | bytes 3538948
  25.7 2.9 %collective-permute-start.4 = (f32[9,256,128]{2,1,0:T(8,128)S(1)}, f32[9,256,128]{2,1,0:T(8,128)S(1)}, u32[]{:S(2)}, u32[]{:S(2)}) collective-permute-start(f32[9,256,128]{2,1,0:T(8,128)S(1)} %broadcast_select_fusion), channel_id=1, source_target_pairs={{0,16},{16,0},{1,17},{17,1},{2,18},{18,2},{3,19},{19,3},{4,20},{20... | collective-permute-start | bytes 3538952 | tf_op jit(solution)/shard_map/ppermute | solution.py:239
  76.9 6.6 %collective-permute-start.5 = (bf16[9,256,128]{2,1,0:T(8,128)(2,1)S(1)}, bf16[9,256,128]{2,1,0:T(8,128)(2,1)S(1)}, u32[]{:S(2)}, u32[]{:S(2)}) collective-permute-start(bf16[9,256,128]{2,1,0:T(8,128)(2,1)S(1)} %bitcast.14), channel_id=1, source_target_pairs={{0,16},{16,0},{1,17},{17,1},{2,18},{18,2},{3,19},{19,3},{4,20},{20... | collective-permute-start | bytes 1769480 | tf_op jit(solution)/shard_map/ppermute | solution.py:247

commit v8 on v7

--- a/solution.py
+++ b/solution.py
@@ -14,15 +14,14 @@
 bf16, f32 = jnp.bfloat16, jnp.float32
 
 
-def exchange(first, second, axes, closed):
+def pairs(axes, near, closed):
     count = 1
     for axis in axes:
         count *= lax.axis_size(axis)
-    near = [(i, i ^ 1) for i in range(count)]
+    if near:
+        return [(i, i ^ 1) for i in range(count)]
     far = [(i, (i + 1 - 2 * (i % 2 == 0)) % count) for i in range(count)]
-    if not closed:
-        far = far[1:-1]
-    return lax.ppermute(first, axes, near), lax.ppermute(second, axes, far)
+    return far if closed else far[1:-1]
 
 
 def parity(axes):
@@ -44,7 +43,7 @@
     return jnp.transpose(table, (0, 2, 1, 3))
 
 
-def rim_kernel(main, near, far, first, second):
+def rim_kernel(main, near, far, second, first):
     lat_dev, lon_dev, _ = main.shape
     half, side = near.shape[0], first.shape[1]
     odd_lon, odd_lat = parity(LON), parity(LAT)
@@ -55,13 +54,15 @@
         def _():
             for ref, at in ((first, last if even else 0), (second, 0 if even else last)):
                 ref[half : half + lat_dev] = main[:, at : at + side, :]
+                own = slice(at, at + side)
+                outer = slice(side, 2 * side) if at else slice(0, side)
                 for upper in (0, 1):
 
                     @pl.when(odd_lat != upper)
                     def _():
-                        up, down = (far, near) if upper else (near, far)
-                        ref[:half] = up[:, at : at + side, :]
-                        ref[half + lat_dev :] = down[:, at : at + side, :]
+                        above, below = slice(0, half), slice(half + lat_dev, None)
+                        ref[above if upper else below] = far[:, outer, :]
+                        ref[below if upper else above] = near[:, own, :]
 
 
 def convolve(band, ext, place, q_ref):
@@ -112,7 +113,7 @@
         f_edge[:, at] = jnp.where(lane < wide, ahead(even), back(odd)).astype(bf16)
 
 
-def middle_kernel(nlat_all, taps, f_ref, main, near, far, band, f_edge, q_ref, total, window, lines, f_mid, ext):
+def middle_kernel(nlat_all, taps, f_ref, main, near, far, rest, band, f_edge, q_ref, total, window, lines, f_mid, ext):
     lat_dev, lon_dev, channels = main.shape
     half, side = near.shape[0], BLOCK // 2
     inner = window.shape[2]
@@ -125,8 +126,12 @@
 
         @pl.when(odd_lat != upper)
         def _():
-            ext[:half] = (far if upper else near)[...]
-            ext[half + lat_dev :] = (near if upper else far)[...]
+            above, below = slice(0, half), slice(half + lat_dev, None)
+            ext[below if upper else above] = near[...]
+            other = above if upper else below
+            ext[other, :side, :] = far[:, :side, :]
+            ext[other, side : lon_dev - side, :] = rest[...]
+            ext[other, lon_dev - side :, :] = far[:, side:, :]
 
     window[:, 0] = ext[:, lon_dev - inner :, :]
     window[:, 1] = ext[:, :inner, :]
@@ -136,7 +141,7 @@
         total[k] = jnp.dot(f_mid[...], cells, preferred_element_type=f32)
 
 
-def edge_kernel(band, window, near, far, f_ref, total, w_ref, q_ref, low, high, w_out, ext, sem):
+def edge_kernel(band, window, far, near, f_ref, total, w_ref, q_ref, low, high, w_out, ext, sem):
     fetch = pltpu.make_async_copy(w_ref, w_out, sem)
     fetch.start()
     channels = window.shape[3]
@@ -228,7 +233,7 @@
     return jnp.broadcast_to(x[None], (count,) + x.shape)
 
 
-def reduce_all(low, high, core, scale, beside, finish):
+def reduce_all(low, high, core, scale, beside):
     swap = [(0, 1), (1, 0)]
     basis_count, channels, half = low.shape
     plane = 1
@@ -243,8 +248,7 @@
     own = jnp.sum(all_to_all(to_all(own, depth), ("z",)).astype(f32), axis=0)
     own = (own * scale).astype(bf16)
     own = all_to_all(to_all(own, plane), PLANE).reshape(basis_count, channels, half)
-    beside = finish(beside)
-    other, summed, beside = lax.optimization_barrier((lax.ppermute(own, "core", swap), place(own, True), beside))
+    other, summed = lax.optimization_barrier((lax.ppermute(own, "core", swap), place(own, True)))
     return place(other, False, summed), beside
 
 
@@ -259,10 +263,15 @@
     upper = core == 0
     main = jnp.transpose(grad_out, (1, 2, 0))
     last, first = main[lat_dev - half :], main[:half]
-    near_lat, far_lat = exchange(jnp.where(upper, last, first), jnp.where(upper, first, last), LAT, False)
+    to_near, to_far = jnp.where(upper, last, first), jnp.where(upper, first, last)
+    outer = jnp.concatenate([to_far[:, :side], to_far[:, lon_dev - side :]], axis=1)
+    far_lat = lax.ppermute(outer, LAT, pairs(LAT, False, False))
+    near_lat = lax.ppermute(to_near, LAT, pairs(LAT, True, False))
+    rest_lat = lax.ppermute(to_far[:, side : lon_dev - side], LAT, pairs(LAT, False, False))
     rim = shape((near, side, channels), bf16)
-    rims = call(rim_kernel, (rim, rim), (main, near_lat, far_lat), flops=10**6, mib=4)
-    near_lon, far_lon = exchange(*rims, LON, True)
+    to_far, to_near = call(rim_kernel, (rim, rim), (main, near_lat, far_lat), flops=10**6, mib=4)
+    far_lon = lax.ppermute(to_far, LON, pairs(LON, False, True))
+    near_lon = lax.ppermute(to_near, LON, pairs(LON, True, True))
     taps = tap_rows(basis_table, lon_reach, start, held)
     q_shape = shape((basis_count, lat_dev, wide, channels), bf16)
     columns = shape((channels, lat_dev * wide), bf16)
@@ -276,7 +285,7 @@
             shape((basis_count, channels, channels), f32),
             shape((near, 2, wide - side, channels), bf16),
         ),
-        (taps, fields.reshape(channels, lat_dev * lon_dev), main, near_lat, far_lat),
+        (taps, fields.reshape(channels, lat_dev * lon_dev), main, near_lat, far_lat, rest_lat),
         [
             pltpu.VMEM((basis_count, row_span, held + 16, 128), f32),
             pltpu.VMEM(columns.shape, bf16),
@@ -286,14 +295,13 @@
     q_edge, low, high, weight = call(
         edge_kernel,
         (q_shape, part, part, shape(weight.shape, bf16)),
-        (band, window, near_lon, far_lon, f_edge, total, weight),
+        (band, window, far_lon, near_lon, f_edge, total, weight),
         [pltpu.VMEM((near, 2, wide, channels), bf16), pltpu.SemaphoreType.DMA],
         hbm=1,
     )
     mixed = call(mix_kernel, shape((channels, lat_dev * lon_dev), bf16), (weight, q_mid, q_edge))
-    weight_grad, field_grad = reduce_all(
-        low, high, core, 1.0 / nlat_all, mixed, lambda x: x.reshape(channels, lat_dev, lon_dev)
-    )
+    field_grad = mixed.reshape(channels, lat_dev, lon_dev)
+    weight_grad, field_grad = reduce_all(low, high, core, 1.0 / nlat_all, field_grad)
     return field_grad, weight_grad
 
 

time: 84.8 us -> 83.7 us (0.987)
  starting transfers between devices: 17.7 us -> 20.7 us
  blocking collectives: 47.7 us -> 45.1 us
  waiting for transfers between devices: 4.88 us -> 3.45 us
    all_to_all x3, blocking collectives: 47.7 us -> 45.1 us  [all_to_all(): return lax.all_to_all(x, axes, 0, 0, tiled=True)]
    ppermute x4 -> x5, starting transfers between devices: 13 us -> 14.6 us  [the longest x1 8.09 us: local(): far_lon = lax.ppermute(to_far, LON, pairs(LON, False, True))]
    ppermute x1, starting transfers between devices: 0.09 us -> 1.35 us  [reduce_all(): lax.ppermute(send, 'core', swap)]
    ppermute x1, waiting for transfers between devices: 1.42 us -> 0.16 us  [reduce_all(): lax.ppermute(send, 'core', swap)]
    ppermute x4 -> x5, waiting for transfers between devices: 3.46 us -> 2.72 us  [the longest x1 2.23 us: local(): near_lon = lax.ppermute(to_near, LON, pairs(LON, True, True))]
  transfers between devices with their start and end apart: 6 -> 7, of which waited for: 2 -> 4; matrix products, arithmetic and copies ran while one was open for 2% -> 2% of each run, Pallas kernels for 7% -> 7%
where the time goes in v8:
time: 83.7 us; the launch traced here: 83.5 us
  blocking collectives  45.1 us (54%)
  starting transfers between devices  20.7 us (25%)
  Pallas kernels  9.4 us (11%)
  waiting for transfers between devices  3.45 us (4%)
  local copies, waits for them, and re-layouts  3.33 us (4%)
  between operations  0.89 us (1%)
    all_to_all x3, blocking collectives, all_to_all(): return lax.all_to_all(x, axes, 0, 0, tiled=True)  45.1 us
    ppermute x1, starting transfers between devices, local(): far_lon = lax.ppermute(to_far, LON, pairs(LON, False, True))  8.09 us
    pallas_call x4, Pallas kernels, call(): pl.pallas_call(kernel, out_shape=out_shape, in_specs=[vmem] * (len(operan...  7.29 us
    ppermute x1, starting transfers between devices, reduce_all(): lax.ppermute(own, 'core', swap)  4.68 us
    ppermute x1, starting transfers between devices, local(): far_lat = lax.ppermute(outer, LAT, pairs(LAT, False, False))  4.51 us
    unnamed x12, local copies, waits for them, and re-layouts  2.89 us
    ppermute x1, waiting for transfers between devices, local(): near_lon = lax.ppermute(to_near, LON, pairs(LON, True, True))  2.23 us
    pallas_call x2, Pallas kernels, place(): pl.pallas_call(functools.partial(place_kernel, own), out_shape=jax.ShapeD...  2.11 us
  transfers between devices with their start and end apart: 7, of which 4 were waited for; matrix products, arithmetic and copies ran while one was open for 2% of the time, Pallas kernels for 7%

profile of v8, /device:TPU:1, one launch (start us, length us, event | category | flops | bytes accessed | tf_op | source)
XLA Modules:
  0.0 83.5 jit_solution(12081082938696294578)
XLA Ops:
  0.6 0.0 copy-start
  0.7 0.0 copy-start.3
  0.7 1.4 %copy.11 = bf16[256,8,128]{0,2,1:T(8,128)(2,1)S(1)} copy(bf16[256,8,128]{2,1,0:T(8,128)(2,1)} %param.6) | data formatting | bytes 1048576 | tf_op args[1]
  2.1 4.5 %collective-permute-start.1 = (bf16[3,32,256]{2,1,0:T(8,128)(2,1)S(1)}, bf16[3,32,256]{2,1,0:T(8,128)(2,1)S(1)}, u32[]{:S(2)}, u32[]{:S(2)}) collective-permute-start(bf16[3,32,256]{2,1,0:T(8,128)(2,1)S(1)} %pad_maximum_fusion), channel_id=1, source_target_pairs={{16,32},{32,16},{48,64},{64,48},{80,96},{96,80},{112,128},{128,112... | collective-permute-start | bytes 147464 | tf_op jit(solution)/shard_map/ppermute | solution.py:268
  6.7 1.9 %collective-permute-start.2 = (bf16[3,96,256]{2,1,0:T(8,128)(2,1)S(1)}, bf16[3,96,256]{2,1,0:T(8,128)(2,1)S(1)}, u32[]{:S(2)}, u32[]{:S(2)}) collective-permute-start(bf16[3,96,256]{2,1,0:T(8,128)(2,1)S(1)} %slice.24), channel_id=1, source_target_pairs={{16,32},{32,16},{48,64},{64,48},{80,96},{96,80},{112,128},{128,112... | collective-permute-start | bytes 442376 | tf_op jit(solution)/shard_map/ppermute | solution.py:270
  8.6 0.1 collective-permute-start
  8.7 0.0 copy-done.3
  8.7 0.1 dynamic_slice.6
  8.8 0.1 broadcast_compare_fusion
  8.9 0.0 copy-done
  8.9 0.2 constant_dynamic-slice_fusion
  9.1 0.0 copy-start.2
  9.1 0.5 copy.12
  9.6 0.0 collective-permute-done.1.far
  9.6 0.5 collective-permute-done.near
  10.1 8.1 %collective-permute-start.3 = (bf16[14,16,256]{2,1,0:T(8,128)(2,1)S(1)}, bf16[14,16,256]{2,1,0:T(8,128)(2,1)S(1)}, u32[]{:S(2)}, u32[]{:S(2)}) collective-permute-start(bf16[14,16,256]{2,1,0:T(8,128)(2,1)S(1)} %get-tuple-element.19), channel_id=1, source_target_pairs={{0,15},{1,2},{2,1},{3,4},{4,3},{5,6},{6,5},{7,8},{8,7},{9,10},{10,... | collective-permute-start | bytes 344072 | tf_op jit(solution)/shard_map/ppermute | solution.py:273
  18.2 0.0 collective-permute-start.4
  18.3 0.0 copy-done.2
  18.3 0.1 copy.16
  18.4 0.0 collective-permute-done.2.rest
  18.4 0.0 copy-start.1
  18.4 3.4 %shard_map.68 = (bf16[8,288,512]{2,1,0:T(8,128)(2,1)S(1)}, bf16[256,512]{1,0:T(8,128)(2,1)S(1)}, bf16[9,8,64,256]{3,2,1,0:T(8,128)(2,1)S(1)}, f32[9,256,256]{2,1,0:T(8,128)S(1)}, bf16[14,2,48,256]{3,2,1,0:T(8,128)(2,1)S(1)}) custom-call(bf16[9,7,16,33]{3,2,1,0:T(8,128)(2,1)S(1)} %select_bitcast_fusion.taps, bf16[256,1024]{1,0:T(8,128)(2,1)S(1)} %bitcast.17, ...), custom_call_target="tpu_custom_call" | custom-call | flops 1000000000 | bytes 1000000 | tf_op jit(solution)/shard_map/pallas_call | solution.py:170
  21.8 0.0 collective-permute-done.3.far
  21.8 2.2 %collective-permute-done.4.near = bf16[14,16,256]{2,1,0:T(8,128)(2,1)S(1)} collective-permute-done((bf16[14,16,256]{2,1,0:T(8,128)(2,1)S(1)}, bf16[14,16,256]{2,1,0:T(8,128)(2,1)S(1)}, u32[]{:S(2)}, u32[]{:S(2)}) %collective-permute-start.4) | collective-permute-done | bytes 114720 | tf_op jit(solution)/shard_map/ppermute | solution.py:274
  24.0 0.0 copy-done.1
  24.0 2.5 %shard_map.70 = (bf16[9,8,64,256]{3,2,1,0:T(8,128)(2,1)S(1)}, f32[9,256,128]{2,1,0:T(8,128)S(1)}, f32[9,256,128]{2,1,0:T(8,128)S(1)}, bf16[9,256,256]{2,1,0:T(8,128)(2,1)S(1)}) custom-call(bf16[8,288,512]{2,1,0:T(8,128)(2,1)S(1)} %get-tuple-element.17.band, bf16[14,2,48,256]{3,2,1,0:T(8,128)(2,1)S(1)} %get-tuple-element.18.window, ...), custom_call_target="tpu_custom_call" | custom-call | flops 1000000000 | bytes 1000000 | tf_op jit(solution)/shard_map/pallas_call | solution.py:170
  26.5 0.1 broadcast_select_fusion
  26.6 1.4 %collective-permute-start.5 = (f32[9,256,128]{2,1,0:T(8,128)S(1)}, f32[9,256,128]{2,1,0:T(8,128)S(1)}, u32[]{:S(2)}, u32[]{:S(2)}) collective-permute-start(f32[9,256,128]{2,1,0:T(8,128)S(1)} %broadcast_select_fusion), channel_id=1, source_target_pairs={{0,16},{16,0},{1,17},{17,1},{2,18},{18,2},{3,19},{19,3},{4,20},{20... | collective-permute-start | bytes 3538952 | tf_op jit(solution)/shard_map/ppermute | solution.py:244
  28.0 1.4 %shard_map.71 = bf16[256,1024]{1,0:T(8,128)(2,1)S(1)} custom-call(bf16[9,256,256]{2,1,0:T(8,128)(2,1)S(1)} %get-tuple-element.25.w_ref, bf16[9,8,64,256]{3,2,1,0:T(8,128)(2,1)S(1)} %get-tuple-element.26.mid_ref, bf16[9,8,64,256]{3,2,1,0:T(8,128)(2,1)S(1)} %get-tuple-element.27.edge_ref), custom_call_target="tpu_custom_call" | custom-call | flops 1000000000 | bytes 1000000 | tf_op jit(solution)/shard_map/pallas_call | solution.py:170
  29.4 0.9 %copy.14 = bf16[32,8,8,128]{3,2,1,0:T(8,128)(2,1)} copy(bf16[32,8,8,128]{3,1,2,0:T(8,128)(2,1)S(1)} %bitcast.16) | data formatting | bytes 1048576
  30.3 0.2 collective-permute-done.5
  30.5 0.2 add_convert_fusion
  30.7 16.8 %all_to_all.15 = bf16[16,144,128]{2,1,0:T(8,128)(2,1)S(1)} all-to-all(bf16[16,144,128]{2,1,0:T(8,128)(2,1)S(1)} %bitcast.18), channel_id=1, replica_groups=mesh['y'=4,'x_lo'=2,'core'=2,'z'=8,'x_hi'=2] {'y','x_hi','x_lo'}, dimensions={0} | all-to-all | bytes 1179648 | tf_op jit(solution)/shard_map/all_to_all | solution.py:229
  47.6 0.1 reduce_sum.21
  47.7 14.7 %all_to_all.16 = bf16[8,144,128]{2,1,0:T(8,128)(2,1)S(1)} all-to-all(bf16[8,144,128]{2,1,0:T(8,128)(2,1)S(1)} %broadcast_in_dim.16), channel_id=1, replica_groups=mesh['y'=4,'x_lo'=2,'core'=2,'z'=8,'x_hi'=2] {'z'}, dimensions={0} | all-to-all | bytes 589824 | tf_op jit(solution)/shard_map/all_to_all | solution.py:229
  62.5 0.1 broadcast_in_dim.17
  62.6 13.5 %all_to_all.17 = bf16[16,144,128]{2,1,0:T(8,128)(2,1)S(1)} all-to-all(bf16[16,144,128]{2,1,0:T(8,128)(2,1)S(1)} %broadcast_in_dim.17), channel_id=1, replica_groups=mesh['y'=4,'x_lo'=2,'core'=2,'z'=8,'x_hi'=2] {'y','x_hi','x_lo'}, dimensions={0} | all-to-all | bytes 1179648 | tf_op jit(solution)/shard_map/all_to_all | solution.py:229
  76.1 4.7 %collective-permute-start.6 = (bf16[9,256,128]{2,1,0:T(8,128)(2,1)S(1)}, bf16[9,256,128]{2,1,0:T(8,128)(2,1)S(1)}, u32[]{:S(2)}, u32[]{:S(2)}) collective-permute-start(bf16[9,256,128]{2,1,0:T(8,128)(2,1)S(1)} %bitcast.14), channel_id=1, source_target_pairs={{0,16},{16,0},{1,17},{17,1},{2,18},{18,2},{3,19},{19,3},{4,20},{20... | collective-permute-start | bytes 1769480 | tf_op jit(solution)/shard_map/ppermute | solution.py:251
  80.8 1.1 %shard_map.72.refs_0_ = f32[9,256,256]{2,1,0:T(8,128)} custom-call(bf16[9,256,128]{2,1,0:T(8,128)(2,1)S(1)} %bitcast.15), custom_call_target="tpu_custom_call" | custom-call | flops 1000000 | bytes 1000000 | tf_op jit(solution)/shard_map/pallas_call | solution.py:216
  81.9 0.6 collective-permute-done.6.half_ref
  82.4 1.1 %shard_map.73 = f32[9,256,256]{2,1,0:T(8,128)} custom-call(bf16[9,256,128]{2,1,0:T(8,128)(2,1)S(1)} %collective-permute-done.6.half_ref, f32[9,256,256]{2,1,0:T(8,128)} %shard_map.72.refs_0_), custom_call_target="tpu_custom_call", output_to_operand_aliasing={{}: (1, {})} | custom-call | flops 1000000 | bytes 1000000 | tf_op jit(solution)/shard_map/pallas_call | solution.py:216
  (10 shorter events, 0.2 us)
Async XLA Ops:
  0.6 8.3 %copy-start = (bf16[9,128,7,33]{1,2,3,0:T(8,128)(2,1)S(1)}, bf16[9,128,7,33]{1,2,3,0:T(8,128)(2,1)}, u32[]{:S(2)}) copy-start(bf16[9,128,7,33]{1,2,3,0:T(8,128)(2,1)} %param.8) | copy-start | bytes 1596676
  0.7 8.1 %copy-start.3 = (s32[128]{0:T(128)S(1)}, s32[128]{0:T(128)}, u32[]{:S(2)}) copy-start(s32[128]{0:T(128)} %param.9) | copy-start | bytes 1540
  2.1 7.5 %collective-permute-start.1 = (bf16[3,32,256]{2,1,0:T(8,128)(2,1)S(1)}, bf16[3,32,256]{2,1,0:T(8,128)(2,1)S(1)}, u32[]{:S(2)}, u32[]{:S(2)}) collective-permute-start(bf16[3,32,256]{2,1,0:T(8,128)(2,1)S(1)} %pad_maximum_fusion), channel_id=1, source_target_pairs={{16,32},{32,16},{48,64},{64,48},{80,96},{96,80},{112,128},{128,112... | collective-permute-start | bytes 147464 | tf_op jit(solution)/shard_map/ppermute | solution.py:268
  6.7 11.7 %collective-permute-start.2 = (bf16[3,96,256]{2,1,0:T(8,128)(2,1)S(1)}, bf16[3,96,256]{2,1,0:T(8,128)(2,1)S(1)}, u32[]{:S(2)}, u32[]{:S(2)}) collective-permute-start(bf16[3,96,256]{2,1,0:T(8,128)(2,1)S(1)} %slice.24), channel_id=1, source_target_pairs={{16,32},{32,16},{48,64},{64,48},{80,96},{96,80},{112,128},{128,112... | collective-permute-start | bytes 442376 | tf_op jit(solution)/shard_map/ppermute | solution.py:270
  8.6 1.5 %collective-permute-start = (bf16[3,128,256]{2,1,0:T(8,128)(2,1)S(1)}, bf16[3,128,256]{2,1,0:T(8,128)(2,1)S(1)}, u32[]{:S(2)}, u32[]{:S(2)}) collective-permute-start(bf16[3,128,256]{2,1,0:T(8,128)(2,1)S(1)} %get-tuple-element.33), channel_id=1, source_target_pairs={{0,16},{16,0},{32,48},{48,32},{64,80},{80,64},{96,112},{112,96},{1... | collective-permute-start | bytes 589832 | tf_op jit(solution)/shard_map/ppermute | solution.py:269
  9.1 9.1 %copy-start.2 = (bf16[256,8,128]{2,1,0:T(8,128)(2,1)S(1)}, bf16[256,8,128]{2,1,0:T(8,128)(2,1)}, u32[]{:S(2)}) copy-start(bf16[256,8,128]{2,1,0:T(8,128)(2,1)} %param.5) | copy-start | bytes 1572868
  10.1 11.7 %collective-permute-start.3 = (bf16[14,16,256]{2,1,0:T(8,128)(2,1)S(1)}, bf16[14,16,256]{2,1,0:T(8,128)(2,1)S(1)}, u32[]{:S(2)}, u32[]{:S(2)}) collective-permute-start(bf16[14,16,256]{2,1,0:T(8,128)(2,1)S(1)} %get-tuple-element.19), channel_id=1, source_target_pairs={{0,15},{1,2},{2,1},{3,4},{4,3},{5,6},{6,5},{7,8},{8,7},{9,10},{10,... | collective-permute-start | bytes 344072 | tf_op jit(solution)/shard_map/ppermute | solution.py:273
  18.2 5.8 %collective-permute-start.4 = (bf16[14,16,256]{2,1,0:T(8,128)(2,1)S(1)}, bf16[14,16,256]{2,1,0:T(8,128)(2,1)S(1)}, u32[]{:S(2)}, u32[]{:S(2)}) collective-permute-start(bf16[14,16,256]{2,1,0:T(8,128)(2,1)S(1)} %get-tuple-element.20), channel_id=1, source_target_pairs={{0,1},{1,0},{2,3},{3,2},{4,5},{5,4},{6,7},{7,6},{8,9},{9,8},{10,11... | collective-permute-start | bytes 344072 | tf_op jit(solution)/shard_map/ppermute | solution.py:274
  18.4 5.7 %copy-start.1 = (bf16[9,256,256]{2,1,0:T(8,128)(2,1)S(1)}, bf16[9,256,256]{2,1,0:T(8,128)(2,1)}, u32[]{:S(2)}) copy-start(bf16[9,256,256]{2,1,0:T(8,128)(2,1)} %w_ref.1) | copy-start | bytes 3538948
  26.6 3.8 %collective-permute-start.5 = (f32[9,256,128]{2,1,0:T(8,128)S(1)}, f32[9,256,128]{2,1,0:T(8,128)S(1)}, u32[]{:S(2)}, u32[]{:S(2)}) collective-permute-start(f32[9,256,128]{2,1,0:T(8,128)S(1)} %broadcast_select_fusion), channel_id=1, source_target_pairs={{0,16},{16,0},{1,17},{17,1},{2,18},{18,2},{3,19},{19,3},{4,20},{20... | collective-permute-start | bytes 3538952 | tf_op jit(solution)/shard_map/ppermute | solution.py:244
  76.1 6.3 %collective-permute-start.6 = (bf16[9,256,128]{2,1,0:T(8,128)(2,1)S(1)}, bf16[9,256,128]{2,1,0:T(8,128)(2,1)S(1)}, u32[]{:S(2)}, u32[]{:S(2)}) collective-permute-start(bf16[9,256,128]{2,1,0:T(8,128)(2,1)S(1)} %bitcast.14), channel_id=1, source_target_pairs={{0,16},{16,0},{1,17},{17,1},{2,18},{18,2},{3,19},{19,3},{4,20},{20... | collective-permute-start | bytes 1769480 | tf_op jit(solution)/shard_map/ppermute | solution.py:251

commit v9 on v8

--- a/solution.py
+++ b/solution.py
@@ -233,22 +233,23 @@
     return jnp.broadcast_to(x[None], (count,) + x.shape)
 
 
-def reduce_all(low, high, core, scale, beside):
+def reduce_all(low, high, core, scale, beside, finish):
     swap = [(0, 1), (1, 0)]
     basis_count, channels, half = low.shape
     plane = 1
     for axis in PLANE:
         plane *= lax.axis_size(axis)
     depth = lax.axis_size("z")
-    keep, send = jnp.where(core == 0, low, high), jnp.where(core == 0, high, low)
+    keep, send = jnp.where(core == 0, low, high), jnp.where(core == 0, high, low).astype(bf16)
     came, beside = lax.optimization_barrier((lax.ppermute(send, "core", swap), beside))
-    own = keep + came
+    own = keep + came.astype(f32)
     own = own.reshape(plane, -1, half).astype(bf16)
     own = jnp.sum(all_to_all(own, PLANE).astype(f32), axis=0).astype(bf16)
     own = jnp.sum(all_to_all(to_all(own, depth), ("z",)).astype(f32), axis=0)
     own = (own * scale).astype(bf16)
     own = all_to_all(to_all(own, plane), PLANE).reshape(basis_count, channels, half)
-    other, summed = lax.optimization_barrier((lax.ppermute(own, "core", swap), place(own, True)))
+    beside = finish(beside)
+    other, summed, beside = lax.optimization_barrier((lax.ppermute(own, "core", swap), place(own, True), beside))
     return place(other, False, summed), beside
 
 
@@ -267,7 +268,8 @@
     outer = jnp.concatenate([to_far[:, :side], to_far[:, lon_dev - side :]], axis=1)
     far_lat = lax.ppermute(outer, LAT, pairs(LAT, False, False))
     near_lat = lax.ppermute(to_near, LAT, pairs(LAT, True, False))
-    rest_lat = lax.ppermute(to_far[:, side : lon_dev - side], LAT, pairs(LAT, False, False))
+    rest, near_lat = lax.optimization_barrier((to_far[:, side : lon_dev - side], near_lat))
+    rest_lat = lax.ppermute(rest, LAT, pairs(LAT, False, False))
     rim = shape((near, side, channels), bf16)
     to_far, to_near = call(rim_kernel, (rim, rim), (main, near_lat, far_lat), flops=10**6, mib=4)
     far_lon = lax.ppermute(to_far, LON, pairs(LON, False, True))
@@ -300,8 +302,9 @@
         hbm=1,
     )
     mixed = call(mix_kernel, shape((channels, lat_dev * lon_dev), bf16), (weight, q_mid, q_edge))
-    field_grad = mixed.reshape(channels, lat_dev, lon_dev)
-    weight_grad, field_grad = reduce_all(low, high, core, 1.0 / nlat_all, field_grad)
+    weight_grad, field_grad = reduce_all(
+        low, high, core, 1.0 / nlat_all, mixed, lambda x: x.reshape(channels, lat_dev, lon_dev)
+    )
     return field_grad, weight_grad
 
 

time: 83.7 us -> 84.2 us (level)
  blocking collectives: 45.1 us -> 46.5 us
    all_to_all x3, blocking collectives: 45.1 us -> 46.5 us  [all_to_all(): return lax.all_to_all(x, axes, 0, 0, tiled=True)]
    ppermute x1, starting transfers between devices: 1.92 us -> 3.19 us  [local(): rest_lat = lax.ppermute(rest, LAT, pairs(LAT, False, False))]
    ppermute x1, starting transfers between devices: 1.35 us -> 0.09 us  [reduce_all(): lax.ppermute(send, 'core', swap)]
  transfers between devices with their start and end apart: 7 -> 7, of which waited for: 4 -> 3; matrix products, arithmetic and copies ran while one was open for 2% -> 2% of each run, Pallas kernels for 7% -> 7%
where the time goes in v9:
time: 84.2 us; the launch traced here: 84 us
  blocking collectives  46.5 us (55%)
  starting transfers between devices  20.6 us (24%)
  Pallas kernels  9.43 us (11%)
  local copies, waits for them, and re-layouts  3.33 us (4%)
  waiting for transfers between devices  2.63 us (3%)
  between operations  0.91 us (1%)
    all_to_all x3, blocking collectives, all_to_all(): return lax.all_to_all(x, axes, 0, 0, tiled=True)  46.5 us
    ppermute x1, starting transfers between devices, local(): far_lon = lax.ppermute(to_far, LON, pairs(LON, False, True))  8.12 us
    pallas_call x4, Pallas kernels, call(): pl.pallas_call(kernel, out_shape=out_shape, in_specs=[vmem] * (len(operan...  7.32 us
    ppermute x1, starting transfers between devices, reduce_all(): lax.ppermute(own, 'core', swap)  4.58 us
    ppermute x1, starting transfers between devices, local(): far_lat = lax.ppermute(outer, LAT, pairs(LAT, False, False))  4.51 us
    ppermute x1, starting transfers between devices, local(): rest_lat = lax.ppermute(rest, LAT, pairs(LAT, False, False))  3.19 us
    unnamed x12, local copies, waits for them, and re-layouts  2.89 us
    pallas_call x2, Pallas kernels, place(): pl.pallas_call(functools.partial(place_kernel, own), out_shape=jax.ShapeD...  2.12 us
  transfers between devices with their start and end apart: 7, of which 3 were waited for; matrix products, arithmetic and copies ran while one was open for 2% of the time, Pallas kernels for 7%

profile of v9, /device:TPU:1, one launch (start us, length us, event | category | flops | bytes accessed | tf_op | source)
XLA Modules:
  0.0 84.0 jit_solution(10734316233994462970)
XLA Ops:
  0.6 0.0 copy-start
  0.6 0.0 copy-start.3
  0.7 1.4 %copy.11 = bf16[256,8,128]{0,2,1:T(8,128)(2,1)S(1)} copy(bf16[256,8,128]{2,1,0:T(8,128)(2,1)} %param.6) | data formatting | bytes 1048576 | tf_op args[1]
  2.1 4.5 %collective-permute-start.1 = (bf16[3,32,256]{2,1,0:T(8,128)(2,1)S(1)}, bf16[3,32,256]{2,1,0:T(8,128)(2,1)S(1)}, u32[]{:S(2)}, u32[]{:S(2)}) collective-permute-start(bf16[3,32,256]{2,1,0:T(8,128)(2,1)S(1)} %pad_maximum_fusion), channel_id=1, source_target_pairs={{16,32},{32,16},{48,64},{64,48},{80,96},{96,80},{112,128},{128,112... | collective-permute-start | bytes 147464 | tf_op jit(solution)/shard_map/ppermute | solution.py:269
  6.6 0.1 collective-permute-start
  6.8 0.0 copy-done.3
  6.8 0.1 dynamic_slice.6
  6.9 0.1 broadcast_compare_fusion
  6.9 0.0 copy-done
  6.9 0.2 constant_dynamic-slice_fusion
  7.2 0.0 copy-start.2
  7.2 0.5 copy.12
  7.7 0.5 collective-permute-done.near
  8.2 3.2 %collective-permute-start.2 = (bf16[3,96,256]{2,1,0:T(8,128)(2,1)S(1)}, bf16[3,96,256]{2,1,0:T(8,128)(2,1)S(1)}, u32[]{:S(2)}, u32[]{:S(2)}) collective-permute-start(bf16[3,96,256]{2,1,0:T(8,128)(2,1)S(1)} %slice.22), channel_id=1, source_target_pairs={{16,32},{32,16},{48,64},{64,48},{80,96},{96,80},{112,128},{128,112... | collective-permute-start | bytes 442376 | tf_op jit(solution)/shard_map/ppermute | solution.py:272
  11.4 0.0 collective-permute-done.1.far
  11.4 8.1 %collective-permute-start.3 = (bf16[14,16,256]{2,1,0:T(8,128)(2,1)S(1)}, bf16[14,16,256]{2,1,0:T(8,128)(2,1)S(1)}, u32[]{:S(2)}, u32[]{:S(2)}) collective-permute-start(bf16[14,16,256]{2,1,0:T(8,128)(2,1)S(1)} %get-tuple-element.24), channel_id=1, source_target_pairs={{0,15},{1,2},{2,1},{3,4},{4,3},{5,6},{6,5},{7,8},{8,7},{9,10},{10,... | collective-permute-start | bytes 344072 | tf_op jit(solution)/shard_map/ppermute | solution.py:275
  19.5 0.0 collective-permute-start.4
  19.6 0.0 copy-done.2
  19.6 0.1 copy.16
  19.7 0.0 collective-permute-done.2.rest
  19.7 0.0 copy-start.1
  19.7 3.4 %shard_map.68 = (bf16[8,288,512]{2,1,0:T(8,128)(2,1)S(1)}, bf16[256,512]{1,0:T(8,128)(2,1)S(1)}, bf16[9,8,64,256]{3,2,1,0:T(8,128)(2,1)S(1)}, f32[9,256,256]{2,1,0:T(8,128)S(1)}, bf16[14,2,48,256]{3,2,1,0:T(8,128)(2,1)S(1)}) custom-call(bf16[9,7,16,33]{3,2,1,0:T(8,128)(2,1)S(1)} %select_bitcast_fusion.taps, bf16[256,1024]{1,0:T(8,128)(2,1)S(1)} %bitcast.17, ...), custom_call_target="tpu_custom_call" | custom-call | flops 1000000000 | bytes 1000000 | tf_op jit(solution)/shard_map/pallas_call | solution.py:170
  23.1 0.0 collective-permute-done.3.far
  23.1 1.6 %collective-permute-done.4.near = bf16[14,16,256]{2,1,0:T(8,128)(2,1)S(1)} collective-permute-done((bf16[14,16,256]{2,1,0:T(8,128)(2,1)S(1)}, bf16[14,16,256]{2,1,0:T(8,128)(2,1)S(1)}, u32[]{:S(2)}, u32[]{:S(2)}) %collective-permute-start.4) | collective-permute-done | bytes 114720 | tf_op jit(solution)/shard_map/ppermute | solution.py:276
  24.7 0.0 copy-done.1
  24.7 2.5 %shard_map.70 = (bf16[9,8,64,256]{3,2,1,0:T(8,128)(2,1)S(1)}, f32[9,256,128]{2,1,0:T(8,128)S(1)}, f32[9,256,128]{2,1,0:T(8,128)S(1)}, bf16[9,256,256]{2,1,0:T(8,128)(2,1)S(1)}) custom-call(bf16[8,288,512]{2,1,0:T(8,128)(2,1)S(1)} %get-tuple-element.22.band, bf16[14,2,48,256]{3,2,1,0:T(8,128)(2,1)S(1)} %get-tuple-element.23.window, ...), custom_call_target="tpu_custom_call" | custom-call | flops 1000000000 | bytes 1000000 | tf_op jit(solution)/shard_map/pallas_call | solution.py:170
  27.2 0.1 select_convert_fusion
  27.3 0.1 collective-permute-start.5
  27.4 1.4 %shard_map.71 = bf16[256,1024]{1,0:T(8,128)(2,1)S(1)} custom-call(bf16[9,256,256]{2,1,0:T(8,128)(2,1)S(1)} %get-tuple-element.30.w_ref, bf16[9,8,64,256]{3,2,1,0:T(8,128)(2,1)S(1)} %get-tuple-element.31.mid_ref, bf16[9,8,64,256]{3,2,1,0:T(8,128)(2,1)S(1)} %get-tuple-element.32.edge_ref), custom_call_target="tpu_custom_call" | custom-call | flops 1000000000 | bytes 1000000 | tf_op jit(solution)/shard_map/pallas_call | solution.py:170
  28.8 0.6 collective-permute-done.5
  29.4 0.2 add_convert_fusion
  29.6 17.1 %all_to_all.15 = bf16[16,144,128]{2,1,0:T(8,128)(2,1)S(1)} all-to-all(bf16[16,144,128]{2,1,0:T(8,128)(2,1)S(1)} %bitcast.18), channel_id=1, replica_groups=mesh['y'=4,'x_lo'=2,'core'=2,'z'=8,'x_hi'=2] {'y','x_hi','x_lo'}, dimensions={0} | all-to-all | bytes 1179648 | tf_op jit(solution)/shard_map/all_to_all | solution.py:229
  46.7 0.1 reduce_sum.21
  46.8 16.5 %all_to_all.16 = bf16[8,144,128]{2,1,0:T(8,128)(2,1)S(1)} all-to-all(bf16[8,144,128]{2,1,0:T(8,128)(2,1)S(1)} %broadcast_in_dim.16), channel_id=1, replica_groups=mesh['y'=4,'x_lo'=2,'core'=2,'z'=8,'x_hi'=2] {'z'}, dimensions={0} | all-to-all | bytes 589824 | tf_op jit(solution)/shard_map/all_to_all | solution.py:229
  63.4 0.1 broadcast_in_dim.17
  63.5 12.9 %all_to_all.17 = bf16[16,144,128]{2,1,0:T(8,128)(2,1)S(1)} all-to-all(bf16[16,144,128]{2,1,0:T(8,128)(2,1)S(1)} %broadcast_in_dim.17), channel_id=1, replica_groups=mesh['y'=4,'x_lo'=2,'core'=2,'z'=8,'x_hi'=2] {'y','x_hi','x_lo'}, dimensions={0} | all-to-all | bytes 1179648 | tf_op jit(solution)/shard_map/all_to_all | solution.py:229
  76.4 4.6 %collective-permute-start.6 = (bf16[9,256,128]{2,1,0:T(8,128)(2,1)S(1)}, bf16[9,256,128]{2,1,0:T(8,128)(2,1)S(1)}, u32[]{:S(2)}, u32[]{:S(2)}) collective-permute-start(bf16[9,256,128]{2,1,0:T(8,128)(2,1)S(1)} %bitcast.14), channel_id=1, source_target_pairs={{0,16},{16,0},{1,17},{17,1},{2,18},{18,2},{3,19},{19,3},{4,20},{20... | collective-permute-start | bytes 1769480 | tf_op jit(solution)/shard_map/ppermute | solution.py:252
  80.9 0.9 %copy.14 = bf16[32,8,8,128]{3,2,1,0:T(8,128)(2,1)} copy(bf16[32,8,8,128]{3,1,2,0:T(8,128)(2,1)S(1)} %bitcast.16) | data formatting | bytes 1048576
  81.8 1.1 %shard_map.72.refs_0_ = f32[9,256,256]{2,1,0:T(8,128)} custom-call(bf16[9,256,128]{2,1,0:T(8,128)(2,1)S(1)} %bitcast.15), custom_call_target="tpu_custom_call" | custom-call | flops 1000000 | bytes 1000000 | tf_op jit(solution)/shard_map/pallas_call | solution.py:216
  82.9 0.0 collective-permute-done.6.half_ref
  82.9 1.1 %shard_map.73 = f32[9,256,256]{2,1,0:T(8,128)} custom-call(bf16[9,256,128]{2,1,0:T(8,128)(2,1)S(1)} %collective-permute-done.6.half_ref, f32[9,256,256]{2,1,0:T(8,128)} %shard_map.72.refs_0_), custom_call_target="tpu_custom_call", output_to_operand_aliasing={{}: (1, {})} | custom-call | flops 1000000 | bytes 1000000 | tf_op jit(solution)/shard_map/pallas_call | solution.py:216
  (10 shorter events, 0.2 us)
Async XLA Ops:
  0.6 6.3 %copy-start = (bf16[9,128,7,33]{1,2,3,0:T(8,128)(2,1)S(1)}, bf16[9,128,7,33]{1,2,3,0:T(8,128)(2,1)}, u32[]{:S(2)}) copy-start(bf16[9,128,7,33]{1,2,3,0:T(8,128)(2,1)} %param.8) | copy-start | bytes 1596676
  0.6 6.1 %copy-start.3 = (s32[128]{0:T(128)S(1)}, s32[128]{0:T(128)}, u32[]{:S(2)}) copy-start(s32[128]{0:T(128)} %param.9) | copy-start | bytes 1540
  2.1 9.2 %collective-permute-start.1 = (bf16[3,32,256]{2,1,0:T(8,128)(2,1)S(1)}, bf16[3,32,256]{2,1,0:T(8,128)(2,1)S(1)}, u32[]{:S(2)}, u32[]{:S(2)}) collective-permute-start(bf16[3,32,256]{2,1,0:T(8,128)(2,1)S(1)} %pad_maximum_fusion), channel_id=1, source_target_pairs={{16,32},{32,16},{48,64},{64,48},{80,96},{96,80},{112,128},{128,112... | collective-permute-start | bytes 147464 | tf_op jit(solution)/shard_map/ppermute | solution.py:269
  6.6 1.5 %collective-permute-start = (bf16[3,128,256]{2,1,0:T(8,128)(2,1)S(1)}, bf16[3,128,256]{2,1,0:T(8,128)(2,1)S(1)}, u32[]{:S(2)}, u32[]{:S(2)}) collective-permute-start(bf16[3,128,256]{2,1,0:T(8,128)(2,1)S(1)} %get-tuple-element.38), channel_id=1, source_target_pairs={{0,16},{16,0},{32,48},{48,32},{64,80},{80,64},{96,112},{112,96},{1... | collective-permute-start | bytes 589832 | tf_op jit(solution)/shard_map/ppermute | solution.py:270
  7.2 12.4 %copy-start.2 = (bf16[256,8,128]{2,1,0:T(8,128)(2,1)S(1)}, bf16[256,8,128]{2,1,0:T(8,128)(2,1)}, u32[]{:S(2)}) copy-start(bf16[256,8,128]{2,1,0:T(8,128)(2,1)} %param.5) | copy-start | bytes 1572868
  8.2 11.5 %collective-permute-start.2 = (bf16[3,96,256]{2,1,0:T(8,128)(2,1)S(1)}, bf16[3,96,256]{2,1,0:T(8,128)(2,1)S(1)}, u32[]{:S(2)}, u32[]{:S(2)}) collective-permute-start(bf16[3,96,256]{2,1,0:T(8,128)(2,1)S(1)} %slice.22), channel_id=1, source_target_pairs={{16,32},{32,16},{48,64},{64,48},{80,96},{96,80},{112,128},{128,112... | collective-permute-start | bytes 442376 | tf_op jit(solution)/shard_map/ppermute | solution.py:272
  11.4 11.7 %collective-permute-start.3 = (bf16[14,16,256]{2,1,0:T(8,128)(2,1)S(1)}, bf16[14,16,256]{2,1,0:T(8,128)(2,1)S(1)}, u32[]{:S(2)}, u32[]{:S(2)}) collective-permute-start(bf16[14,16,256]{2,1,0:T(8,128)(2,1)S(1)} %get-tuple-element.24), channel_id=1, source_target_pairs={{0,15},{1,2},{2,1},{3,4},{4,3},{5,6},{6,5},{7,8},{8,7},{9,10},{10,... | collective-permute-start | bytes 344072 | tf_op jit(solution)/shard_map/ppermute | solution.py:275
  19.5 5.1 %collective-permute-start.4 = (bf16[14,16,256]{2,1,0:T(8,128)(2,1)S(1)}, bf16[14,16,256]{2,1,0:T(8,128)(2,1)S(1)}, u32[]{:S(2)}, u32[]{:S(2)}) collective-permute-start(bf16[14,16,256]{2,1,0:T(8,128)(2,1)S(1)} %get-tuple-element.25), channel_id=1, source_target_pairs={{0,1},{1,0},{2,3},{3,2},{4,5},{5,4},{6,7},{7,6},{8,9},{9,8},{10,11... | collective-permute-start | bytes 344072 | tf_op jit(solution)/shard_map/ppermute | solution.py:276
  19.7 5.0 %copy-start.1 = (bf16[9,256,256]{2,1,0:T(8,128)(2,1)S(1)}, bf16[9,256,256]{2,1,0:T(8,128)(2,1)}, u32[]{:S(2)}) copy-start(bf16[9,256,256]{2,1,0:T(8,128)(2,1)} %w_ref.1) | copy-start | bytes 3538948
  27.3 2.1 %collective-permute-start.5 = (bf16[9,256,128]{2,1,0:T(8,128)(2,1)S(1)}, bf16[9,256,128]{2,1,0:T(8,128)(2,1)S(1)}, u32[]{:S(2)}, u32[]{:S(2)}) collective-permute-start(bf16[9,256,128]{2,1,0:T(8,128)(2,1)S(1)} %select_convert_fusion), channel_id=1, source_target_pairs={{0,16},{16,0},{1,17},{17,1},{2,18},{18,2},{3,19},{19,3},{4,20},{20... | collective-permute-start | bytes 1769480 | tf_op jit(solution)/shard_map/ppermute | solution.py:244
  76.4 6.5 %collective-permute-start.6 = (bf16[9,256,128]{2,1,0:T(8,128)(2,1)S(1)}, bf16[9,256,128]{2,1,0:T(8,128)(2,1)S(1)}, u32[]{:S(2)}, u32[]{:S(2)}) collective-permute-start(bf16[9,256,128]{2,1,0:T(8,128)(2,1)S(1)} %bitcast.14), channel_id=1, source_target_pairs={{0,16},{16,0},{1,17},{17,1},{2,18},{18,2},{3,19},{19,3},{4,20},{20... | collective-permute-start | bytes 1769480 | tf_op jit(solution)/shard_map/ppermute | solution.py:252

commit v10 on v9

--- a/solution.py
+++ b/solution.py
@@ -268,8 +268,7 @@
     outer = jnp.concatenate([to_far[:, :side], to_far[:, lon_dev - side :]], axis=1)
     far_lat = lax.ppermute(outer, LAT, pairs(LAT, False, False))
     near_lat = lax.ppermute(to_near, LAT, pairs(LAT, True, False))
-    rest, near_lat = lax.optimization_barrier((to_far[:, side : lon_dev - side], near_lat))
-    rest_lat = lax.ppermute(rest, LAT, pairs(LAT, False, False))
+    rest_lat = lax.ppermute(to_far[:, side : lon_dev - side], LAT, pairs(LAT, False, False))
     rim = shape((near, side, channels), bf16)
     to_far, to_near = call(rim_kernel, (rim, rim), (main, near_lat, far_lat), flops=10**6, mib=4)
     far_lon = lax.ppermute(to_far, LON, pairs(LON, False, True))

time: 84.2 us -> 83.2 us (0.988)
  blocking collectives: 46.5 us -> 45.1 us
    all_to_all x3, blocking collectives: 46.5 us -> 45.1 us  [all_to_all(): return lax.all_to_all(x, axes, 0, 0, tiled=True)]
    ppermute x1, starting transfers between devices: 3.19 us -> 1.92 us  [local(): lax.ppermute(to_far[:, side:lon_dev - side], LAT, pairs(LAT, False, False))]
    ppermute x1, starting transfers between devices: 0.09 us -> 1.35 us  [reduce_all(): lax.ppermute(send, 'core', swap)]
where the time goes in v10:
time: 83.2 us; the launch traced here: 82.9 us
  blocking collectives  45.1 us (54%)
  starting transfers between devices  20.7 us (25%)
  Pallas kernels  9.4 us (11%)
  local copies, waits for them, and re-layouts  3.33 us (4%)
  waiting for transfers between devices  2.94 us (4%)
  between operations  0.9 us (1%)
    all_to_all x3, blocking collectives, all_to_all(): return lax.all_to_all(x, axes, 0, 0, tiled=True)  45.1 us
    ppermute x1, starting transfers between devices, local(): far_lon = lax.ppermute(to_far, LON, pairs(LON, False, True))  8.09 us
    pallas_call x4, Pallas kernels, call(): pl.pallas_call(kernel, out_shape=out_shape, in_specs=[vmem] * (len(operan...  7.29 us
    ppermute x1, starting transfers between devices, reduce_all(): lax.ppermute(own, 'core', swap)  4.68 us
    ppermute x1, starting transfers between devices, local(): far_lat = lax.ppermute(outer, LAT, pairs(LAT, False, False))  4.51 us
    unnamed x12, local copies, waits for them, and re-layouts  2.89 us
    ppermute x1, waiting for transfers between devices, local(): near_lon = lax.ppermute(to_near, LON, pairs(LON, True, True))  2.23 us
    pallas_call x2, Pallas kernels, place(): pl.pallas_call(functools.partial(place_kernel, own), out_shape=jax.ShapeD...  2.12 us
  transfers between devices with their start and end apart: 7, of which 3 were waited for; matrix products, arithmetic and copies ran while one was open for 2% of the time, Pallas kernels for 7%

profile of v10, /device:TPU:1, one launch (start us, length us, event | category | flops | bytes accessed | tf_op | source)
XLA Modules:
  0.0 82.9 jit_solution(497077647197557795)
XLA Ops:
  0.6 0.0 copy-start
  0.7 0.0 copy-start.3
  0.7 1.4 %copy.11 = bf16[256,8,128]{0,2,1:T(8,128)(2,1)S(1)} copy(bf16[256,8,128]{2,1,0:T(8,128)(2,1)} %param.6) | data formatting | bytes 1048576 | tf_op args[1]
  2.1 4.5 %collective-permute-start.1 = (bf16[3,32,256]{2,1,0:T(8,128)(2,1)S(1)}, bf16[3,32,256]{2,1,0:T(8,128)(2,1)S(1)}, u32[]{:S(2)}, u32[]{:S(2)}) collective-permute-start(bf16[3,32,256]{2,1,0:T(8,128)(2,1)S(1)} %pad_maximum_fusion), channel_id=1, source_target_pairs={{16,32},{32,16},{48,64},{64,48},{80,96},{96,80},{112,128},{128,112... | collective-permute-start | bytes 147464 | tf_op jit(solution)/shard_map/ppermute | solution.py:269
  6.7 1.9 %collective-permute-start.2 = (bf16[3,96,256]{2,1,0:T(8,128)(2,1)S(1)}, bf16[3,96,256]{2,1,0:T(8,128)(2,1)S(1)}, u32[]{:S(2)}, u32[]{:S(2)}) collective-permute-start(bf16[3,96,256]{2,1,0:T(8,128)(2,1)S(1)} %slice.24), channel_id=1, source_target_pairs={{16,32},{32,16},{48,64},{64,48},{80,96},{96,80},{112,128},{128,112... | collective-permute-start | bytes 442376 | tf_op jit(solution)/shard_map/ppermute | solution.py:271
  8.6 0.1 collective-permute-start
  8.7 0.0 copy-done.3
  8.7 0.1 dynamic_slice.6
  8.8 0.1 broadcast_compare_fusion
  8.9 0.0 copy-done
  8.9 0.2 constant_dynamic-slice_fusion
  9.1 0.0 copy-start.2
  9.1 0.5 copy.12
  9.6 0.0 collective-permute-done.1.far
  9.6 0.5 collective-permute-done.near
  10.1 8.1 %collective-permute-start.3 = (bf16[14,16,256]{2,1,0:T(8,128)(2,1)S(1)}, bf16[14,16,256]{2,1,0:T(8,128)(2,1)S(1)}, u32[]{:S(2)}, u32[]{:S(2)}) collective-permute-start(bf16[14,16,256]{2,1,0:T(8,128)(2,1)S(1)} %get-tuple-element.20), channel_id=1, source_target_pairs={{0,15},{1,2},{2,1},{3,4},{4,3},{5,6},{6,5},{7,8},{8,7},{9,10},{10,... | collective-permute-start | bytes 344072 | tf_op jit(solution)/shard_map/ppermute | solution.py:274
  18.2 0.0 collective-permute-start.4
  18.3 0.0 copy-done.2
  18.3 0.1 copy.16
  18.4 0.0 collective-permute-done.2.rest
  18.4 0.0 copy-start.1
  18.4 3.4 %shard_map.68 = (bf16[8,288,512]{2,1,0:T(8,128)(2,1)S(1)}, bf16[256,512]{1,0:T(8,128)(2,1)S(1)}, bf16[9,8,64,256]{3,2,1,0:T(8,128)(2,1)S(1)}, f32[9,256,256]{2,1,0:T(8,128)S(1)}, bf16[14,2,48,256]{3,2,1,0:T(8,128)(2,1)S(1)}) custom-call(bf16[9,7,16,33]{3,2,1,0:T(8,128)(2,1)S(1)} %select_bitcast_fusion.taps, bf16[256,1024]{1,0:T(8,128)(2,1)S(1)} %bitcast.17, ...), custom_call_target="tpu_custom_call" | custom-call | flops 1000000000 | bytes 1000000 | tf_op jit(solution)/shard_map/pallas_call | solution.py:170
  21.8 0.0 collective-permute-done.3.far
  21.8 2.2 %collective-permute-done.4.near = bf16[14,16,256]{2,1,0:T(8,128)(2,1)S(1)} collective-permute-done((bf16[14,16,256]{2,1,0:T(8,128)(2,1)S(1)}, bf16[14,16,256]{2,1,0:T(8,128)(2,1)S(1)}, u32[]{:S(2)}, u32[]{:S(2)}) %collective-permute-start.4) | collective-permute-done | bytes 114720 | tf_op jit(solution)/shard_map/ppermute | solution.py:275
  24.0 0.0 copy-done.1
  24.0 2.5 %shard_map.70 = (bf16[9,8,64,256]{3,2,1,0:T(8,128)(2,1)S(1)}, f32[9,256,128]{2,1,0:T(8,128)S(1)}, f32[9,256,128]{2,1,0:T(8,128)S(1)}, bf16[9,256,256]{2,1,0:T(8,128)(2,1)S(1)}) custom-call(bf16[8,288,512]{2,1,0:T(8,128)(2,1)S(1)} %get-tuple-element.18.band, bf16[14,2,48,256]{3,2,1,0:T(8,128)(2,1)S(1)} %get-tuple-element.19.window, ...), custom_call_target="tpu_custom_call" | custom-call | flops 1000000000 | bytes 1000000 | tf_op jit(solution)/shard_map/pallas_call | solution.py:170
  26.5 0.1 select_convert_fusion
  26.6 1.4 %collective-permute-start.5 = (bf16[9,256,128]{2,1,0:T(8,128)(2,1)S(1)}, bf16[9,256,128]{2,1,0:T(8,128)(2,1)S(1)}, u32[]{:S(2)}, u32[]{:S(2)}) collective-permute-start(bf16[9,256,128]{2,1,0:T(8,128)(2,1)S(1)} %select_convert_fusion), channel_id=1, source_target_pairs={{0,16},{16,0},{1,17},{17,1},{2,18},{18,2},{3,19},{19,3},{4,20},{20... | collective-permute-start | bytes 1769480 | tf_op jit(solution)/shard_map/ppermute | solution.py:244
  28.0 1.4 %shard_map.71 = bf16[256,1024]{1,0:T(8,128)(2,1)S(1)} custom-call(bf16[9,256,256]{2,1,0:T(8,128)(2,1)S(1)} %get-tuple-element.26.w_ref, bf16[9,8,64,256]{3,2,1,0:T(8,128)(2,1)S(1)} %get-tuple-element.27.mid_ref, bf16[9,8,64,256]{3,2,1,0:T(8,128)(2,1)S(1)} %get-tuple-element.28.edge_ref), custom_call_target="tpu_custom_call" | custom-call | flops 1000000000 | bytes 1000000 | tf_op jit(solution)/shard_map/pallas_call | solution.py:170
  29.4 0.2 collective-permute-done.5
  29.6 0.2 add_convert_fusion
  29.8 16.8 %all_to_all.15 = bf16[16,144,128]{2,1,0:T(8,128)(2,1)S(1)} all-to-all(bf16[16,144,128]{2,1,0:T(8,128)(2,1)S(1)} %bitcast.18), channel_id=1, replica_groups=mesh['y'=4,'x_lo'=2,'core'=2,'z'=8,'x_hi'=2] {'y','x_hi','x_lo'}, dimensions={0} | all-to-all | bytes 1179648 | tf_op jit(solution)/shard_map/all_to_all | solution.py:229
  46.7 0.1 reduce_sum.21
  46.8 14.7 %all_to_all.16 = bf16[8,144,128]{2,1,0:T(8,128)(2,1)S(1)} all-to-all(bf16[8,144,128]{2,1,0:T(8,128)(2,1)S(1)} %broadcast_in_dim.16), channel_id=1, replica_groups=mesh['y'=4,'x_lo'=2,'core'=2,'z'=8,'x_hi'=2] {'z'}, dimensions={0} | all-to-all | bytes 589824 | tf_op jit(solution)/shard_map/all_to_all | solution.py:229
  61.6 0.1 broadcast_in_dim.17
  61.7 13.5 %all_to_all.17 = bf16[16,144,128]{2,1,0:T(8,128)(2,1)S(1)} all-to-all(bf16[16,144,128]{2,1,0:T(8,128)(2,1)S(1)} %broadcast_in_dim.17), channel_id=1, replica_groups=mesh['y'=4,'x_lo'=2,'core'=2,'z'=8,'x_hi'=2] {'y','x_hi','x_lo'}, dimensions={0} | all-to-all | bytes 1179648 | tf_op jit(solution)/shard_map/all_to_all | solution.py:229
  75.2 4.7 %collective-permute-start.6 = (bf16[9,256,128]{2,1,0:T(8,128)(2,1)S(1)}, bf16[9,256,128]{2,1,0:T(8,128)(2,1)S(1)}, u32[]{:S(2)}, u32[]{:S(2)}) collective-permute-start(bf16[9,256,128]{2,1,0:T(8,128)(2,1)S(1)} %bitcast.14), channel_id=1, source_target_pairs={{0,16},{16,0},{1,17},{17,1},{2,18},{18,2},{3,19},{19,3},{4,20},{20... | collective-permute-start | bytes 1769480 | tf_op jit(solution)/shard_map/ppermute | solution.py:252
  79.9 0.9 %copy.14 = bf16[32,8,8,128]{3,2,1,0:T(8,128)(2,1)} copy(bf16[32,8,8,128]{3,1,2,0:T(8,128)(2,1)S(1)} %bitcast.16) | data formatting | bytes 1048576
  80.8 1.1 %shard_map.72.refs_0_ = f32[9,256,256]{2,1,0:T(8,128)} custom-call(bf16[9,256,128]{2,1,0:T(8,128)(2,1)S(1)} %bitcast.15), custom_call_target="tpu_custom_call" | custom-call | flops 1000000 | bytes 1000000 | tf_op jit(solution)/shard_map/pallas_call | solution.py:216
  81.9 0.0 collective-permute-done.6.half_ref
  81.9 1.1 %shard_map.73 = f32[9,256,256]{2,1,0:T(8,128)} custom-call(bf16[9,256,128]{2,1,0:T(8,128)(2,1)S(1)} %collective-permute-done.6.half_ref, f32[9,256,256]{2,1,0:T(8,128)} %shard_map.72.refs_0_), custom_call_target="tpu_custom_call", output_to_operand_aliasing={{}: (1, {})} | custom-call | flops 1000000 | bytes 1000000 | tf_op jit(solution)/shard_map/pallas_call | solution.py:216
  (10 shorter events, 0.2 us)
Async XLA Ops:
  0.6 8.3 %copy-start = (bf16[9,128,7,33]{1,2,3,0:T(8,128)(2,1)S(1)}, bf16[9,128,7,33]{1,2,3,0:T(8,128)(2,1)}, u32[]{:S(2)}) copy-start(bf16[9,128,7,33]{1,2,3,0:T(8,128)(2,1)} %param.8) | copy-start | bytes 1596676
  0.7 8.1 %copy-start.3 = (s32[128]{0:T(128)S(1)}, s32[128]{0:T(128)}, u32[]{:S(2)}) copy-start(s32[128]{0:T(128)} %param.9) | copy-start | bytes 1540
  2.1 7.5 %collective-permute-start.1 = (bf16[3,32,256]{2,1,0:T(8,128)(2,1)S(1)}, bf16[3,32,256]{2,1,0:T(8,128)(2,1)S(1)}, u32[]{:S(2)}, u32[]{:S(2)}) collective-permute-start(bf16[3,32,256]{2,1,0:T(8,128)(2,1)S(1)} %pad_maximum_fusion), channel_id=1, source_target_pairs={{16,32},{32,16},{48,64},{64,48},{80,96},{96,80},{112,128},{128,112... | collective-permute-start | bytes 147464 | tf_op jit(solution)/shard_map/ppermute | solution.py:269
  6.7 11.7 %collective-permute-start.2 = (bf16[3,96,256]{2,1,0:T(8,128)(2,1)S(1)}, bf16[3,96,256]{2,1,0:T(8,128)(2,1)S(1)}, u32[]{:S(2)}, u32[]{:S(2)}) collective-permute-start(bf16[3,96,256]{2,1,0:T(8,128)(2,1)S(1)} %slice.24), channel_id=1, source_target_pairs={{16,32},{32,16},{48,64},{64,48},{80,96},{96,80},{112,128},{128,112... | collective-permute-start | bytes 442376 | tf_op jit(solution)/shard_map/ppermute | solution.py:271
  8.6 1.5 %collective-permute-start = (bf16[3,128,256]{2,1,0:T(8,128)(2,1)S(1)}, bf16[3,128,256]{2,1,0:T(8,128)(2,1)S(1)}, u32[]{:S(2)}, u32[]{:S(2)}) collective-permute-start(bf16[3,128,256]{2,1,0:T(8,128)(2,1)S(1)} %get-tuple-element.35), channel_id=1, source_target_pairs={{0,16},{16,0},{32,48},{48,32},{64,80},{80,64},{96,112},{112,96},{1... | collective-permute-start | bytes 589832 | tf_op jit(solution)/shard_map/ppermute | solution.py:270
  9.1 9.1 %copy-start.2 = (bf16[256,8,128]{2,1,0:T(8,128)(2,1)S(1)}, bf16[256,8,128]{2,1,0:T(8,128)(2,1)}, u32[]{:S(2)}) copy-start(bf16[256,8,128]{2,1,0:T(8,128)(2,1)} %param.5) | copy-start | bytes 1572868
  10.1 11.7 %collective-permute-start.3 = (bf16[14,16,256]{2,1,0:T(8,128)(2,1)S(1)}, bf16[14,16,256]{2,1,0:T(8,128)(2,1)S(1)}, u32[]{:S(2)}, u32[]{:S(2)}) collective-permute-start(bf16[14,16,256]{2,1,0:T(8,128)(2,1)S(1)} %get-tuple-element.20), channel_id=1, source_target_pairs={{0,15},{1,2},{2,1},{3,4},{4,3},{5,6},{6,5},{7,8},{8,7},{9,10},{10,... | collective-permute-start | bytes 344072 | tf_op jit(solution)/shard_map/ppermute | solution.py:274
  18.2 5.8 %collective-permute-start.4 = (bf16[14,16,256]{2,1,0:T(8,128)(2,1)S(1)}, bf16[14,16,256]{2,1,0:T(8,128)(2,1)S(1)}, u32[]{:S(2)}, u32[]{:S(2)}) collective-permute-start(bf16[14,16,256]{2,1,0:T(8,128)(2,1)S(1)} %get-tuple-element.21), channel_id=1, source_target_pairs={{0,1},{1,0},{2,3},{3,2},{4,5},{5,4},{6,7},{7,6},{8,9},{9,8},{10,11... | collective-permute-start | bytes 344072 | tf_op jit(solution)/shard_map/ppermute | solution.py:275
  18.4 5.7 %copy-start.1 = (bf16[9,256,256]{2,1,0:T(8,128)(2,1)S(1)}, bf16[9,256,256]{2,1,0:T(8,128)(2,1)}, u32[]{:S(2)}) copy-start(bf16[9,256,256]{2,1,0:T(8,128)(2,1)} %w_ref.1) | copy-start | bytes 3538948
  26.6 3.0 %collective-permute-start.5 = (bf16[9,256,128]{2,1,0:T(8,128)(2,1)S(1)}, bf16[9,256,128]{2,1,0:T(8,128)(2,1)S(1)}, u32[]{:S(2)}, u32[]{:S(2)}) collective-permute-start(bf16[9,256,128]{2,1,0:T(8,128)(2,1)S(1)} %select_convert_fusion), channel_id=1, source_target_pairs={{0,16},{16,0},{1,17},{17,1},{2,18},{18,2},{3,19},{19,3},{4,20},{20... | collective-permute-start | bytes 1769480 | tf_op jit(solution)/shard_map/ppermute | solution.py:244
  75.2 6.6 %collective-permute-start.6 = (bf16[9,256,128]{2,1,0:T(8,128)(2,1)S(1)}, bf16[9,256,128]{2,1,0:T(8,128)(2,1)S(1)}, u32[]{:S(2)}, u32[]{:S(2)}) collective-permute-start(bf16[9,256,128]{2,1,0:T(8,128)(2,1)S(1)} %bitcast.14), channel_id=1, source_target_pairs={{0,16},{16,0},{1,17},{17,1},{2,18},{18,2},{3,19},{19,3},{4,20},{20... | collective-permute-start | bytes 1769480 | tf_op jit(solution)/shard_map/ppermute | solution.py:252

commit v11 on v10

--- a/solution.py
+++ b/solution.py
@@ -43,26 +43,36 @@
     return jnp.transpose(table, (0, 2, 1, 3))
 
 
-def rim_kernel(main, near, far, second, first):
+def own_rows(half, lat_dev):
+    return (slice(half, half + lat_dev), slice(0, half)), (slice(0, lat_dev), slice(lat_dev, None))
+
+
+def rim_kernel(main, far, second, first):
     lat_dev, lon_dev, _ = main.shape
-    half, side = near.shape[0], first.shape[1]
+    half, side = far.shape[0], first.shape[1]
     odd_lon, odd_lat = parity(LON), parity(LAT)
-    for even in (0, 1):
-        last = lon_dev - side
-
-        @pl.when(odd_lon != even)
+    last = lon_dev - side
+    for odd, (own, other) in enumerate(own_rows(half, lat_dev)):
+        for even in (0, 1):
+
+            @pl.when((odd_lon != even) & (odd_lat == odd))
+            def _():
+                for ref, at in ((first, last if even else 0), (second, 0 if even else last)):
+                    outer = slice(side, 2 * side) if at else slice(0, side)
+                    ref[own] = main[:, at : at + side, :]
+                    ref[other] = far[:, outer, :]
+
+
+def corner_kernel(far, near, out):
+    half, side = out.shape[0], far.shape[1]
+    lat_dev = far.shape[0] - half
+    odd_lat = parity(LAT)
+    for odd, rows in enumerate((slice(lat_dev, None), slice(0, half))):
+
+        @pl.when(odd_lat == odd)
         def _():
-            for ref, at in ((first, last if even else 0), (second, 0 if even else last)):
-                ref[half : half + lat_dev] = main[:, at : at + side, :]
-                own = slice(at, at + side)
-                outer = slice(side, 2 * side) if at else slice(0, side)
-                for upper in (0, 1):
-
-                    @pl.when(odd_lat != upper)
-                    def _():
-                        above, below = slice(0, half), slice(half + lat_dev, None)
-                        ref[above if upper else below] = far[:, outer, :]
-                        ref[below if upper else above] = near[:, own, :]
+            out[:, :side, :] = far[rows]
+            out[:, side:, :] = near[rows]
 
 
 def convolve(band, ext, place, q_ref):
@@ -141,20 +151,25 @@
         total[k] = jnp.dot(f_mid[...], cells, preferred_element_type=f32)
 
 
-def edge_kernel(band, window, far, near, f_ref, total, w_ref, q_ref, low, high, w_out, ext, sem):
+def edge_kernel(band, window, far, near, corner, f_ref, total, w_ref, q_ref, low, high, w_out, ext, sem):
     fetch = pltpu.make_async_copy(w_ref, w_out, sem)
     fetch.start()
     channels = window.shape[3]
     side, inner = near.shape[1], window.shape[2]
     ext[:, 0, :inner, :] = window[:, 0]
     ext[:, 1, side:, :] = window[:, 1]
-    odd_lon = parity(LON)
-    for even in (0, 1):
-
-        @pl.when(odd_lon != even)
-        def _():
-            ext[:, 0, inner:, :] = (near if even else far)[...]
-            ext[:, 1, :side, :] = (far if even else near)[...]
+    odd_lon, odd_lat = parity(LON), parity(LAT)
+    half, held = corner.shape[0], far.shape[0]
+    for odd, (rows, rest) in enumerate(((slice(0, held), slice(held, None)), (slice(half, None), slice(0, half)))):
+        for even in (0, 1):
+
+            @pl.when((odd_lon != even) & (odd_lat == odd))
+            def _():
+                right, left = (near, far) if even else (far, near)
+                ext[rows, 0, inner:, :] = right[...]
+                ext[rows, 1, :side, :] = left[...]
+                ext[rest, 0, inner:, :] = corner[:, side:] if even else corner[:, :side]
+                ext[rest, 1, :side, :] = corner[:, :side] if even else corner[:, side:]
 
     convolve(band, ext, lambda j: (j,), q_ref)
     for k in range(q_ref.shape[0]):
@@ -267,12 +282,13 @@
     to_near, to_far = jnp.where(upper, last, first), jnp.where(upper, first, last)
     outer = jnp.concatenate([to_far[:, :side], to_far[:, lon_dev - side :]], axis=1)
     far_lat = lax.ppermute(outer, LAT, pairs(LAT, False, False))
+    rest_lat = lax.ppermute(to_far[:, side : lon_dev - side], LAT, pairs(LAT, False, False))
+    rim = shape((near - half, side, channels), bf16)
+    second, first = call(rim_kernel, (rim, rim), (main, far_lat), flops=10**6, mib=4)
+    to_near, second, first = lax.optimization_barrier((to_near, second, first))
+    far_lon = lax.ppermute(second, LON, pairs(LON, False, True))
+    near_lon = lax.ppermute(first, LON, pairs(LON, True, True))
     near_lat = lax.ppermute(to_near, LAT, pairs(LAT, True, False))
-    rest_lat = lax.ppermute(to_far[:, side : lon_dev - side], LAT, pairs(LAT, False, False))
-    rim = shape((near, side, channels), bf16)
-    to_far, to_near = call(rim_kernel, (rim, rim), (main, near_lat, far_lat), flops=10**6, mib=4)
-    far_lon = lax.ppermute(to_far, LON, pairs(LON, False, True))
-    near_lon = lax.ppermute(to_near, LON, pairs(LON, True, True))
     taps = tap_rows(basis_table, lon_reach, start, held)
     q_shape = shape((basis_count, lat_dev, wide, channels), bf16)
     columns = shape((channels, lat_dev * wide), bf16)
@@ -293,10 +309,13 @@
             pltpu.VMEM((near, lon_dev, channels), bf16),
         ],
     )
+    far_lon, near_lon, total = lax.optimization_barrier((far_lon, near_lon, total))
+    corner = call(corner_kernel, shape((half, 2 * side, channels), bf16), (far_lon, near_lon), flops=10**6, mib=4)
+    corner = lax.ppermute(corner, LAT, pairs(LAT, True, False))
     q_edge, low, high, weight = call(
         edge_kernel,
         (q_shape, part, part, shape(weight.shape, bf16)),
-        (band, window, far_lon, near_lon, f_edge, total, weight),
+        (band, window, far_lon, near_lon, corner, f_edge, total, weight),
         [pltpu.VMEM((near, 2, wide, channels), bf16), pltpu.SemaphoreType.DMA],
         hbm=1,
     )

time: 83.2 us -> 83.6 us (level)
  starting transfers between devices: 20.7 us -> 21.8 us
    ppermute x2 -> x3, starting transfers between devices: 8.09 us -> 10 us  [the longest x1 8.08 us: local(): far_lon = lax.ppermute(second, LON, pairs(LON, False, True))]
    ppermute x1, starting transfers between devices: 1.35 us -> 0.44 us  [reduce_all(): lax.ppermute(send, 'core', swap)]
    ppermute x2 -> x3, waiting for transfers between devices: 2.23 us -> 2.33 us  [the longest x1 1.44 us: local(): near_lon = lax.ppermute(first, LON, pairs(LON, True, True))]
    pallas_call x4 -> x5, Pallas kernels: 7.29 us -> 7.33 us  [call(): pl.pallas_call(kernel, out_shape=out_shape, in_specs=[vmem] * (len(operan...]
  transfers between devices with their start and end apart: 7 -> 8, of which waited for: 3 -> 3; matrix products, arithmetic and copies ran while one was open for 2% -> 2% of each run, Pallas kernels for 7% -> 7%
where the time goes in v11:
time: 83.6 us; the launch traced here: 83.3 us
  blocking collectives  44.7 us (53%)
  starting transfers between devices  21.8 us (26%)
  Pallas kernels  9.44 us (11%)
  local copies, waits for them, and re-layouts  3.33 us (4%)
  waiting for transfers between devices  2.57 us (3%)
  between operations  0.9 us (1%)
    all_to_all x3, blocking collectives, all_to_all(): return lax.all_to_all(x, axes, 0, 0, tiled=True)  44.7 us
    ppermute x1, starting transfers between devices, local(): far_lon = lax.ppermute(second, LON, pairs(LON, False, True))  8.08 us
    pallas_call x5, Pallas kernels, call(): pl.pallas_call(kernel, out_shape=out_shape, in_specs=[vmem] * (len(operan...  7.33 us
    ppermute x1, starting transfers between devices, reduce_all(): lax.ppermute(own, 'core', swap)  4.69 us
    ppermute x1, starting transfers between devices, local(): far_lat = lax.ppermute(outer, LAT, pairs(LAT, False, False))  4.64 us
    unnamed x12, local copies, waits for them, and re-layouts  2.89 us
    pallas_call x2, Pallas kernels, place(): pl.pallas_call(functools.partial(place_kernel, own), out_shape=jax.ShapeD...  2.12 us
    ppermute x1, starting transfers between devices, local(): lax.ppermute(to_far[:, side:lon_dev - side], LAT, pairs(LAT, False, False))  1.92 us
  transfers between devices with their start and end apart: 8, of which 3 were waited for; matrix products, arithmetic and copies ran while one was open for 2% of the time, Pallas kernels for 7%

profile of v11, /device:TPU:1, one launch (start us, length us, event | category | flops | bytes accessed | tf_op | source)
XLA Modules:
  0.0 83.3 jit_solution(6138482941171218532)
XLA Ops:
  0.6 0.0 copy-start
  0.7 0.0 copy-start.3
  0.7 1.4 %copy.11 = bf16[256,8,128]{0,2,1:T(8,128)(2,1)S(1)} copy(bf16[256,8,128]{2,1,0:T(8,128)(2,1)} %param.6) | data formatting | bytes 1048576 | tf_op args[1]
  2.1 0.0 copy-start.2
  2.1 4.6 %collective-permute-start = (bf16[3,32,256]{2,1,0:T(8,128)(2,1)S(1)}, bf16[3,32,256]{2,1,0:T(8,128)(2,1)S(1)}, u32[]{:S(2)}, u32[]{:S(2)}) collective-permute-start(bf16[3,32,256]{2,1,0:T(8,128)(2,1)S(1)} %pad_maximum_fusion), channel_id=1, source_target_pairs={{16,32},{32,16},{48,64},{64,48},{80,96},{96,80},{112,128},{128,112... | collective-permute-start | bytes 147464 | tf_op jit(solution)/shard_map/ppermute | solution.py:284
  6.8 1.9 %collective-permute-start.2 = (bf16[3,96,256]{2,1,0:T(8,128)(2,1)S(1)}, bf16[3,96,256]{2,1,0:T(8,128)(2,1)S(1)}, u32[]{:S(2)}, u32[]{:S(2)}) collective-permute-start(bf16[3,96,256]{2,1,0:T(8,128)(2,1)S(1)} %slice.24), channel_id=1, source_target_pairs={{16,32},{32,16},{48,64},{64,48},{80,96},{96,80},{112,128},{128,112... | collective-permute-start | bytes 442376 | tf_op jit(solution)/shard_map/ppermute | solution.py:285
  8.8 0.0 copy-done.3
  8.8 0.1 dynamic_slice.6
  8.8 0.1 broadcast_compare_fusion
  8.9 0.0 copy-done
  8.9 0.2 constant_dynamic-slice_fusion
  9.2 0.0 copy-done.2
  9.2 0.1 copy.16
  9.3 0.5 copy.12
  9.8 0.0 collective-permute-done.far
  9.8 0.1 collective-permute-start.1
  10.0 8.1 %collective-permute-start.3 = (bf16[11,16,256]{2,1,0:T(8,128)(2,1)S(1)}, bf16[11,16,256]{2,1,0:T(8,128)(2,1)S(1)}, u32[]{:S(2)}, u32[]{:S(2)}) collective-permute-start(bf16[11,16,256]{2,1,0:T(8,128)(2,1)S(1)} %get-tuple-element.29), channel_id=1, source_target_pairs={{0,15},{1,2},{2,1},{3,4},{4,3},{5,6},{6,5},{7,8},{8,7},{9,10},{10,... | collective-permute-start | bytes 270344 | tf_op jit(solution)/shard_map/ppermute | solution.py:289
  18.0 0.0 collective-permute-start.4
  18.0 0.0 collective-permute-done.2.rest
  18.0 0.0 collective-permute-done.1.near
  18.1 0.0 copy-start.1
  18.1 3.4 %shard_map.69 = (bf16[8,288,512]{2,1,0:T(8,128)(2,1)S(1)}, bf16[256,512]{1,0:T(8,128)(2,1)S(1)}, bf16[9,8,64,256]{3,2,1,0:T(8,128)(2,1)S(1)}, f32[9,256,256]{2,1,0:T(8,128)S(1)}, bf16[14,2,48,256]{3,2,1,0:T(8,128)(2,1)S(1)}) custom-call(bf16[9,7,16,33]{3,2,1,0:T(8,128)(2,1)S(1)} %select_bitcast_fusion.taps, bf16[256,1024]{1,0:T(8,128)(2,1)S(1)} %bitcast.17, ...), custom_call_target="tpu_custom_call" | custom-call | flops 1000000000 | bytes 1000000 | tf_op jit(solution)/shard_map/pallas_call | solution.py:185
  21.5 0.0 collective-permute-done.3.far
  21.5 1.4 %collective-permute-done.4.near = bf16[11,16,256]{2,1,0:T(8,128)(2,1)S(1)} collective-permute-done((bf16[11,16,256]{2,1,0:T(8,128)(2,1)S(1)}, bf16[11,16,256]{2,1,0:T(8,128)(2,1)S(1)}, u32[]{:S(2)}, u32[]{:S(2)}) %collective-permute-start.4) | collective-permute-done | bytes 90144 | tf_op jit(solution)/shard_map/ppermute | solution.py:290
  22.9 1.9 %collective-permute-start.5 = (bf16[3,32,256]{2,1,0:T(8,128)(2,1)S(1)}, bf16[3,32,256]{2,1,0:T(8,128)(2,1)S(1)}, u32[]{:S(2)}, u32[]{:S(2)}) collective-permute-start(bf16[3,32,256]{2,1,0:T(8,128)(2,1)S(1)} %shard_map.70), channel_id=1, source_target_pairs={{0,16},{16,0},{32,48},{48,32},{64,80},{80,64},{96,112},{112,96},{1... | collective-permute-start | bytes 147464 | tf_op jit(solution)/shard_map/ppermute | solution.py:314
  24.8 0.9 %collective-permute-done.5.corner = bf16[3,32,256]{2,1,0:T(8,128)(2,1)S(1)} collective-permute-done((bf16[3,32,256]{2,1,0:T(8,128)(2,1)S(1)}, bf16[3,32,256]{2,1,0:T(8,128)(2,1)S(1)}, u32[]{:S(2)}, u32[]{:S(2)}) %collective-permute-start.5) | collective-permute-done | bytes 49184 | tf_op jit(solution)/shard_map/ppermute | solution.py:314
  25.7 0.0 copy-done.1
  25.7 2.5 %shard_map.71 = (bf16[9,8,64,256]{3,2,1,0:T(8,128)(2,1)S(1)}, f32[9,256,128]{2,1,0:T(8,128)S(1)}, f32[9,256,128]{2,1,0:T(8,128)S(1)}, bf16[9,256,256]{2,1,0:T(8,128)(2,1)S(1)}) custom-call(bf16[8,288,512]{2,1,0:T(8,128)(2,1)S(1)} %get-tuple-element.27.band, bf16[14,2,48,256]{3,2,1,0:T(8,128)(2,1)S(1)} %get-tuple-element.28.window, ...), custom_call_target="tpu_custom_call" | custom-call | flops 1000000000 | bytes 1000000 | tf_op jit(solution)/shard_map/pallas_call | solution.py:185
  28.2 0.1 select_convert_fusion
  28.3 0.4 collective-permute-start.6
  28.8 1.4 %shard_map.72 = bf16[256,1024]{1,0:T(8,128)(2,1)S(1)} custom-call(bf16[9,256,256]{2,1,0:T(8,128)(2,1)S(1)} %get-tuple-element.38.w_ref, bf16[9,8,64,256]{3,2,1,0:T(8,128)(2,1)S(1)} %get-tuple-element.39.mid_ref, bf16[9,8,64,256]{3,2,1,0:T(8,128)(2,1)S(1)} %get-tuple-element.40.edge_ref), custom_call_target="tpu_custom_call" | custom-call | flops 1000000000 | bytes 1000000 | tf_op jit(solution)/shard_map/pallas_call | solution.py:185
  30.2 0.2 collective-permute-done.6
  30.4 0.2 add_convert_fusion
  30.6 17.1 %all_to_all.15 = bf16[16,144,128]{2,1,0:T(8,128)(2,1)S(1)} all-to-all(bf16[16,144,128]{2,1,0:T(8,128)(2,1)S(1)} %bitcast.18), channel_id=1, replica_groups=mesh['y'=4,'x_lo'=2,'core'=2,'z'=8,'x_hi'=2] {'y','x_hi','x_lo'}, dimensions={0} | all-to-all | bytes 1179648 | tf_op jit(solution)/shard_map/all_to_all | solution.py:244
  47.7 0.1 reduce_sum.21
  47.9 14.1 %all_to_all.16 = bf16[8,144,128]{2,1,0:T(8,128)(2,1)S(1)} all-to-all(bf16[8,144,128]{2,1,0:T(8,128)(2,1)S(1)} %broadcast_in_dim.16), channel_id=1, replica_groups=mesh['y'=4,'x_lo'=2,'core'=2,'z'=8,'x_hi'=2] {'z'}, dimensions={0} | all-to-all | bytes 589824 | tf_op jit(solution)/shard_map/all_to_all | solution.py:244
  62.0 0.1 broadcast_in_dim.17
  62.1 13.5 %all_to_all.17 = bf16[16,144,128]{2,1,0:T(8,128)(2,1)S(1)} all-to-all(bf16[16,144,128]{2,1,0:T(8,128)(2,1)S(1)} %broadcast_in_dim.17), channel_id=1, replica_groups=mesh['y'=4,'x_lo'=2,'core'=2,'z'=8,'x_hi'=2] {'y','x_hi','x_lo'}, dimensions={0} | all-to-all | bytes 1179648 | tf_op jit(solution)/shard_map/all_to_all | solution.py:244
  75.6 4.7 %collective-permute-start.7 = (bf16[9,256,128]{2,1,0:T(8,128)(2,1)S(1)}, bf16[9,256,128]{2,1,0:T(8,128)(2,1)S(1)}, u32[]{:S(2)}, u32[]{:S(2)}) collective-permute-start(bf16[9,256,128]{2,1,0:T(8,128)(2,1)S(1)} %bitcast.14), channel_id=1, source_target_pairs={{0,16},{16,0},{1,17},{17,1},{2,18},{18,2},{3,19},{19,3},{4,20},{20... | collective-permute-start | bytes 1769480 | tf_op jit(solution)/shard_map/ppermute | solution.py:267
  80.3 0.9 %copy.14 = bf16[32,8,8,128]{3,2,1,0:T(8,128)(2,1)} copy(bf16[32,8,8,128]{3,1,2,0:T(8,128)(2,1)S(1)} %bitcast.16) | data formatting | bytes 1048576
  81.2 1.1 %shard_map.73.refs_0_ = f32[9,256,256]{2,1,0:T(8,128)} custom-call(bf16[9,256,128]{2,1,0:T(8,128)(2,1)S(1)} %bitcast.15), custom_call_target="tpu_custom_call" | custom-call | flops 1000000 | bytes 1000000 | tf_op jit(solution)/shard_map/pallas_call | solution.py:231
  82.3 0.0 collective-permute-done.7.half_ref
  82.3 1.1 %shard_map.74 = f32[9,256,256]{2,1,0:T(8,128)} custom-call(bf16[9,256,128]{2,1,0:T(8,128)(2,1)S(1)} %collective-permute-done.7.half_ref, f32[9,256,256]{2,1,0:T(8,128)} %shard_map.73.refs_0_), custom_call_target="tpu_custom_call", output_to_operand_aliasing={{}: (1, {})} | custom-call | flops 1000000 | bytes 1000000 | tf_op jit(solution)/shard_map/pallas_call | solution.py:231
  (11 shorter events, 0.2 us)
Async XLA Ops:
  0.6 8.3 %copy-start = (bf16[9,128,7,33]{1,2,3,0:T(8,128)(2,1)S(1)}, bf16[9,128,7,33]{1,2,3,0:T(8,128)(2,1)}, u32[]{:S(2)}) copy-start(bf16[9,128,7,33]{1,2,3,0:T(8,128)(2,1)} %param.8) | copy-start | bytes 1596676
  0.7 8.1 %copy-start.3 = (s32[128]{0:T(128)S(1)}, s32[128]{0:T(128)}, u32[]{:S(2)}) copy-start(s32[128]{0:T(128)} %param.9) | copy-start | bytes 1540
  2.1 7.1 %copy-start.2 = (bf16[256,8,128]{2,1,0:T(8,128)(2,1)S(1)}, bf16[256,8,128]{2,1,0:T(8,128)(2,1)}, u32[]{:S(2)}) copy-start(bf16[256,8,128]{2,1,0:T(8,128)(2,1)} %param.5) | copy-start | bytes 1572868
  2.1 7.6 %collective-permute-start = (bf16[3,32,256]{2,1,0:T(8,128)(2,1)S(1)}, bf16[3,32,256]{2,1,0:T(8,128)(2,1)S(1)}, u32[]{:S(2)}, u32[]{:S(2)}) collective-permute-start(bf16[3,32,256]{2,1,0:T(8,128)(2,1)S(1)} %pad_maximum_fusion), channel_id=1, source_target_pairs={{16,32},{32,16},{48,64},{64,48},{80,96},{96,80},{112,128},{128,112... | collective-permute-start | bytes 147464 | tf_op jit(solution)/shard_map/ppermute | solution.py:284
  6.8 11.2 %collective-permute-start.2 = (bf16[3,96,256]{2,1,0:T(8,128)(2,1)S(1)}, bf16[3,96,256]{2,1,0:T(8,128)(2,1)S(1)}, u32[]{:S(2)}, u32[]{:S(2)}) collective-permute-start(bf16[3,96,256]{2,1,0:T(8,128)(2,1)S(1)} %slice.24), channel_id=1, source_target_pairs={{16,32},{32,16},{48,64},{64,48},{80,96},{96,80},{112,128},{128,112... | collective-permute-start | bytes 442376 | tf_op jit(solution)/shard_map/ppermute | solution.py:285
  9.8 8.2 %collective-permute-start.1 = (bf16[3,128,256]{2,1,0:T(8,128)(2,1)S(1)}, bf16[3,128,256]{2,1,0:T(8,128)(2,1)S(1)}, u32[]{:S(2)}, u32[]{:S(2)}) collective-permute-start(bf16[3,128,256]{2,1,0:T(8,128)(2,1)S(1)} %get-tuple-element.26), channel_id=1, source_target_pairs={{0,16},{16,0},{32,48},{48,32},{64,80},{80,64},{96,112},{112,96},{1... | collective-permute-start | bytes 589832 | tf_op jit(solution)/shard_map/ppermute | solution.py:291
  10.0 11.5 %collective-permute-start.3 = (bf16[11,16,256]{2,1,0:T(8,128)(2,1)S(1)}, bf16[11,16,256]{2,1,0:T(8,128)(2,1)S(1)}, u32[]{:S(2)}, u32[]{:S(2)}) collective-permute-start(bf16[11,16,256]{2,1,0:T(8,128)(2,1)S(1)} %get-tuple-element.29), channel_id=1, source_target_pairs={{0,15},{1,2},{2,1},{3,4},{4,3},{5,6},{6,5},{7,8},{8,7},{9,10},{10,... | collective-permute-start | bytes 270344 | tf_op jit(solution)/shard_map/ppermute | solution.py:289
  18.0 4.9 %collective-permute-start.4 = (bf16[11,16,256]{2,1,0:T(8,128)(2,1)S(1)}, bf16[11,16,256]{2,1,0:T(8,128)(2,1)S(1)}, u32[]{:S(2)}, u32[]{:S(2)}) collective-permute-start(bf16[11,16,256]{2,1,0:T(8,128)(2,1)S(1)} %get-tuple-element.30), channel_id=1, source_target_pairs={{0,1},{1,0},{2,3},{3,2},{4,5},{5,4},{6,7},{7,6},{8,9},{9,8},{10,11... | collective-permute-start | bytes 270344 | tf_op jit(solution)/shard_map/ppermute | solution.py:290
  18.1 7.7 %copy-start.1 = (bf16[9,256,256]{2,1,0:T(8,128)(2,1)S(1)}, bf16[9,256,256]{2,1,0:T(8,128)(2,1)}, u32[]{:S(2)}) copy-start(bf16[9,256,256]{2,1,0:T(8,128)(2,1)} %w_ref.1) | copy-start | bytes 3538948
  22.9 2.8 %collective-permute-start.5 = (bf16[3,32,256]{2,1,0:T(8,128)(2,1)S(1)}, bf16[3,32,256]{2,1,0:T(8,128)(2,1)S(1)}, u32[]{:S(2)}, u32[]{:S(2)}) collective-permute-start(bf16[3,32,256]{2,1,0:T(8,128)(2,1)S(1)} %shard_map.70), channel_id=1, source_target_pairs={{0,16},{16,0},{32,48},{48,32},{64,80},{80,64},{96,112},{112,96},{1... | collective-permute-start | bytes 147464 | tf_op jit(solution)/shard_map/ppermute | solution.py:314
  28.3 2.1 %collective-permute-start.6 = (bf16[9,256,128]{2,1,0:T(8,128)(2,1)S(1)}, bf16[9,256,128]{2,1,0:T(8,128)(2,1)S(1)}, u32[]{:S(2)}, u32[]{:S(2)}) collective-permute-start(bf16[9,256,128]{2,1,0:T(8,128)(2,1)S(1)} %select_convert_fusion), channel_id=1, source_target_pairs={{0,16},{16,0},{1,17},{17,1},{2,18},{18,2},{3,19},{19,3},{4,20},{20... | collective-permute-start | bytes 1769480 | tf_op jit(solution)/shard_map/ppermute | solution.py:259
  75.6 6.6 %collective-permute-start.7 = (bf16[9,256,128]{2,1,0:T(8,128)(2,1)S(1)}, bf16[9,256,128]{2,1,0:T(8,128)(2,1)S(1)}, u32[]{:S(2)}, u32[]{:S(2)}) collective-permute-start(bf16[9,256,128]{2,1,0:T(8,128)(2,1)S(1)} %bitcast.14), channel_id=1, source_target_pairs={{0,16},{16,0},{1,17},{17,1},{2,18},{18,2},{3,19},{19,3},{4,20},{20... | collective-permute-start | bytes 1769480 | tf_op jit(solution)/shard_map/ppermute | solution.py:267

commit v12 on v11

--- a/solution.py
+++ b/solution.py
@@ -34,10 +34,8 @@
     return above, jnp.clip(above, 0, nlat_all - held), held
 
 
-def tap_rows(basis_table, lon_reach, start, near):
-    tap_count = basis_table.shape[3]
-    table = lax.dynamic_slice_in_dim(basis_table, start, near, 1)
-    reach = lax.dynamic_slice_in_dim(lon_reach, start, near, 0)
+def mask_taps(table, reach):
+    tap_count = table.shape[3]
     offset = jnp.abs(lax.iota(jnp.int32, tap_count) - tap_count // 2)
     table = jnp.where((offset[None, :] <= reach[:, None])[None, :, None, :], table, jnp.zeros_like(table))
     return jnp.transpose(table, (0, 2, 1, 3))
@@ -285,11 +283,13 @@
     rest_lat = lax.ppermute(to_far[:, side : lon_dev - side], LAT, pairs(LAT, False, False))
     rim = shape((near - half, side, channels), bf16)
     second, first = call(rim_kernel, (rim, rim), (main, far_lat), flops=10**6, mib=4)
-    to_near, second, first = lax.optimization_barrier((to_near, second, first))
+    start, to_near, second, first = lax.optimization_barrier((start, to_near, second, first))
+    table = lax.dynamic_slice_in_dim(basis_table, start, held, 1)
+    reach = lax.dynamic_slice_in_dim(lon_reach, start, held, 0)
+    taps = mask_taps(table, reach)
     far_lon = lax.ppermute(second, LON, pairs(LON, False, True))
     near_lon = lax.ppermute(first, LON, pairs(LON, True, True))
     near_lat = lax.ppermute(to_near, LAT, pairs(LAT, True, False))
-    taps = tap_rows(basis_table, lon_reach, start, held)
     q_shape = shape((basis_count, lat_dev, wide, channels), bf16)
     columns = shape((channels, lat_dev * wide), bf16)
     part = shape((basis_count, channels, channels // 2), f32)

time: 83.6 us -> 84.6 us (1.012)
  blocking collectives: 44.7 us -> 47.8 us
  starting transfers between devices: 21.8 us -> 19.6 us
    all_to_all x3, blocking collectives: 44.7 us -> 47.8 us  [all_to_all(): return lax.all_to_all(x, axes, 0, 0, tiled=True)]
    ppermute x1, starting transfers between devices: 1.92 us -> 0.28 us  [local(): corner = lax.ppermute(corner, LAT, pairs(LAT, True, False))]
    ppermute x1, waiting for transfers between devices: 1.44 us -> 0.03 us  [local(): near_lon = lax.ppermute(first, LON, pairs(LON, True, True))]
  transfers between devices with their start and end apart: 8 -> 8, of which waited for: 3 -> 3; matrix products, arithmetic and copies ran while one was open for 2% -> 3% of each run, Pallas kernels for 7% -> 7%
where the time goes in v12:
time: 84.6 us; the launch traced here: 84.3 us
  blocking collectives  47.8 us (57%)
  starting transfers between devices  19.6 us (23%)
  Pallas kernels  9.43 us (11%)
  local copies, waits for them, and re-layouts  4.01 us (5%)
  waiting for transfers between devices  1.98 us (2%)
  between operations  0.9 us (1%)
    all_to_all x3, blocking collectives, all_to_all(): return lax.all_to_all(x, axes, 0, 0, tiled=True)  47.8 us
    ppermute x1, starting transfers between devices, local(): far_lon = lax.ppermute(second, LON, pairs(LON, False, True))  8.08 us
    pallas_call x5, Pallas kernels, call(): pl.pallas_call(kernel, out_shape=out_shape, in_specs=[vmem] * (len(operan...  7.32 us
    ppermute x1, starting transfers between devices, reduce_all(): lax.ppermute(own, 'core', swap)  4.58 us
    ppermute x1, starting transfers between devices, local(): far_lat = lax.ppermute(outer, LAT, pairs(LAT, False, False))  4.51 us
    unnamed x12, local copies, waits for them, and re-layouts  2.91 us
    pallas_call x2, Pallas kernels, place(): pl.pallas_call(functools.partial(place_kernel, own), out_shape=jax.ShapeD...  2.12 us
    ppermute x1, starting transfers between devices, local(): lax.ppermute(to_far[:, side:lon_dev - side], LAT, pairs(LAT, False, False))  1.91 us
  transfers between devices with their start and end apart: 8, of which 3 were waited for; matrix products, arithmetic and copies ran while one was open for 3% of the time, Pallas kernels for 7%

profile of v12, /device:TPU:1, one launch (start us, length us, event | category | flops | bytes accessed | tf_op | source)
XLA Modules:
  0.0 84.3 jit_solution(6698977944693665882)
XLA Ops:
  0.6 0.0 copy-start
  0.7 0.0 copy-start.2
  0.7 1.4 %copy.10 = bf16[256,8,128]{0,2,1:T(8,128)(2,1)S(1)} copy(bf16[256,8,128]{2,1,0:T(8,128)(2,1)} %param.6) | data formatting | bytes 1048576 | tf_op args[1]
  2.1 0.0 copy-start.3
  2.2 4.5 %collective-permute-start = (bf16[3,32,256]{2,1,0:T(8,128)(2,1)S(1)}, bf16[3,32,256]{2,1,0:T(8,128)(2,1)S(1)}, u32[]{:S(2)}, u32[]{:S(2)}) collective-permute-start(bf16[3,32,256]{2,1,0:T(8,128)(2,1)S(1)} %pad_maximum_fusion), channel_id=1, source_target_pairs={{16,32},{32,16},{48,64},{64,48},{80,96},{96,80},{112,128},{128,112... | collective-permute-start | bytes 147464 | tf_op jit(solution)/shard_map/ppermute | solution.py:282
  6.7 0.7 slice.24
  7.3 1.9 %collective-permute-start.2 = (bf16[3,96,256]{2,1,0:T(8,128)(2,1)}, bf16[3,96,256]{2,1,0:T(8,128)(2,1)S(1)}, u32[]{:S(2)}, u32[]{:S(2)}) collective-permute-start(bf16[3,96,256]{2,1,0:T(8,128)(2,1)} %slice.24), channel_id=1, source_target_pairs={{16,32},{32,16},{48,64},{64,48},{80,96},{96,80},{112,128},{128,112... | collective-permute-start | bytes 442376 | tf_op jit(solution)/shard_map/ppermute | solution.py:283
  9.3 0.0 copy-done.2
  9.3 0.1 copy.16
  9.4 0.0 collective-permute-done.far
  9.5 8.1 %collective-permute-start.3 = (bf16[11,16,256]{2,1,0:T(8,128)(2,1)S(1)}, bf16[11,16,256]{2,1,0:T(8,128)(2,1)S(1)}, u32[]{:S(2)}, u32[]{:S(2)}) collective-permute-start(bf16[11,16,256]{2,1,0:T(8,128)(2,1)S(1)} %get-tuple-element.31), channel_id=1, source_target_pairs={{0,15},{1,2},{2,1},{3,4},{4,3},{5,6},{6,5},{7,8},{8,7},{9,10},{10,... | collective-permute-start | bytes 270344 | tf_op jit(solution)/shard_map/ppermute | solution.py:290
  17.6 0.0 collective-permute-start.4
  17.6 0.0 collective-permute-start.1
  17.6 0.0 copy-done.3
  17.6 0.1 dynamic_slice.6
  17.6 0.0 copy-done
  17.6 0.2 constant_dynamic-slice_fusion
  17.9 0.5 copy.12
  18.4 0.1 broadcast_compare_fusion
  18.5 0.0 collective-permute-done.2.rest
  18.5 0.5 collective-permute-done.1.near
  19.0 0.0 copy-start.1
  19.0 3.4 %shard_map.69 = (bf16[8,288,512]{2,1,0:T(8,128)(2,1)S(1)}, bf16[256,512]{1,0:T(8,128)(2,1)S(1)}, bf16[9,8,64,256]{3,2,1,0:T(8,128)(2,1)S(1)}, f32[9,256,256]{2,1,0:T(8,128)S(1)}, bf16[14,2,48,256]{3,2,1,0:T(8,128)(2,1)S(1)}) custom-call(bf16[9,7,16,33]{3,2,1,0:T(8,128)(2,1)S(1)} %select_bitcast_fusion.taps, bf16[256,1024]{1,0:T(8,128)(2,1)S(1)} %bitcast.17, ...), custom_call_target="tpu_custom_call" | custom-call | flops 1000000000 | bytes 1000000 | tf_op jit(solution)/shard_map/pallas_call | solution.py:183
  22.4 0.0 collective-permute-done.3.far
  22.4 0.0 collective-permute-done.4.near
  22.4 0.3 collective-permute-start.5
  22.7 1.0 %collective-permute-done.5.corner = bf16[3,32,256]{2,1,0:T(8,128)(2,1)S(1)} collective-permute-done((bf16[3,32,256]{2,1,0:T(8,128)(2,1)S(1)}, bf16[3,32,256]{2,1,0:T(8,128)(2,1)S(1)}, u32[]{:S(2)}, u32[]{:S(2)}) %collective-permute-start.5) | collective-permute-done | bytes 49184 | tf_op jit(solution)/shard_map/ppermute | solution.py:314
  23.8 0.0 copy-done.1
  23.8 2.5 %shard_map.71 = (bf16[9,8,64,256]{3,2,1,0:T(8,128)(2,1)S(1)}, f32[9,256,128]{2,1,0:T(8,128)S(1)}, f32[9,256,128]{2,1,0:T(8,128)S(1)}, bf16[9,256,256]{2,1,0:T(8,128)(2,1)S(1)}) custom-call(bf16[8,288,512]{2,1,0:T(8,128)(2,1)S(1)} %get-tuple-element.29.band, bf16[14,2,48,256]{3,2,1,0:T(8,128)(2,1)S(1)} %get-tuple-element.30.window, ...), custom_call_target="tpu_custom_call" | custom-call | flops 1000000000 | bytes 1000000 | tf_op jit(solution)/shard_map/pallas_call | solution.py:183
  26.2 0.1 select_convert_fusion
  26.4 0.3 collective-permute-start.6
  26.7 1.4 %shard_map.72 = bf16[256,1024]{1,0:T(8,128)(2,1)S(1)} custom-call(bf16[9,256,256]{2,1,0:T(8,128)(2,1)S(1)} %get-tuple-element.40.w_ref, bf16[9,8,64,256]{3,2,1,0:T(8,128)(2,1)S(1)} %get-tuple-element.41.mid_ref, bf16[9,8,64,256]{3,2,1,0:T(8,128)(2,1)S(1)} %get-tuple-element.42.edge_ref), custom_call_target="tpu_custom_call" | custom-call | flops 1000000000 | bytes 1000000 | tf_op jit(solution)/shard_map/pallas_call | solution.py:183
  28.1 0.4 collective-permute-done.6
  28.5 0.2 add_convert_fusion
  28.7 20.0 %all_to_all.15 = bf16[16,144,128]{2,1,0:T(8,128)(2,1)S(1)} all-to-all(bf16[16,144,128]{2,1,0:T(8,128)(2,1)S(1)} %bitcast.18), channel_id=1, replica_groups=mesh['y'=4,'x_lo'=2,'core'=2,'z'=8,'x_hi'=2] {'y','x_hi','x_lo'}, dimensions={0} | all-to-all | bytes 1179648 | tf_op jit(solution)/shard_map/all_to_all | solution.py:242
  48.7 0.1 reduce_sum.21
  48.8 14.8 %all_to_all.16 = bf16[8,144,128]{2,1,0:T(8,128)(2,1)S(1)} all-to-all(bf16[8,144,128]{2,1,0:T(8,128)(2,1)S(1)} %broadcast_in_dim.16), channel_id=1, replica_groups=mesh['y'=4,'x_lo'=2,'core'=2,'z'=8,'x_hi'=2] {'z'}, dimensions={0} | all-to-all | bytes 589824 | tf_op jit(solution)/shard_map/all_to_all | solution.py:242
  63.7 0.1 broadcast_in_dim.17
  63.8 12.9 %all_to_all.17 = bf16[16,144,128]{2,1,0:T(8,128)(2,1)S(1)} all-to-all(bf16[16,144,128]{2,1,0:T(8,128)(2,1)S(1)} %broadcast_in_dim.17), channel_id=1, replica_groups=mesh['y'=4,'x_lo'=2,'core'=2,'z'=8,'x_hi'=2] {'y','x_hi','x_lo'}, dimensions={0} | all-to-all | bytes 1179648 | tf_op jit(solution)/shard_map/all_to_all | solution.py:242
  76.7 4.6 %collective-permute-start.7 = (bf16[9,256,128]{2,1,0:T(8,128)(2,1)S(1)}, bf16[9,256,128]{2,1,0:T(8,128)(2,1)S(1)}, u32[]{:S(2)}, u32[]{:S(2)}) collective-permute-start(bf16[9,256,128]{2,1,0:T(8,128)(2,1)S(1)} %bitcast.14), channel_id=1, source_target_pairs={{0,16},{16,0},{1,17},{17,1},{2,18},{18,2},{3,19},{19,3},{4,20},{20... | collective-permute-start | bytes 1769480 | tf_op jit(solution)/shard_map/ppermute | solution.py:265
  81.3 0.9 %copy.14 = bf16[32,8,8,128]{3,2,1,0:T(8,128)(2,1)} copy(bf16[32,8,8,128]{3,1,2,0:T(8,128)(2,1)S(1)} %bitcast.16) | data formatting | bytes 1048576
  82.2 1.1 %shard_map.73.refs_0_ = f32[9,256,256]{2,1,0:T(8,128)} custom-call(bf16[9,256,128]{2,1,0:T(8,128)(2,1)S(1)} %bitcast.15), custom_call_target="tpu_custom_call" | custom-call | flops 1000000 | bytes 1000000 | tf_op jit(solution)/shard_map/pallas_call | solution.py:229
  83.2 0.0 collective-permute-done.7.half_ref
  83.2 1.1 %shard_map.74 = f32[9,256,256]{2,1,0:T(8,128)} custom-call(bf16[9,256,128]{2,1,0:T(8,128)(2,1)S(1)} %collective-permute-done.7.half_ref, f32[9,256,256]{2,1,0:T(8,128)} %shard_map.73.refs_0_), custom_call_target="tpu_custom_call", output_to_operand_aliasing={{}: (1, {})} | custom-call | flops 1000000 | bytes 1000000 | tf_op jit(solution)/shard_map/pallas_call | solution.py:229
  (10 shorter events, 0.2 us)
Async XLA Ops:
  0.6 17.0 %copy-start = (bf16[9,128,7,33]{1,2,3,0:T(8,128)(2,1)S(1)}, bf16[9,128,7,33]{1,2,3,0:T(8,128)(2,1)}, u32[]{:S(2)}) copy-start(bf16[9,128,7,33]{1,2,3,0:T(8,128)(2,1)} %param.8) | copy-start | bytes 1596676
  0.7 8.6 %copy-start.2 = (bf16[256,8,128]{2,1,0:T(8,128)(2,1)S(1)}, bf16[256,8,128]{2,1,0:T(8,128)(2,1)}, u32[]{:S(2)}) copy-start(bf16[256,8,128]{2,1,0:T(8,128)(2,1)} %param.5) | copy-start | bytes 1572868
  2.1 15.4 %copy-start.3 = (s32[128]{0:T(128)S(1)}, s32[128]{0:T(128)}, u32[]{:S(2)}) copy-start(s32[128]{0:T(128)} %param.9) | copy-start | bytes 1540
  2.2 7.2 %collective-permute-start = (bf16[3,32,256]{2,1,0:T(8,128)(2,1)S(1)}, bf16[3,32,256]{2,1,0:T(8,128)(2,1)S(1)}, u32[]{:S(2)}, u32[]{:S(2)}) collective-permute-start(bf16[3,32,256]{2,1,0:T(8,128)(2,1)S(1)} %pad_maximum_fusion), channel_id=1, source_target_pairs={{16,32},{32,16},{48,64},{64,48},{80,96},{96,80},{112,128},{128,112... | collective-permute-start | bytes 147464 | tf_op jit(solution)/shard_map/ppermute | solution.py:282
  7.3 11.1 %collective-permute-start.2 = (bf16[3,96,256]{2,1,0:T(8,128)(2,1)}, bf16[3,96,256]{2,1,0:T(8,128)(2,1)S(1)}, u32[]{:S(2)}, u32[]{:S(2)}) collective-permute-start(bf16[3,96,256]{2,1,0:T(8,128)(2,1)} %slice.24), channel_id=1, source_target_pairs={{16,32},{32,16},{48,64},{64,48},{80,96},{96,80},{112,128},{128,112... | collective-permute-start | bytes 442376 | tf_op jit(solution)/shard_map/ppermute | solution.py:283
  9.5 12.9 %collective-permute-start.3 = (bf16[11,16,256]{2,1,0:T(8,128)(2,1)S(1)}, bf16[11,16,256]{2,1,0:T(8,128)(2,1)S(1)}, u32[]{:S(2)}, u32[]{:S(2)}) collective-permute-start(bf16[11,16,256]{2,1,0:T(8,128)(2,1)S(1)} %get-tuple-element.31), channel_id=1, source_target_pairs={{0,15},{1,2},{2,1},{3,4},{4,3},{5,6},{6,5},{7,8},{8,7},{9,10},{10,... | collective-permute-start | bytes 270344 | tf_op jit(solution)/shard_map/ppermute | solution.py:290
  17.6 4.9 %collective-permute-start.4 = (bf16[11,16,256]{2,1,0:T(8,128)(2,1)S(1)}, bf16[11,16,256]{2,1,0:T(8,128)(2,1)S(1)}, u32[]{:S(2)}, u32[]{:S(2)}) collective-permute-start(bf16[11,16,256]{2,1,0:T(8,128)(2,1)S(1)} %get-tuple-element.32), channel_id=1, source_target_pairs={{0,1},{1,0},{2,3},{3,2},{4,5},{5,4},{6,7},{7,6},{8,9},{9,8},{10,11... | collective-permute-start | bytes 270344 | tf_op jit(solution)/shard_map/ppermute | solution.py:291
  17.6 1.4 %collective-permute-start.1 = (bf16[3,128,256]{2,1,0:T(8,128)(2,1)S(1)}, bf16[3,128,256]{2,1,0:T(8,128)(2,1)S(1)}, u32[]{:S(2)}, u32[]{:S(2)}) collective-permute-start(bf16[3,128,256]{2,1,0:T(8,128)(2,1)S(1)} %get-tuple-element.28), channel_id=1, source_target_pairs={{0,16},{16,0},{32,48},{48,32},{64,80},{80,64},{96,112},{112,96},{1... | collective-permute-start | bytes 589832 | tf_op jit(solution)/shard_map/ppermute | solution.py:292
  19.0 4.8 %copy-start.1 = (bf16[9,256,256]{2,1,0:T(8,128)(2,1)S(1)}, bf16[9,256,256]{2,1,0:T(8,128)(2,1)}, u32[]{:S(2)}) copy-start(bf16[9,256,256]{2,1,0:T(8,128)(2,1)} %w_ref.1) | copy-start | bytes 3538948
  22.4 1.3 %collective-permute-start.5 = (bf16[3,32,256]{2,1,0:T(8,128)(2,1)S(1)}, bf16[3,32,256]{2,1,0:T(8,128)(2,1)S(1)}, u32[]{:S(2)}, u32[]{:S(2)}) collective-permute-start(bf16[3,32,256]{2,1,0:T(8,128)(2,1)S(1)} %shard_map.70), channel_id=1, source_target_pairs={{0,16},{16,0},{32,48},{48,32},{64,80},{80,64},{96,112},{112,96},{1... | collective-permute-start | bytes 147464 | tf_op jit(solution)/shard_map/ppermute | solution.py:314
  26.4 2.1 %collective-permute-start.6 = (bf16[9,256,128]{2,1,0:T(8,128)(2,1)S(1)}, bf16[9,256,128]{2,1,0:T(8,128)(2,1)S(1)}, u32[]{:S(2)}, u32[]{:S(2)}) collective-permute-start(bf16[9,256,128]{2,1,0:T(8,128)(2,1)S(1)} %select_convert_fusion), channel_id=1, source_target_pairs={{0,16},{16,0},{1,17},{17,1},{2,18},{18,2},{3,19},{19,3},{4,20},{20... | collective-permute-start | bytes 1769480 | tf_op jit(solution)/shard_map/ppermute | solution.py:257
  76.7 6.5 %collective-permute-start.7 = (bf16[9,256,128]{2,1,0:T(8,128)(2,1)S(1)}, bf16[9,256,128]{2,1,0:T(8,128)(2,1)S(1)}, u32[]{:S(2)}, u32[]{:S(2)}) collective-permute-start(bf16[9,256,128]{2,1,0:T(8,128)(2,1)S(1)} %bitcast.14), channel_id=1, source_target_pairs={{0,16},{16,0},{1,17},{17,1},{2,18},{18,2},{3,19},{19,3},{4,20},{20... | collective-permute-start | bytes 1769480 | tf_op jit(solution)/shard_map/ppermute | solution.py:265

commit v13 on v12

--- a/solution.py
+++ b/solution.py
@@ -59,6 +59,21 @@
                     outer = slice(side, 2 * side) if at else slice(0, side)
                     ref[own] = main[:, at : at + side, :]
                     ref[other] = far[:, outer, :]
+
+
+def cut_kernel(main, outer, rest, to_near):
+    lat_dev, lon_dev, _ = main.shape
+    half, side = outer.shape[0], outer.shape[1] // 2
+    odd_lat = parity(LAT)
+    first, last = slice(0, half), slice(lat_dev - half, lat_dev)
+    for odd, (far, near) in enumerate(((first, last), (last, first))):
+
+        @pl.when(odd_lat == odd)
+        def _():
+            outer[:, :side] = main[far, :side]
+            outer[:, side:] = main[far, lon_dev - side :]
+            rest[...] = main[far, side : lon_dev - side]
+            to_near[...] = main[near]
 
 
 def corner_kernel(far, near, out):
@@ -121,12 +136,16 @@
         f_edge[:, at] = jnp.where(lane < wide, ahead(even), back(odd)).astype(bf16)
 
 
-def middle_kernel(nlat_all, taps, f_ref, main, near, far, rest, band, f_edge, q_ref, total, window, lines, f_mid, ext):
+def band_kernel(nlat_all, taps, band, lines):
+    lat_dev = band.shape[0]
+    above, start, _ = held_rows(lat_dev, taps.shape[1] // 2, nlat_all)
+    build_band(above - start, taps, band, lines)
+
+
+def middle_kernel(band, f_ref, main, near, far, rest, f_edge, q_ref, total, window, f_mid, ext):
     lat_dev, lon_dev, channels = main.shape
     half, side = near.shape[0], BLOCK // 2
     inner = window.shape[2]
-    above, start, _ = held_rows(lat_dev, half, nlat_all)
-    build_band(above - start, taps, band, lines)
     cut_fields(f_ref, f_mid, f_edge)
     ext[half : half + lat_dev] = main[...]
     odd_lat = parity(LAT)
@@ -274,13 +293,16 @@
     shape = jax.ShapeDtypeStruct
     core = lax.axis_index("core")
     _, start, held = held_rows(lat_dev, half, nlat_all)
-    upper = core == 0
     main = jnp.transpose(grad_out, (1, 2, 0))
-    last, first = main[lat_dev - half :], main[:half]
-    to_near, to_far = jnp.where(upper, last, first), jnp.where(upper, first, last)
-    outer = jnp.concatenate([to_far[:, :side], to_far[:, lon_dev - side :]], axis=1)
+    outer, rest, to_near = call(
+        cut_kernel,
+        tuple(shape((half, count, channels), bf16) for count in (2 * side, lon_dev - 2 * side, lon_dev)),
+        (main,),
+        flops=10**6,
+        mib=4,
+    )
     far_lat = lax.ppermute(outer, LAT, pairs(LAT, False, False))
-    rest_lat = lax.ppermute(to_far[:, side : lon_dev - side], LAT, pairs(LAT, False, False))
+    rest_lat = lax.ppermute(rest, LAT, pairs(LAT, False, False))
     rim = shape((near - half, side, channels), bf16)
     second, first = call(rim_kernel, (rim, rim), (main, far_lat), flops=10**6, mib=4)
     start, to_near, second, first = lax.optimization_barrier((start, to_near, second, first))
@@ -293,21 +315,24 @@
     q_shape = shape((basis_count, lat_dev, wide, channels), bf16)
     columns = shape((channels, lat_dev * wide), bf16)
     part = shape((basis_count, channels, channels // 2), f32)
-    band, f_edge, q_mid, total, window = call(
-        functools.partial(middle_kernel, nlat_all),
+    band = call(
+        functools.partial(band_kernel, nlat_all),
+        shape((lat_dev, basis_count * BLOCK, (row_span + 1) * wide), bf16),
+        (taps,),
+        [pltpu.VMEM((basis_count, row_span, held + 16, 128), f32)],
+        flops=10**8,
+        mib=8,
+    )
+    f_edge, q_mid, total, window = call(
+        middle_kernel,
         (
-            shape((lat_dev, basis_count * BLOCK, (row_span + 1) * wide), bf16),
             columns,
             q_shape,
             shape((basis_count, channels, channels), f32),
             shape((near, 2, wide - side, channels), bf16),
         ),
-        (taps, fields.reshape(channels, lat_dev * lon_dev), main, near_lat, far_lat, rest_lat),
-        [
-            pltpu.VMEM((basis_count, row_span, held + 16, 128), f32),
-            pltpu.VMEM(columns.shape, bf16),
-            pltpu.VMEM((near, lon_dev, channels), bf16),
-        ],
+        (band, fields.reshape(channels, lat_dev * lon_dev), main, near_lat, far_lat, rest_lat),
+        [pltpu.VMEM(columns.shape, bf16), pltpu.VMEM((near, lon_dev, channels), bf16)],
     )
     far_lon, near_lon, total = lax.optimization_barrier((far_lon, near_lon, total))
     corner = call(corner_kernel, shape((half, 2 * side, channels), bf16), (far_lon, near_lon), flops=10**6, mib=4)

time: 84.6 us -> 97.2 us (1.15)
  local copies, waits for them, and re-layouts: 4.01 us -> 14.6 us
  Pallas kernels: 9.43 us -> 13.9 us
  blocking collectives: 47.8 us -> 45.9 us
  waiting for transfers between devices: 1.98 us -> 0.9 us
    unnamed x12 -> x30, local copies, waits for them, and re-layouts: 2.91 us -> 14.2 us
    pallas_call x5 -> x7, Pallas kernels: 7.32 us -> 11.8 us  [call(): pl.pallas_call(kernel, out_shape=out_shape, in_specs=[vmem] * (len(operan...]
    all_to_all x3, blocking collectives: 47.8 us -> 45.9 us  [all_to_all(): return lax.all_to_all(x, axes, 0, 0, tiled=True)]
  transfers between devices with their start and end apart: 8 -> 8, of which waited for: 3 -> 1; matrix products, arithmetic and copies ran while one was open for 3% -> 3% of each run, Pallas kernels for 7% -> 8%
where the time goes in v13:
time: 97.2 us; the launch traced here: 96.7 us
  blocking collectives  45.9 us (47%)
  starting transfers between devices  19.9 us (20%)
  local copies, waits for them, and re-layouts  14.6 us (15%)
  Pallas kernels  13.9 us (14%)
    all_to_all x3, blocking collectives, all_to_all(): return lax.all_to_all(x, axes, 0, 0, tiled=True)  45.9 us
    unnamed x30, local copies, waits for them, and re-layouts  14.2 us
    pallas_call x7, Pallas kernels, call(): pl.pallas_call(kernel, out_shape=out_shape, in_specs=[vmem] * (len(operan...  11.8 us
    ppermute x1, starting transfers between devices, local(): far_lon = lax.ppermute(second, LON, pairs(LON, False, True))  8 us
    ppermute x1, starting transfers between devices, reduce_all(): lax.ppermute(own, 'core', swap)  4.58 us
    ppermute x1, starting transfers between devices, local(): far_lat = lax.ppermute(outer, LAT, pairs(LAT, False, False))  4.5 us
    pallas_call x2, Pallas kernels, place(): pl.pallas_call(functools.partial(place_kernel, own), out_shape=jax.ShapeD...  2.12 us
  transfers between devices with their start and end apart: 8, of which 1 were waited for; matrix products, arithmetic and copies ran while one was open for 3% of the time, Pallas kernels for 8%

profile of v13, /device:TPU:1, one launch (start us, length us, event | category | flops | bytes accessed | tf_op | source)
XLA Modules:
  0.0 96.7 jit_solution(10211664551418191918)
XLA Ops:
  0.6 0.0 copy-start
  0.6 0.0 copy-start.11
  0.7 1.4 %copy.10 = bf16[256,8,128]{0,2,1:T(8,128)(2,1)S(1)} copy(bf16[256,8,128]{2,1,0:T(8,128)(2,1)} %param.6) | data formatting | bytes 1048576 | tf_op args[1]
  2.1 0.0 copy-start.12
  2.1 0.8 shard_map.68
  2.9 4.5 %collective-permute-start = (bf16[3,32,256]{2,1,0:T(8,128)(2,1)S(1)}, bf16[3,32,256]{2,1,0:T(8,128)(2,1)S(1)}, u32[]{:S(2)}, u32[]{:S(2)}) collective-permute-start(bf16[3,32,256]{2,1,0:T(8,128)(2,1)S(1)} %get-tuple-element.28), channel_id=1, source_target_pairs={{16,32},{32,16},{48,64},{64,48},{80,96},{96,80},{112,128},{128,112... | collective-permute-start | bytes 147464 | tf_op jit(solution)/shard_map/ppermute | solution.py:304
  7.4 1.9 %collective-permute-start.2 = (bf16[3,96,256]{2,1,0:T(8,128)(2,1)}, bf16[3,96,256]{2,1,0:T(8,128)(2,1)}, u32[]{:S(2)}, u32[]{:S(2)}) collective-permute-start(bf16[3,96,256]{2,1,0:T(8,128)(2,1)} %get-tuple-element.33), channel_id=1, source_target_pairs={{16,32},{32,16},{48,64},{64,48},{80,96},{96,80},{112,128},{128,112... | collective-permute-start | bytes 442376 | tf_op jit(solution)/shard_map/ppermute | solution.py:305
  9.3 0.0 copy-done.11
  9.3 0.9 copy.16
  10.2 0.0 collective-permute-done.far
  10.2 0.7 shard_map.69
  10.9 8.0 %collective-permute-start.3 = (bf16[11,16,256]{2,1,0:T(8,128)(2,1)}, bf16[11,16,256]{2,1,0:T(8,128)(2,1)}, u32[]{:S(2)}, u32[]{:S(2)}) collective-permute-start(bf16[11,16,256]{2,1,0:T(8,128)(2,1)} %get-tuple-element.35), channel_id=1, source_target_pairs={{0,15},{1,2},{2,1},{3,4},{4,3},{5,6},{6,5},{7,8},{8,7},{9,10},{10,... | collective-permute-start | bytes 270344 | tf_op jit(solution)/shard_map/ppermute | solution.py:312
  18.9 0.0 collective-permute-start.4
  18.9 0.0 collective-permute-start.1
  18.9 0.0 copy-done.12
  18.9 0.1 dynamic_slice.6
  19.0 0.0 copy-done
  19.0 0.2 constant_dynamic-slice_fusion
  19.2 0.5 copy.12
  19.7 0.1 broadcast_compare_fusion
  19.8 0.0 copy-start.5
  19.8 1.0 %shard_map.70.band = bf16[8,288,512]{2,1,0:T(8,128)(2,1)S(1)} custom-call(bf16[9,7,16,33]{3,2,1,0:T(8,128)(2,1)S(1)} %select_bitcast_fusion.taps), custom_call_target="tpu_custom_call" | custom-call | flops 100000000 | bytes 1000000 | tf_op jit(solution)/shard_map/pallas_call | solution.py:202
  20.9 0.0 collective-permute-done.2.rest
  20.9 0.0 collective-permute-done.1.near
  20.9 0.0 copy-done.5
  20.9 3.6 %shard_map.71 = (bf16[256,512]{1,0:T(8,128)(2,1)S(1)}, bf16[9,8,64,256]{3,2,1,0:T(8,128)(2,1)S(1)}, f32[9,256,256]{2,1,0:T(8,128)S(1)}, bf16[14,2,48,256]{3,2,1,0:T(8,128)(2,1)S(1)}) custom-call(bf16[8,288,512]{2,1,0:T(8,128)(2,1)S(1)} %shard_map.70.band, bf16[256,1024]{1,0:T(8,128)(2,1)S(1)} %bitcast.17, bf16[8,128,256]{2,1,0:T(8,128)(2,1)S(1)} %bitcast.13, ...), custom_call_target="tpu_custom_call" | custom-call | flops 1000000000 | bytes 1000000 | tf_op jit(solution)/shard_map/pallas_call | solution.py:202
  24.5 0.0 copy-start.1
  24.5 1.4 %copy-done.1 = bf16[9,8,64,256]{3,2,1,0:T(8,128)(2,1)} copy-done((bf16[9,8,64,256]{3,2,1,0:T(8,128)(2,1)}, bf16[9,8,64,256]{3,2,1,0:T(8,128)(2,1)S(1)}, u32[]{:S(2)}) %copy-start.1) | copy-done | bytes 2359320
  25.9 0.0 copy-start.3
  25.9 1.4 %copy-done.3 = f32[9,256,256]{2,1,0:T(8,128)} copy-done((f32[9,256,256]{2,1,0:T(8,128)}, f32[9,256,256]{2,1,0:T(8,128)S(1)}, u32[]{:S(2)}) %copy-start.3) | copy-done | bytes 2359320
  27.3 0.0 copy-start.7
  27.3 0.9 copy-done.7
  28.2 0.0 copy-start.9
  28.2 0.7 copy-done.9
  28.9 0.0 collective-permute-done.3.far
  28.9 0.0 collective-permute-done.4.near
  28.9 0.9 shard_map.72
  29.8 0.5 collective-permute-start.5
  30.3 0.9 collective-permute-done.5.corner
  31.2 0.0 copy-start.4
  31.2 1.7 %copy-done.4 = f32[9,256,256]{2,1,0:T(8,128)S(1)} copy-done((f32[9,256,256]{2,1,0:T(8,128)S(1)}, f32[9,256,256]{2,1,0:T(8,128)}, u32[]{:S(2)}) %copy-start.4) | copy-done | bytes 2359320
  32.9 0.0 copy-start.6
  32.9 1.3 %copy-done.6 = bf16[9,256,256]{2,1,0:T(8,128)(2,1)S(1)} copy-done((bf16[9,256,256]{2,1,0:T(8,128)(2,1)S(1)}, bf16[9,256,256]{2,1,0:T(8,128)(2,1)}, u32[]{:S(2)}) %copy-start.6) | copy-done | bytes 1179672
  34.2 0.0 copy-start.8
  34.2 1.1 %copy-done.8 = bf16[14,2,48,256]{3,2,1,0:T(8,128)(2,1)S(1)} copy-done((bf16[14,2,48,256]{3,2,1,0:T(8,128)(2,1)S(1)}, bf16[14,2,48,256]{3,2,1,0:T(8,128)(2,1)}, u32[]{:S(2)}) %copy-start.8) | copy-done | bytes 688152
  35.3 0.9 copy-done.10
  36.2 3.4 %shard_map.73 = (bf16[9,8,64,256]{3,2,1,0:T(8,128)(2,1)S(1)}, f32[9,256,128]{2,1,0:T(8,128)S(1)}, f32[9,256,128]{2,1,0:T(8,128)S(1)}, bf16[9,256,256]{2,1,0:T(8,128)(2,1)S(1)}) custom-call(bf16[8,288,512]{2,1,0:T(8,128)(2,1)S(1)} %shard_map.70.band, bf16[14,2,48,256]{3,2,1,0:T(8,128)(2,1)S(1)} %copy-done.8, bf16[11,16,256]{2,1,0:T(8,128)(2,1)} %collective-permute-done.3.far, ...), custom_call_target="tpu_custom_call" | custom-call | flops 1000000000 | bytes 1000000 | tf_op jit(solution)/shard_map/pallas_call | solution.py:202
  39.6 0.0 copy-start.2
  39.6 0.1 select_convert_fusion
  39.7 0.4 collective-permute-start.6
  40.2 1.1 %copy-done.2 = bf16[9,8,64,256]{3,2,1,0:T(8,128)(2,1)S(1)} copy-done((bf16[9,8,64,256]{3,2,1,0:T(8,128)(2,1)S(1)}, bf16[9,8,64,256]{3,2,1,0:T(8,128)(2,1)}, u32[]{:S(2)}) %copy-start.2) | copy-done | bytes 2359320
  41.3 1.4 %shard_map.74 = bf16[256,1024]{1,0:T(8,128)(2,1)S(1)} custom-call(bf16[9,256,256]{2,1,0:T(8,128)(2,1)S(1)} %get-tuple-element.44.w_ref, bf16[9,8,64,256]{3,2,1,0:T(8,128)(2,1)S(1)} %copy-done.2, bf16[9,8,64,256]{3,2,1,0:T(8,128)(2,1)S(1)} %get-tuple-element.46.edge_ref), custom_call_target="tpu_custom_call" | custom-call | flops 1000000000 | bytes 1000000 | tf_op jit(solution)/shard_map/pallas_call | solution.py:202
  42.7 0.0 collective-permute-done.6
  42.7 0.2 add_convert_fusion
  42.9 20.4 %all_to_all.15 = bf16[16,144,128]{2,1,0:T(8,128)(2,1)S(1)} all-to-all(bf16[16,144,128]{2,1,0:T(8,128)(2,1)S(1)} %bitcast.18), channel_id=1, replica_groups=mesh['y'=4,'x_lo'=2,'core'=2,'z'=8,'x_hi'=2] {'y','x_hi','x_lo'}, dimensions={0} | all-to-all | bytes 1179648 | tf_op jit(solution)/shard_map/all_to_all | solution.py:261
  63.3 0.1 reduce_sum.21
  63.4 12.6 %all_to_all.16 = bf16[8,144,128]{2,1,0:T(8,128)(2,1)S(1)} all-to-all(bf16[8,144,128]{2,1,0:T(8,128)(2,1)S(1)} %broadcast_in_dim.16), channel_id=1, replica_groups=mesh['y'=4,'x_lo'=2,'core'=2,'z'=8,'x_hi'=2] {'z'}, dimensions={0} | all-to-all | bytes 589824 | tf_op jit(solution)/shard_map/all_to_all | solution.py:261
  76.0 0.1 broadcast_in_dim.17
  76.1 12.9 %all_to_all.17 = bf16[16,144,128]{2,1,0:T(8,128)(2,1)S(1)} all-to-all(bf16[16,144,128]{2,1,0:T(8,128)(2,1)S(1)} %broadcast_in_dim.17), channel_id=1, replica_groups=mesh['y'=4,'x_lo'=2,'core'=2,'z'=8,'x_hi'=2] {'y','x_hi','x_lo'}, dimensions={0} | all-to-all | bytes 1179648 | tf_op jit(solution)/shard_map/all_to_all | solution.py:261
  89.1 4.6 %collective-permute-start.7 = (bf16[9,256,128]{2,1,0:T(8,128)(2,1)S(1)}, bf16[9,256,128]{2,1,0:T(8,128)(2,1)S(1)}, u32[]{:S(2)}, u32[]{:S(2)}) collective-permute-start(bf16[9,256,128]{2,1,0:T(8,128)(2,1)S(1)} %bitcast.14), channel_id=1, source_target_pairs={{0,16},{16,0},{1,17},{17,1},{2,18},{18,2},{3,19},{19,3},{4,20},{20... | collective-permute-start | bytes 1769480 | tf_op jit(solution)/shard_map/ppermute | solution.py:284
  93.6 0.9 copy.14
  94.5 1.1 %shard_map.75.refs_0_ = f32[9,256,256]{2,1,0:T(8,128)} custom-call(bf16[9,256,128]{2,1,0:T(8,128)(2,1)S(1)} %bitcast.15), custom_call_target="tpu_custom_call" | custom-call | flops 1000000 | bytes 1000000 | tf_op jit(solution)/shard_map/pallas_call | solution.py:248
  95.6 0.0 collective-permute-done.7.half_ref
  95.6 1.1 %shard_map.76 = f32[9,256,256]{2,1,0:T(8,128)} custom-call(bf16[9,256,128]{2,1,0:T(8,128)(2,1)S(1)} %collective-permute-done.7.half_ref, f32[9,256,256]{2,1,0:T(8,128)} %shard_map.75.refs_0_), custom_call_target="tpu_custom_call", output_to_operand_aliasing={{}: (1, {})} | custom-call | flops 1000000 | bytes 1000000 | tf_op jit(solution)/shard_map/pallas_call | solution.py:248
  (6 shorter events, 0.1 us)
Async XLA Ops:
  0.6 18.4 %copy-start = (bf16[9,128,7,33]{1,2,3,0:T(8,128)(2,1)S(1)}, bf16[9,128,7,33]{1,2,3,0:T(8,128)(2,1)}, u32[]{:S(2)}) copy-start(bf16[9,128,7,33]{1,2,3,0:T(8,128)(2,1)} %param.8) | copy-start | bytes 1596676
  0.6 8.7 %copy-start.11 = (bf16[256,8,128]{2,1,0:T(8,128)(2,1)S(1)}, bf16[256,8,128]{2,1,0:T(8,128)(2,1)}, u32[]{:S(2)}) copy-start(bf16[256,8,128]{2,1,0:T(8,128)(2,1)} %param.5) | copy-start | bytes 1572868
  2.1 16.8 %copy-start.12 = (s32[128]{0:T(128)S(1)}, s32[128]{0:T(128)}, u32[]{:S(2)}) copy-start(s32[128]{0:T(128)} %param.9) | copy-start | bytes 1540
  2.9 7.4 %collective-permute-start = (bf16[3,32,256]{2,1,0:T(8,128)(2,1)S(1)}, bf16[3,32,256]{2,1,0:T(8,128)(2,1)S(1)}, u32[]{:S(2)}, u32[]{:S(2)}) collective-permute-start(bf16[3,32,256]{2,1,0:T(8,128)(2,1)S(1)} %get-tuple-element.28), channel_id=1, source_target_pairs={{16,32},{32,16},{48,64},{64,48},{80,96},{96,80},{112,128},{128,112... | collective-permute-start | bytes 147464 | tf_op jit(solution)/shard_map/ppermute | solution.py:304
  7.4 13.5 %collective-permute-start.2 = (bf16[3,96,256]{2,1,0:T(8,128)(2,1)}, bf16[3,96,256]{2,1,0:T(8,128)(2,1)}, u32[]{:S(2)}, u32[]{:S(2)}) collective-permute-start(bf16[3,96,256]{2,1,0:T(8,128)(2,1)} %get-tuple-element.33), channel_id=1, source_target_pairs={{16,32},{32,16},{48,64},{64,48},{80,96},{96,80},{112,128},{128,112... | collective-permute-start | bytes 442376 | tf_op jit(solution)/shard_map/ppermute | solution.py:305
  10.9 18.0 %collective-permute-start.3 = (bf16[11,16,256]{2,1,0:T(8,128)(2,1)}, bf16[11,16,256]{2,1,0:T(8,128)(2,1)}, u32[]{:S(2)}, u32[]{:S(2)}) collective-permute-start(bf16[11,16,256]{2,1,0:T(8,128)(2,1)} %get-tuple-element.35), channel_id=1, source_target_pairs={{0,15},{1,2},{2,1},{3,4},{4,3},{5,6},{6,5},{7,8},{8,7},{9,10},{10,... | collective-permute-start | bytes 270344 | tf_op jit(solution)/shard_map/ppermute | solution.py:312
  18.9 10.0 %collective-permute-start.4 = (bf16[11,16,256]{2,1,0:T(8,128)(2,1)}, bf16[11,16,256]{2,1,0:T(8,128)(2,1)}, u32[]{:S(2)}, u32[]{:S(2)}) collective-permute-start(bf16[11,16,256]{2,1,0:T(8,128)(2,1)} %get-tuple-element.36), channel_id=1, source_target_pairs={{0,1},{1,0},{2,3},{3,2},{4,5},{5,4},{6,7},{7,6},{8,9},{9,8},{10,11... | collective-permute-start | bytes 270344 | tf_op jit(solution)/shard_map/ppermute | solution.py:313
  18.9 2.0 %collective-permute-start.1 = (bf16[3,128,256]{2,1,0:T(8,128)(2,1)}, bf16[3,128,256]{2,1,0:T(8,128)(2,1)}, u32[]{:S(2)}, u32[]{:S(2)}) collective-permute-start(bf16[3,128,256]{2,1,0:T(8,128)(2,1)} %get-tuple-element.32), channel_id=1, source_target_pairs={{0,16},{16,0},{32,48},{48,32},{64,80},{80,64},{96,112},{112,96},{1... | collective-permute-start | bytes 589832 | tf_op jit(solution)/shard_map/ppermute | solution.py:314
  19.8 1.1 %copy-start.5 = (bf16[32,8,8,128]{3,1,2,0:T(8,128)(2,1)S(1)}, bf16[32,8,8,128]{3,1,2,0:T(8,128)(2,1)}, u32[]{:S(2)}) copy-start(bf16[32,8,8,128]{3,1,2,0:T(8,128)(2,1)} %copy.16) | copy-start | bytes 1572868
  24.5 1.4 %copy-start.1 = (bf16[9,8,64,256]{3,2,1,0:T(8,128)(2,1)}, bf16[9,8,64,256]{3,2,1,0:T(8,128)(2,1)S(1)}, u32[]{:S(2)}) copy-start(bf16[9,8,64,256]{3,2,1,0:T(8,128)(2,1)S(1)} %get-tuple-element.45.mid_ref) | copy-start | bytes 7077892
  25.9 1.4 %copy-start.3 = (f32[9,256,256]{2,1,0:T(8,128)}, f32[9,256,256]{2,1,0:T(8,128)S(1)}, u32[]{:S(2)}) copy-start(f32[9,256,256]{2,1,0:T(8,128)S(1)} %get-tuple-element.41.total) | copy-start | bytes 7077892
  27.3 0.9 copy-start.7
  28.2 0.7 copy-start.9
  29.8 1.4 %collective-permute-start.5 = (bf16[3,32,256]{2,1,0:T(8,128)(2,1)S(1)}, bf16[3,32,256]{2,1,0:T(8,128)(2,1)S(1)}, u32[]{:S(2)}, u32[]{:S(2)}) collective-permute-start(bf16[3,32,256]{2,1,0:T(8,128)(2,1)S(1)} %shard_map.72), channel_id=1, source_target_pairs={{0,16},{16,0},{32,48},{48,32},{64,80},{80,64},{96,112},{112,96},{1... | collective-permute-start | bytes 147464 | tf_op jit(solution)/shard_map/ppermute | solution.py:339
  31.2 1.7 %copy-start.4 = (f32[9,256,256]{2,1,0:T(8,128)S(1)}, f32[9,256,256]{2,1,0:T(8,128)}, u32[]{:S(2)}) copy-start(f32[9,256,256]{2,1,0:T(8,128)} %copy-done.3) | copy-start | bytes 7077892
  32.9 1.3 %copy-start.6 = (bf16[9,256,256]{2,1,0:T(8,128)(2,1)S(1)}, bf16[9,256,256]{2,1,0:T(8,128)(2,1)}, u32[]{:S(2)}) copy-start(bf16[9,256,256]{2,1,0:T(8,128)(2,1)} %w_ref.1) | copy-start | bytes 3538948
  34.2 1.1 %copy-start.8 = (bf16[14,2,48,256]{3,2,1,0:T(8,128)(2,1)S(1)}, bf16[14,2,48,256]{3,2,1,0:T(8,128)(2,1)}, u32[]{:S(2)}) copy-start(bf16[14,2,48,256]{3,2,1,0:T(8,128)(2,1)} %copy-done.7) | copy-start | bytes 2064388
  35.3 0.9 copy-start.10
  39.6 1.7 %copy-start.2 = (bf16[9,8,64,256]{3,2,1,0:T(8,128)(2,1)S(1)}, bf16[9,8,64,256]{3,2,1,0:T(8,128)(2,1)}, u32[]{:S(2)}) copy-start(bf16[9,8,64,256]{3,2,1,0:T(8,128)(2,1)} %copy-done.1) | copy-start | bytes 7077892
  39.7 2.9 %collective-permute-start.6 = (bf16[9,256,128]{2,1,0:T(8,128)(2,1)S(1)}, bf16[9,256,128]{2,1,0:T(8,128)(2,1)S(1)}, u32[]{:S(2)}, u32[]{:S(2)}) collective-permute-start(bf16[9,256,128]{2,1,0:T(8,128)(2,1)S(1)} %select_convert_fusion), channel_id=1, source_target_pairs={{0,16},{16,0},{1,17},{17,1},{2,18},{18,2},{3,19},{19,3},{4,20},{20... | collective-permute-start | bytes 1769480 | tf_op jit(solution)/shard_map/ppermute | solution.py:276
  89.1 6.5 %collective-permute-start.7 = (bf16[9,256,128]{2,1,0:T(8,128)(2,1)S(1)}, bf16[9,256,128]{2,1,0:T(8,128)(2,1)S(1)}, u32[]{:S(2)}, u32[]{:S(2)}) collective-permute-start(bf16[9,256,128]{2,1,0:T(8,128)(2,1)S(1)} %bitcast.14), channel_id=1, source_target_pairs={{0,16},{16,0},{1,17},{17,1},{2,18},{18,2},{3,19},{19,3},{4,20},{20... | collective-permute-start | bytes 1769480 | tf_op jit(solution)/shard_map/ppermute | solution.py:284

commit v14 on v12

--- a/solution.py
+++ b/solution.py
@@ -283,9 +283,9 @@
     rest_lat = lax.ppermute(to_far[:, side : lon_dev - side], LAT, pairs(LAT, False, False))
     rim = shape((near - half, side, channels), bf16)
     second, first = call(rim_kernel, (rim, rim), (main, far_lat), flops=10**6, mib=4)
-    start, to_near, second, first = lax.optimization_barrier((start, to_near, second, first))
     table = lax.dynamic_slice_in_dim(basis_table, start, held, 1)
     reach = lax.dynamic_slice_in_dim(lon_reach, start, held, 0)
+    table, to_near, second, first = lax.optimization_barrier((table, to_near, second, first))
     taps = mask_taps(table, reach)
     far_lon = lax.ppermute(second, LON, pairs(LON, False, True))
     near_lon = lax.ppermute(first, LON, pairs(LON, True, True))

time: 84.6 us -> 82.8 us (0.979)
  blocking collectives: 47.8 us -> 45.5 us
  waiting for transfers between devices: 1.98 us -> 2.99 us
    all_to_all x3, blocking collectives: 47.8 us -> 45.5 us  [all_to_all(): return lax.all_to_all(x, axes, 0, 0, tiled=True)]
    ppermute x1, waiting for transfers between devices: 0.51 us -> 1.4 us  [local(): near_lat = lax.ppermute(to_near, LAT, pairs(LAT, True, False))]
    unnamed x12 -> x11, local copies, waits for them, and re-layouts: 2.91 us -> 2.4 us
  transfers between devices with their start and end apart: 8 -> 8, of which waited for: 3 -> 3; matrix products, arithmetic and copies ran while one was open for 3% -> 2% of each run, Pallas kernels for 7% -> 7%
where the time goes in v14:
time: 82.8 us; the launch traced here: 82.6 us
  blocking collectives  45.5 us (55%)
  starting transfers between devices  19.8 us (24%)
  Pallas kernels  9.51 us (11%)
  local copies, waits for them, and re-layouts  3.33 us (4%)
  waiting for transfers between devices  2.99 us (4%)
  between operations  0.91 us (1%)
    all_to_all x3, blocking collectives, all_to_all(): return lax.all_to_all(x, axes, 0, 0, tiled=True)  45.5 us
    ppermute x1, starting transfers between devices, local(): far_lon = lax.ppermute(second, LON, pairs(LON, False, True))  8.08 us
    pallas_call x5, Pallas kernels, call(): pl.pallas_call(kernel, out_shape=out_shape, in_specs=[vmem] * (len(operan...  7.39 us
    ppermute x1, starting transfers between devices, reduce_all(): lax.ppermute(own, 'core', swap)  4.69 us
    ppermute x1, starting transfers between devices, local(): far_lat = lax.ppermute(outer, LAT, pairs(LAT, False, False))  4.64 us
    unnamed x11, local copies, waits for them, and re-layouts  2.4 us
    pallas_call x2, Pallas kernels, place(): pl.pallas_call(functools.partial(place_kernel, own), out_shape=jax.ShapeD...  2.12 us
    ppermute x1, starting transfers between devices, local(): lax.ppermute(to_far[:, side:lon_dev - side], LAT, pairs(LAT, False, False))  1.92 us
  transfers between devices with their start and end apart: 8, of which 3 were waited for; matrix products, arithmetic and copies ran while one was open for 2% of the time, Pallas kernels for 7%

profile of v14, /device:TPU:1, one launch (start us, length us, event | category | flops | bytes accessed | tf_op | source)
XLA Modules:
  0.0 82.6 jit_solution(10107215050274048056)
XLA Ops:
  0.6 0.0 copy-start
  0.7 0.0 copy-start.3
  0.7 1.4 %copy.11 = bf16[256,8,128]{0,2,1:T(8,128)(2,1)S(1)} copy(bf16[256,8,128]{2,1,0:T(8,128)(2,1)} %param.6) | data formatting | bytes 1048576 | tf_op args[1]
  2.1 0.0 copy-start.2
  2.1 4.6 %collective-permute-start = (bf16[3,32,256]{2,1,0:T(8,128)(2,1)S(1)}, bf16[3,32,256]{2,1,0:T(8,128)(2,1)S(1)}, u32[]{:S(2)}, u32[]{:S(2)}) collective-permute-start(bf16[3,32,256]{2,1,0:T(8,128)(2,1)S(1)} %pad_maximum_fusion), channel_id=1, source_target_pairs={{16,32},{32,16},{48,64},{64,48},{80,96},{96,80},{112,128},{128,112... | collective-permute-start | bytes 147464 | tf_op jit(solution)/shard_map/ppermute | solution.py:282
  6.8 1.9 %collective-permute-start.2 = (bf16[3,96,256]{2,1,0:T(8,128)(2,1)S(1)}, bf16[3,96,256]{2,1,0:T(8,128)(2,1)S(1)}, u32[]{:S(2)}, u32[]{:S(2)}) collective-permute-start(bf16[3,96,256]{2,1,0:T(8,128)(2,1)S(1)} %slice.24), channel_id=1, source_target_pairs={{16,32},{32,16},{48,64},{64,48},{80,96},{96,80},{112,128},{128,112... | collective-permute-start | bytes 442376 | tf_op jit(solution)/shard_map/ppermute | solution.py:283
  8.8 0.0 copy-done.3
  8.8 0.1 dynamic_slice.6
  8.8 0.1 broadcast_compare_fusion
  8.9 0.0 copy-done
  8.9 0.2 constant_dynamic-slice_fusion
  9.2 0.0 copy-done.2
  9.2 0.1 copy.16
  9.3 0.5 copy.12
  9.8 0.0 collective-permute-done.far
  9.8 8.1 %collective-permute-start.3 = (bf16[11,16,256]{2,1,0:T(8,128)(2,1)S(1)}, bf16[11,16,256]{2,1,0:T(8,128)(2,1)S(1)}, u32[]{:S(2)}, u32[]{:S(2)}) collective-permute-start(bf16[11,16,256]{2,1,0:T(8,128)(2,1)S(1)} %get-tuple-element.31), channel_id=1, source_target_pairs={{0,15},{1,2},{2,1},{3,4},{4,3},{5,6},{6,5},{7,8},{8,7},{9,10},{10,... | collective-permute-start | bytes 270344 | tf_op jit(solution)/shard_map/ppermute | solution.py:290
  17.9 0.0 collective-permute-start.4
  17.9 0.0 collective-permute-start.1
  17.9 0.0 collective-permute-done.2.rest
  18.0 1.4 %collective-permute-done.1.near = bf16[3,128,256]{2,1,0:T(8,128)(2,1)S(1)} collective-permute-done((bf16[3,128,256]{2,1,0:T(8,128)(2,1)S(1)}, bf16[3,128,256]{2,1,0:T(8,128)(2,1)S(1)}, u32[]{:S(2)}, u32[]{:S(2)}) %collective-permute-start.1) | collective-permute-done | bytes 196640 | tf_op jit(solution)/shard_map/ppermute | solution.py:292
  19.4 0.0 copy-start.1
  19.4 3.4 %shard_map.69 = (bf16[8,288,512]{2,1,0:T(8,128)(2,1)S(1)}, bf16[256,512]{1,0:T(8,128)(2,1)S(1)}, bf16[9,8,64,256]{3,2,1,0:T(8,128)(2,1)S(1)}, f32[9,256,256]{2,1,0:T(8,128)S(1)}, bf16[14,2,48,256]{3,2,1,0:T(8,128)(2,1)S(1)}) custom-call(bf16[9,7,16,33]{3,2,1,0:T(8,128)(2,1)S(1)} %select_bitcast_fusion.taps, bf16[256,1024]{1,0:T(8,128)(2,1)S(1)} %bitcast.17, ...), custom_call_target="tpu_custom_call" | custom-call | flops 1000000000 | bytes 1000000 | tf_op jit(solution)/shard_map/pallas_call | solution.py:183
  22.8 0.0 collective-permute-done.3.far
  22.8 0.0 collective-permute-done.4.near
  22.9 0.2 collective-permute-start.5
  23.0 1.1 %collective-permute-done.5.corner = bf16[3,32,256]{2,1,0:T(8,128)(2,1)S(1)} collective-permute-done((bf16[3,32,256]{2,1,0:T(8,128)(2,1)S(1)}, bf16[3,32,256]{2,1,0:T(8,128)(2,1)S(1)}, u32[]{:S(2)}, u32[]{:S(2)}) %collective-permute-start.5) | collective-permute-done | bytes 49184 | tf_op jit(solution)/shard_map/ppermute | solution.py:314
  24.2 0.0 copy-done.1
  24.2 2.5 %shard_map.71 = (bf16[9,8,64,256]{3,2,1,0:T(8,128)(2,1)S(1)}, f32[9,256,128]{2,1,0:T(8,128)S(1)}, f32[9,256,128]{2,1,0:T(8,128)S(1)}, bf16[9,256,256]{2,1,0:T(8,128)(2,1)S(1)}) custom-call(bf16[8,288,512]{2,1,0:T(8,128)(2,1)S(1)} %get-tuple-element.29.band, bf16[14,2,48,256]{3,2,1,0:T(8,128)(2,1)S(1)} %get-tuple-element.30.window, ...), custom_call_target="tpu_custom_call" | custom-call | flops 1000000000 | bytes 1000000 | tf_op jit(solution)/shard_map/pallas_call | solution.py:183
  26.7 0.1 select_convert_fusion
  26.8 0.2 collective-permute-start.6
  27.0 1.4 %shard_map.72 = bf16[256,1024]{1,0:T(8,128)(2,1)S(1)} custom-call(bf16[9,256,256]{2,1,0:T(8,128)(2,1)S(1)} %get-tuple-element.40.w_ref, bf16[9,8,64,256]{3,2,1,0:T(8,128)(2,1)S(1)} %get-tuple-element.41.mid_ref, bf16[9,8,64,256]{3,2,1,0:T(8,128)(2,1)S(1)} %get-tuple-element.42.edge_ref), custom_call_target="tpu_custom_call" | custom-call | flops 1000000000 | bytes 1000000 | tf_op jit(solution)/shard_map/pallas_call | solution.py:183
  28.5 0.4 collective-permute-done.6
  28.9 0.2 add_convert_fusion
  29.1 20.0 %all_to_all.15 = bf16[16,144,128]{2,1,0:T(8,128)(2,1)S(1)} all-to-all(bf16[16,144,128]{2,1,0:T(8,128)(2,1)S(1)} %bitcast.18), channel_id=1, replica_groups=mesh['y'=4,'x_lo'=2,'core'=2,'z'=8,'x_hi'=2] {'y','x_hi','x_lo'}, dimensions={0} | all-to-all | bytes 1179648 | tf_op jit(solution)/shard_map/all_to_all | solution.py:242
  49.0 0.1 reduce_sum.21
  49.2 12.1 %all_to_all.16 = bf16[8,144,128]{2,1,0:T(8,128)(2,1)S(1)} all-to-all(bf16[8,144,128]{2,1,0:T(8,128)(2,1)S(1)} %broadcast_in_dim.16), channel_id=1, replica_groups=mesh['y'=4,'x_lo'=2,'core'=2,'z'=8,'x_hi'=2] {'z'}, dimensions={0} | all-to-all | bytes 589824 | tf_op jit(solution)/shard_map/all_to_all | solution.py:242
  61.3 0.1 broadcast_in_dim.17
  61.4 13.5 %all_to_all.17 = bf16[16,144,128]{2,1,0:T(8,128)(2,1)S(1)} all-to-all(bf16[16,144,128]{2,1,0:T(8,128)(2,1)S(1)} %broadcast_in_dim.17), channel_id=1, replica_groups=mesh['y'=4,'x_lo'=2,'core'=2,'z'=8,'x_hi'=2] {'y','x_hi','x_lo'}, dimensions={0} | all-to-all | bytes 1179648 | tf_op jit(solution)/shard_map/all_to_all | solution.py:242
  74.9 4.7 %collective-permute-start.7 = (bf16[9,256,128]{2,1,0:T(8,128)(2,1)S(1)}, bf16[9,256,128]{2,1,0:T(8,128)(2,1)S(1)}, u32[]{:S(2)}, u32[]{:S(2)}) collective-permute-start(bf16[9,256,128]{2,1,0:T(8,128)(2,1)S(1)} %bitcast.14), channel_id=1, source_target_pairs={{0,16},{16,0},{1,17},{17,1},{2,18},{18,2},{3,19},{19,3},{4,20},{20... | collective-permute-start | bytes 1769480 | tf_op jit(solution)/shard_map/ppermute | solution.py:265
  79.5 0.9 %copy.14 = bf16[32,8,8,128]{3,2,1,0:T(8,128)(2,1)} copy(bf16[32,8,8,128]{3,1,2,0:T(8,128)(2,1)S(1)} %bitcast.16) | data formatting | bytes 1048576
  80.4 1.1 %shard_map.73.refs_0_ = f32[9,256,256]{2,1,0:T(8,128)} custom-call(bf16[9,256,128]{2,1,0:T(8,128)(2,1)S(1)} %bitcast.15), custom_call_target="tpu_custom_call" | custom-call | flops 1000000 | bytes 1000000 | tf_op jit(solution)/shard_map/pallas_call | solution.py:229
  81.5 0.0 collective-permute-done.7.half_ref
  81.5 1.1 %shard_map.74 = f32[9,256,256]{2,1,0:T(8,128)} custom-call(bf16[9,256,128]{2,1,0:T(8,128)(2,1)S(1)} %collective-permute-done.7.half_ref, f32[9,256,256]{2,1,0:T(8,128)} %shard_map.73.refs_0_), custom_call_target="tpu_custom_call", output_to_operand_aliasing={{}: (1, {})} | custom-call | flops 1000000 | bytes 1000000 | tf_op jit(solution)/shard_map/pallas_call | solution.py:229
  (11 shorter events, 0.2 us)
Async XLA Ops:
  0.6 8.3 %copy-start = (bf16[9,128,7,33]{1,2,3,0:T(8,128)(2,1)S(1)}, bf16[9,128,7,33]{1,2,3,0:T(8,128)(2,1)}, u32[]{:S(2)}) copy-start(bf16[9,128,7,33]{1,2,3,0:T(8,128)(2,1)} %param.8) | copy-start | bytes 1596676
  0.7 8.1 %copy-start.3 = (s32[128]{0:T(128)S(1)}, s32[128]{0:T(128)}, u32[]{:S(2)}) copy-start(s32[128]{0:T(128)} %param.9) | copy-start | bytes 1540
  2.1 7.1 %copy-start.2 = (bf16[256,8,128]{2,1,0:T(8,128)(2,1)S(1)}, bf16[256,8,128]{2,1,0:T(8,128)(2,1)}, u32[]{:S(2)}) copy-start(bf16[256,8,128]{2,1,0:T(8,128)(2,1)} %param.5) | copy-start | bytes 1572868
  2.1 7.6 %collective-permute-start = (bf16[3,32,256]{2,1,0:T(8,128)(2,1)S(1)}, bf16[3,32,256]{2,1,0:T(8,128)(2,1)S(1)}, u32[]{:S(2)}, u32[]{:S(2)}) collective-permute-start(bf16[3,32,256]{2,1,0:T(8,128)(2,1)S(1)} %pad_maximum_fusion), channel_id=1, source_target_pairs={{16,32},{32,16},{48,64},{64,48},{80,96},{96,80},{112,128},{128,112... | collective-permute-start | bytes 147464 | tf_op jit(solution)/shard_map/ppermute | solution.py:282
  6.8 11.1 %collective-permute-start.2 = (bf16[3,96,256]{2,1,0:T(8,128)(2,1)S(1)}, bf16[3,96,256]{2,1,0:T(8,128)(2,1)S(1)}, u32[]{:S(2)}, u32[]{:S(2)}) collective-permute-start(bf16[3,96,256]{2,1,0:T(8,128)(2,1)S(1)} %slice.24), channel_id=1, source_target_pairs={{16,32},{32,16},{48,64},{64,48},{80,96},{96,80},{112,128},{128,112... | collective-permute-start | bytes 442376 | tf_op jit(solution)/shard_map/ppermute | solution.py:283
  9.8 13.0 %collective-permute-start.3 = (bf16[11,16,256]{2,1,0:T(8,128)(2,1)S(1)}, bf16[11,16,256]{2,1,0:T(8,128)(2,1)S(1)}, u32[]{:S(2)}, u32[]{:S(2)}) collective-permute-start(bf16[11,16,256]{2,1,0:T(8,128)(2,1)S(1)} %get-tuple-element.31), channel_id=1, source_target_pairs={{0,15},{1,2},{2,1},{3,4},{4,3},{5,6},{6,5},{7,8},{8,7},{9,10},{10,... | collective-permute-start | bytes 270344 | tf_op jit(solution)/shard_map/ppermute | solution.py:290
  17.9 4.9 %collective-permute-start.4 = (bf16[11,16,256]{2,1,0:T(8,128)(2,1)S(1)}, bf16[11,16,256]{2,1,0:T(8,128)(2,1)S(1)}, u32[]{:S(2)}, u32[]{:S(2)}) collective-permute-start(bf16[11,16,256]{2,1,0:T(8,128)(2,1)S(1)} %get-tuple-element.32), channel_id=1, source_target_pairs={{0,1},{1,0},{2,3},{3,2},{4,5},{5,4},{6,7},{7,6},{8,9},{9,8},{10,11... | collective-permute-start | bytes 270344 | tf_op jit(solution)/shard_map/ppermute | solution.py:291
  17.9 1.4 %collective-permute-start.1 = (bf16[3,128,256]{2,1,0:T(8,128)(2,1)S(1)}, bf16[3,128,256]{2,1,0:T(8,128)(2,1)S(1)}, u32[]{:S(2)}, u32[]{:S(2)}) collective-permute-start(bf16[3,128,256]{2,1,0:T(8,128)(2,1)S(1)} %get-tuple-element.28), channel_id=1, source_target_pairs={{0,16},{16,0},{32,48},{48,32},{64,80},{80,64},{96,112},{112,96},{1... | collective-permute-start | bytes 589832 | tf_op jit(solution)/shard_map/ppermute | solution.py:292
  19.4 4.8 %copy-start.1 = (bf16[9,256,256]{2,1,0:T(8,128)(2,1)S(1)}, bf16[9,256,256]{2,1,0:T(8,128)(2,1)}, u32[]{:S(2)}) copy-start(bf16[9,256,256]{2,1,0:T(8,128)(2,1)} %w_ref.1) | copy-start | bytes 3538948
  22.9 1.3 %collective-permute-start.5 = (bf16[3,32,256]{2,1,0:T(8,128)(2,1)S(1)}, bf16[3,32,256]{2,1,0:T(8,128)(2,1)S(1)}, u32[]{:S(2)}, u32[]{:S(2)}) collective-permute-start(bf16[3,32,256]{2,1,0:T(8,128)(2,1)S(1)} %shard_map.70), channel_id=1, source_target_pairs={{0,16},{16,0},{32,48},{48,32},{64,80},{80,64},{96,112},{112,96},{1... | collective-permute-start | bytes 147464 | tf_op jit(solution)/shard_map/ppermute | solution.py:314
  26.8 2.1 %collective-permute-start.6 = (bf16[9,256,128]{2,1,0:T(8,128)(2,1)S(1)}, bf16[9,256,128]{2,1,0:T(8,128)(2,1)S(1)}, u32[]{:S(2)}, u32[]{:S(2)}) collective-permute-start(bf16[9,256,128]{2,1,0:T(8,128)(2,1)S(1)} %select_convert_fusion), channel_id=1, source_target_pairs={{0,16},{16,0},{1,17},{17,1},{2,18},{18,2},{3,19},{19,3},{4,20},{20... | collective-permute-start | bytes 1769480 | tf_op jit(solution)/shard_map/ppermute | solution.py:257
  74.9 6.6 %collective-permute-start.7 = (bf16[9,256,128]{2,1,0:T(8,128)(2,1)S(1)}, bf16[9,256,128]{2,1,0:T(8,128)(2,1)S(1)}, u32[]{:S(2)}, u32[]{:S(2)}) collective-permute-start(bf16[9,256,128]{2,1,0:T(8,128)(2,1)S(1)} %bitcast.14), channel_id=1, source_target_pairs={{0,16},{16,0},{1,17},{17,1},{2,18},{18,2},{3,19},{19,3},{4,20},{20... | collective-permute-start | bytes 1769480 | tf_op jit(solution)/shard_map/ppermute | solution.py:265
